TPU v7x, 32 devices: a whole 2x2x4 slice. The times are simulated.
32 devices in a mesh: grp: 2 (over y), mig: 4 (over x, core), pen: 4 (over z).
Axes of the slice: x: 2, y: 2, z: 4, core: 2. Of those that a mesh axis runs over, the one named last changes fastest.
Arguments:
- fields: float32 [1024, 9, 4096], P(('grp', 'mig', 'pen')), may hold values from -6 to 6
- ghosts: float32 [1024, 9, 1536], P(('grp', 'mig', 'pen')), may hold values from -6 to 6
- velocity: float32 [3, 1024], P(None, ('grp', 'mig', 'pen')), may hold values from -1 to 1
- rate_matrix: float32 [9, 9], replicated, may hold values from -2 to 2
- recent_tend: bfloat16 [1024, 9, 4096], P(('grp', 'mig', 'pen')), may hold values from -6 to 6
- older_tend: bfloat16 [1024, 9, 4096], P(('grp', 'mig', 'pen')), may hold values from -6 to 6
- destination: int32 [1024], P(('grp', 'mig', 'pen')), may hold values from 0 to 15, as said below
- target_slot: int32 [1024], P(('grp', 'mig', 'pen')), may hold values from 0 to 32, as said below
- live_counts: int32 [32], P(('grp', 'mig', 'pen')), may hold values from 0 to 32, as said below
- tile_ids: int32 [1024], P(('grp', 'mig', 'pen')), may hold values from 0 to 1023, each once
- sensor: float32 [128, 32768], P('pen', ('grp', 'mig')), may hold values from 0 to 4
- flame_flags: int32 [8, 128], P('pen', ('grp', 'mig')), may hold values 0 or 1
Outputs:
- new_fields: float32 [1024, 9, 4096], P(('grp', 'mig', 'pen'))
- new_tend: bfloat16 [1024, 9, 4096], P(('grp', 'mig', 'pen'))
- filtered: float32 [128, 32768], P('pen', ('grp', 'mig'))
Inputs may be any that keep to these rules, and one draw needn't show every extreme that they name: `destination`: index (mig-major) within the old slot's group of devices sharing its grp index; a device names every other device of its group for at most one of its slots; slots whose tile stays, and slots without a tile, name the device itself. `target_slot`: 32 marks an old slot without a tile; at each device the kept and arriving tiles take the slots 0 to its live count - 1, each exactly once. `live_counts`: equals the number of tiles that a device keeps or receives.
All inputs are finite; a program needn't handle non-finite values. No bound on the sum of `flame_flags` on one device may be relied on, other than what follows from the above.
Results may differ from a plain program's by a relative error of at most 0.001.
Values may be sent and summed in bfloat16 or wider, within the bound.
No kernel may reach another device: no remote copies, remote signals or barrier semaphores. Data moves between devices by JAX's collectives and lax.ppermute only.
A program may use at most 320 MiB of HBM per device.

v0:
```python
import jax
import jax.numpy as jnp
import numpy as np
from jax import lax
from jax.experimental import pallas as pl
from jax.experimental.pallas import tpu as pltpu
from jax.sharding import PartitionSpec as P

TE = 16
TZ = 2
TCOL = 16
FACE = TE * TE
CELLS = TE**3
LANES = 128
ROWS = CELLS // LANES

viscous = 0.05
step_size = 0.25
thicken = 5.0

SCALE = 4096.0
PLANES = 4

EVERY = ("grp", "mig", "pen")
TEAM = ("mig", "pen")


def passed_along(x, axis, by):
    peers = lax.axis_size(axis)
    return lax.ppermute(x, axis, [(i, (i + by) % peers) for i in range(peers)])


def banded(brick_rows, reach):
    sigma = reach / 2.0
    offsets = np.arange(-reach, reach + 1, dtype=np.float64)
    total = np.sum(np.exp(-offsets * offsets / (2.0 * sigma * sigma)))
    row = np.arange(brick_rows)[:, None]
    col = np.arange(brick_rows + 2 * reach)[None, :]
    offset = (col - reach - row).astype(np.float64)
    weights = np.where(np.abs(offset) <= reach, np.exp(-offset * offset / (2.0 * sigma * sigma)), 0)
    return (weights / total).astype(np.float32)


def raw_kernel(flags_ref, sensor_ref, raw_ref):
    for r in range(TZ):
        for k in range(TCOL):
            rows, cols = slice(r * TE, (r + 1) * TE), slice(k * FACE, (k + 1) * FACE)
            flag = flags_ref[r, k].astype(jnp.float32)
            raw_ref[rows, cols] = (sensor_ref[rows, cols] * flag).astype(jnp.bfloat16)


def filter_kernel(flags_ref, weights_ref, sensor_ref, below_ref, above_ref, notes_ref, filtered_ref, row_ref):
    lane = lax.broadcasted_iota(jnp.int32, (1, LANES), 1)
    row = notes_ref[...]
    brick = sensor_ref.shape[0]
    for k in range(TCOL):
        cols = slice(k * FACE, (k + 1) * FACE)
        own = [
            sensor_ref[r * TE : (r + 1) * TE, cols] * flags_ref[r, k].astype(jnp.float32)
            for r in range(TZ)
        ]
        widened = jnp.concatenate(
            [below_ref[:, cols].astype(jnp.float32)] + own + [above_ref[:, cols].astype(jnp.float32)],
            axis=0,
        )
        filtered = jnp.dot(
            weights_ref[...],
            widened,
            precision=lax.Precision.HIGHEST,
            preferred_element_type=jnp.float32,
        )
        filtered_ref[:, cols] = filtered
        clipped = jnp.minimum(filtered, 1.0)
        for r in range(TZ):
            total = jnp.sum(
                jnp.sum(clipped[r * TE : (r + 1) * TE], axis=0, keepdims=True), axis=1, keepdims=True
            )
            thick = 1.0 + (thicken - 1.0) * (total / float(TE * FACE))
            row = jnp.where(lane == r * TCOL + k, thick, row)
    row_ref[...] = row


def send_kernel(
    me_ref, destination_ref, recent_hbm, older_hbm, out_ref, recent_ref, older_ref, got
):
    species, slots, _ = recent_ref.shape
    peers = out_ref.shape[0]

    def fetches(s):
        return (
            pltpu.make_async_copy(recent_hbm.at[s], recent_ref.at[s], got.at[0, s]),
            pltpu.make_async_copy(older_hbm.at[s], older_ref.at[s], got.at[1, s]),
        )

    for s in range(species):
        for copy in fetches(s):
            copy.start()
    peer = lax.broadcasted_iota(jnp.int32, (peers, slots), 0)
    hot = ((destination_ref[...] == peer) & (peer != me_ref[0])).astype(jnp.bfloat16)
    flat = out_ref.reshape(peers * species * ROWS, LANES)
    for s in range(species):
        for copy in fetches(s):
            copy.wait()
        recent = jnp.dot(hot, recent_ref[s], preferred_element_type=jnp.float32)
        older = jnp.dot(hot, older_ref[s], preferred_element_type=jnp.float32)
        mixed = recent * (-16.0 / 12.0 * SCALE) + older * (5.0 / 12.0 * SCALE)
        for k in range(ROWS):
            flat[pl.ds(s * ROWS + k, peers, stride=species * ROWS), :] = mixed[
                :, k * LANES : (k + 1) * LANES
            ]


def prepare_kernel(
    me_ref,
    live_ref,
    moves_ref,
    fields_hbm,
    recent_hbm,
    older_hbm,
    ghosts_hbm,
    base_hbm,
    rims_hbm,
    fields_ref,
    recent_ref,
    older_ref,
    ghosts_ref,
    rims_ref,
    got,
    sent,
):
    species, slots, _ = fields_ref.shape

    def fetches(s):
        pairs = (
            (fields_hbm, fields_ref),
            (recent_hbm, recent_ref),
            (older_hbm, older_ref),
            (ghosts_hbm, ghosts_ref),
        )
        return [
            pltpu.make_async_copy(here.at[s], there.at[s], got.at[n, s])
            for n, (here, there) in enumerate(pairs)
        ]

    def stores(s):
        return (
            pltpu.make_async_copy(fields_ref.at[s], base_hbm.at[s], sent.at[0, s]),
            pltpu.make_async_copy(rims_ref.at[s], rims_hbm.at[s], sent.at[1, s]),
        )

    for s in range(species):
        for copy in fetches(s):
            copy.start()
    slot = lax.broadcasted_iota(jnp.int32, (slots, slots), 0)
    keep = (moves_ref[0:1, :] == me_ref[0]) & (moves_ref[1:2, :] == slot)
    keep = keep.astype(jnp.bfloat16)
    live = lax.broadcasted_iota(jnp.int32, (slots, 1), 0) < live_ref[0]
    live = jnp.where(live, 1.0, 0.0)
    quarter = lax.broadcasted_iota(jnp.int32, (slots, LANES), 1) // (2 * TE)

    def one(s, carry):
        for copy in fetches(s):
            copy.wait()
        recent = jnp.dot(keep, recent_ref[s], preferred_element_type=jnp.float32)
        older = jnp.dot(keep, older_ref[s], preferred_element_type=jnp.float32)
        kept = recent * (-16.0 / 12.0 * step_size) + older * (5.0 / 12.0 * step_size)
        fields_ref[s] = (fields_ref[s] + kept) * live
        for block in range(2):
            faces = [
                ghosts_ref[s, :, w * FACE + block * LANES : w * FACE + (block + 1) * LANES]
                for w in (4, 5, 2, 3)
            ]
            for q in range(4):
                rim = faces[0]
                for n in range(4):
                    turned = pltpu.roll(faces[n], (n - q) % 4 * 2 * TE, 1) if n != q else faces[n]
                    rim = turned if n == 0 else jnp.where(quarter == n, turned, rim)
                high = rim.astype(jnp.bfloat16)
                low = (rim - high.astype(jnp.float32)).astype(jnp.bfloat16)
                start = (block * 4 + q) * 2 * LANES
                rims_ref[s, :, start : start + LANES] = high
                rims_ref[s, :, start + LANES : start + 2 * LANES] = low
        for copy in stores(s):
            copy.start()
        return carry

    lax.fori_loop(0, species, one, 0)
    for s in range(species):
        for copy in stores(s):
            copy.wait()


def plane_weights():
    weights = np.zeros((6 * LANES, 3 * FACE), np.float32)
    for cell in range(FACE):
        y, z = divmod(cell, TE)
        for d, at, step in ((0, y, TE), (1, z, 1)):
            for way in (-1, 1):
                if 0 <= at + way < TE:
                    rows = [cell + way * step, FACE + cell + way * step]
                else:
                    face = (2 + (way > 0)) if d == 0 else (way > 0)
                    spot = 2 * FACE + face * 2 * TE + (z if d == 0 else y)
                    rows = [spot, spot + TE, spot + LANES, spot + LANES + TE]
                weights[rows, cell] += 1.0
                weights[rows, (1 + d) * FACE + cell] += way
        weights[[cell, FACE + cell], cell] -= 6.0
    return weights


def main_kernel(
    live_ref,
    rate_ref,
    table_ref,
    tile_ref,
    speed_ref,
    weights_hbm,
    fields_hbm,
    ghosts_hbm,
    rims_hbm,
    base_hbm,
    new_fields_hbm,
    new_tend_hbm,
    weights_ref,
    fields_ref,
    rims_ref,
    base_ref,
    new_tend_ref,
    rates_ref,
    wide_ref,
    left_even_ref,
    left_odd_ref,
    sums_even_ref,
    sums_odd_ref,
    got,
    sent,
):
    species, slots, cells = base_ref.shape
    peers = table_ref.shape[0]
    chunk = PLANES * FACE
    chunks = cells // chunk

    def span(c, length, skipped=0):
        return pl.ds(pl.multiple_of(skipped + c * length, LANES), length)

    def bases(c):
        lanes = span(c, chunk)
        return pltpu.make_async_copy(
            base_hbm.at[:, :, lanes], base_ref.at[:, :, lanes], got.at[2, c]
        )

    def cells_in(c):
        lanes, rims, inner = span(c, chunk), span(c, chunk // 2), span(c, chunk, FACE)
        return (
            pltpu.make_async_copy(
                fields_hbm.at[:, :, lanes], fields_ref.at[:, :, inner], got.at[0, c]
            ),
            pltpu.make_async_copy(
                rims_hbm.at[:, :, rims], rims_ref.at[:, :, rims], got.at[1, c]
            ),
        )

    def ends():
        return (
            pltpu.make_async_copy(weights_hbm, weights_ref, got.at[3, 0]),
            pltpu.make_async_copy(
                ghosts_hbm.at[:, :, pl.ds(0, FACE)], fields_ref.at[:, :, pl.ds(0, FACE)], got.at[3, 1]
            ),
            pltpu.make_async_copy(
                ghosts_hbm.at[:, :, pl.ds(FACE, FACE)],
                fields_ref.at[:, :, pl.ds(FACE + cells, FACE)],
                got.at[3, 2],
            ),
        )

    def stores(c):
        lanes = span(c, chunk)
        return (
            pltpu.make_async_copy(
                base_ref.at[:, :, lanes], new_fields_hbm.at[:, :, lanes], sent.at[0, c]
            ),
            pltpu.make_async_copy(
                new_tend_ref.at[:, :, lanes], new_tend_hbm.at[:, :, lanes], sent.at[1, c]
            ),
        )

    for copy in ends():
        copy.start()
    for c in range(chunks):
        for copy in (*cells_in(c), bases(c)):
            copy.start()

    wanted = lax.broadcasted_iota(jnp.int32, (slots, peers), 1) == tile_ref[:, 0:1]
    picked = jnp.dot(
        wanted.astype(jnp.float32),
        table_ref[...],
        precision=lax.Precision.HIGHEST,
        preferred_element_type=jnp.float32,
    )
    lane = lax.broadcasted_iota(jnp.int32, picked.shape, 1)
    thick = jnp.sum(jnp.where(lane == tile_ref[:, 1:2], picked, 0.0), axis=1, keepdims=True)
    live = lax.broadcasted_iota(jnp.int32, (slots, 1), 0) < live_ref[0]
    live = jnp.where(live, 1.0, 0.0)
    parts = [viscous * thick * live, live / thick]
    parts += [0.5 * live * speed_ref[:, d : d + 1] for d in range(3)]
    for n, part in enumerate(parts):
        wide_ref[n] = jnp.broadcast_to(part, (slots, LANES))
    for s in range(species):
        for k in range(species):
            rates_ref[s * species + k] = jnp.full((8, LANES), rate_ref[s, k], jnp.float32)
    parity = lax.broadcasted_iota(jnp.int32, (slots, 2 * LANES), 1) // TE % 2

    def sums(pair, odd):
        left_ref, sums_ref = ((left_even_ref, sums_even_ref), (left_odd_ref, sums_odd_ref))[odd]
        rims = pl.ds(pl.multiple_of(pair * FACE, FACE), FACE)
        for s in range(species):
            both = rims_ref[s, :, rims]
            for p in range(2):
                lanes = pl.ds(pl.multiple_of((2 * pair + p + 1) * FACE, FACE), FACE)
                rows = slice((p * species + s) * slots, (p * species + s + 1) * slots)
                f = fields_ref[s, :, lanes]
                high = f.astype(jnp.bfloat16)
                left_ref[rows, 0:FACE] = high
                left_ref[rows, FACE : 2 * FACE] = (f - high.astype(jnp.float32)).astype(jnp.bfloat16)
                left_ref[rows, 2 * FACE :] = jnp.where(parity == p, both, jnp.zeros_like(both))
        sums_ref[...] = jnp.dot(left_ref[...], weights_ref[...], preferred_element_type=jnp.float32)

    def finish(pair, odd):
        sums_ref = (sums_even_ref, sums_odd_ref)[odd]
        for p in range(2):
            inner, before, here, after = (
                pl.ds(pl.multiple_of((2 * pair + p + n) * FACE, FACE), FACE) for n in (0, 0, 1, 2)
            )
            for g in range(slots // 8):
                rows = slice(g * 8, (g + 1) * 8)
                smooth, over, vx, vy, vz = (
                    jnp.concatenate([wide_ref[n, rows, :]] * 2, axis=1) for n in range(5)
                )
                fuel = [fields_ref[s, rows, here] for s in range(species)]
                burning = fuel[0] * fuel[1] * over
                fuel = [f * burning for f in fuel]
                for s in range(species):
                    react = None
                    for k in range(species):
                        rate = rates_ref[s * species + k]
                        term = jnp.concatenate([rate, rate], axis=1) * fuel[k]
                        react = term if react is None else react + term
                    low, high = fields_ref[s, rows, before], fields_ref[s, rows, after]
                    line = (p * species + s) * slots + g * 8
                    total, along_y, along_z = (
                        sums_ref[line : line + 8, d * FACE : (d + 1) * FACE] for d in range(3)
                    )
                    tend = smooth * (total + (low + high)) - vx * (high - low)
                    tend = (tend - vy * along_y) + (react - vz * along_z)
                    base_ref[s, rows, inner] += (step_size * 23.0 / 12.0) * tend
                    sums_ref[line : line + 8, 0:FACE] = tend
            for s in range(species):
                line = (p * species + s) * slots
                new_tend_ref[s, :, inner] = sums_ref[line : line + slots, 0:FACE].astype(jnp.bfloat16)

    for copy in (*ends(), *cells_in(0)):
        copy.wait()
    sums(0, 0)

    def four(c, carry):
        bases(c).wait()
        sums(2 * c + 1, 1)
        finish(2 * c, 0)

        @pl.when(c + 1 < chunks)
        def _():
            for copy in cells_in(c + 1):
                copy.wait()

        sums(jnp.minimum(2 * c + 2, 2 * (chunks - 1)), 0)
        finish(2 * c + 1, 1)
        for copy in stores(c):
            copy.start()
        return carry

    lax.fori_loop(0, chunks, four, 0)
    for c in range(chunks):
        for copy in stores(c):
            copy.wait()


def add_kernel(
    me_ref, live_ref, table_ref, fields_hbm, arrived_hbm, out_hbm, fields_ref, arrived_ref, got, sent
):
    species, peers = arrived_ref.shape[:2]
    slots = fields_ref.shape[1]

    def fetches(s):
        part = arrived_hbm.at[:, pl.ds(s * ROWS, ROWS)]
        return (
            pltpu.make_async_copy(part, arrived_ref.at[s], got.at[0, s]),
            pltpu.make_async_copy(fields_hbm.at[s], fields_ref.at[s], got.at[1, s]),
        )

    def store(s):
        return pltpu.make_async_copy(fields_ref.at[s], out_hbm.at[s], sent.at[s])

    for s in range(species):
        for copy in fetches(s):
            copy.start()
    me, first = me_ref[0], pl.multiple_of(me_ref[1] * LANES, LANES)
    notes = table_ref[:, pl.ds(first, LANES)]
    destination = notes[:, slots : 2 * slots]
    target = notes[:, 2 * slots : 3 * slots]
    peer = lax.broadcasted_iota(jnp.int32, (peers, slots), 0)
    mine = (destination == me.astype(jnp.float32)) & (peer != me)
    slot = jnp.max(jnp.where(mine, target, -1.0), axis=1, keepdims=True)
    index = lax.broadcasted_iota(jnp.int32, (peers, slots), 1)
    hot = (slot == index.astype(jnp.float32)) & (index < live_ref[0])
    hot = jnp.where(hot, step_size / SCALE, 0.0)
    hot = jnp.concatenate([hot, hot], axis=0).T.astype(jnp.bfloat16)
    for s in range(species):
        for copy in fetches(s):
            copy.wait()
        flat = arrived_ref.at[s].reshape(peers * ROWS, LANES)
        for c in range(ROWS // 2):
            lanes = slice(c * 2 * LANES, (c + 1) * 2 * LANES)
            arrived = jnp.concatenate(
                [flat[pl.ds(2 * c + k, peers, stride=ROWS), :] for k in range(2)], axis=1
            )
            high = arrived.astype(jnp.bfloat16)
            low = (arrived - high.astype(jnp.float32)).astype(jnp.bfloat16)
            fields_ref[s, :, lanes] += jnp.dot(
                hot, jnp.concatenate([high, low], axis=0), preferred_element_type=jnp.float32
            )
        store(s).start()
    for s in range(species):
        store(s).wait()


def smem():
    return pl.BlockSpec(memory_space=pltpu.SMEM)


def whole(shape):
    return pl.BlockSpec(shape, lambda i: (0,) * len(shape))


def params(mib, semantics=None):
    return pltpu.CompilerParams(vmem_limit_bytes=mib << 20, dimension_semantics=semantics)


def local(
    fields,
    ghosts,
    velocity,
    rate_matrix,
    recent_tend,
    older_tend,
    destination,
    target_slot,
    live_counts,
    tile_ids,
    sensor,
    flame_flags,
):
    slots, species, cells = fields.shape
    peers = lax.axis_size(TEAM)
    brick = sensor.shape[0]
    me = jnp.stack([lax.axis_index(TEAM), lax.axis_index("grp")]).astype(jnp.int32)
    fields, ghosts, recent, older = (
        a.transpose(1, 0, 2) for a in (fields, ghosts, recent_tend, older_tend)
    )
    moves = jnp.stack([destination, target_slot])

    raw = pl.pallas_call(
        raw_kernel,
        name="raw_sensor",
        out_shape=jax.ShapeDtypeStruct(sensor.shape, jnp.bfloat16),
        in_specs=[smem(), pl.BlockSpec(memory_space=pltpu.VMEM)],
        out_specs=pl.BlockSpec(memory_space=pltpu.VMEM),
        compiler_params=params(58),
    )(flame_flags, sensor)
    below = passed_along(raw, "pen", 1)
    above = passed_along(raw, "pen", -1)

    anywhere = pl.BlockSpec(memory_space=pl.ANY)
    in_hbm = pl.BlockSpec(memory_space=pltpu.HBM)
    vmem = pl.BlockSpec(memory_space=pltpu.VMEM)
    outgoing = pl.pallas_call(
        send_kernel,
        name="outgoing_histories",
        out_shape=jax.ShapeDtypeStruct((peers, species * ROWS, LANES), jnp.float32),
        in_specs=[smem(), vmem, in_hbm, in_hbm],
        out_specs=vmem,
        scratch_shapes=[
            pltpu.VMEM(recent.shape, jnp.bfloat16),
            pltpu.VMEM(older.shape, jnp.bfloat16),
            pltpu.SemaphoreType.DMA((2, species)),
        ],
        compiler_params=params(50),
        cost_estimate=pl.CostEstimate(flops=0, bytes_accessed=8 << 20, transcendentals=0),
    )(me, destination.reshape(1, slots), recent, older)
    outgoing = outgoing.astype(jnp.float16)

    shape = jax.ShapeDtypeStruct((species, slots, cells), jnp.float32)
    rims = jax.ShapeDtypeStruct((species, slots, TE * LANES), jnp.bfloat16)
    base, rims = pl.pallas_call(
        prepare_kernel,
        name="base_and_rims",
        out_shape=(shape, rims),
        in_specs=[smem(), smem(), vmem] + [anywhere] * 4,
        out_specs=(anywhere, anywhere),
        scratch_shapes=[
            pltpu.VMEM(shape.shape, jnp.float32),
            pltpu.VMEM(shape.shape, jnp.bfloat16),
            pltpu.VMEM(shape.shape, jnp.bfloat16),
            pltpu.VMEM(ghosts.shape, jnp.float32),
            pltpu.VMEM(rims.shape, jnp.bfloat16),
            pltpu.SemaphoreType.DMA((4, species)),
            pltpu.SemaphoreType.DMA((2, species)),
        ],
        compiler_params=params(58),
        cost_estimate=pl.CostEstimate(flops=0, bytes_accessed=24 << 20, transcendentals=0),
    )(me, live_counts, moves, fields, recent, older, ghosts)
    below, above, base, rims, outgoing = lax.optimization_barrier(
        (below, above, base, rims, outgoing)
    )

    notes = jnp.concatenate(
        [jnp.zeros((1, slots), jnp.float32), moves.astype(jnp.float32).reshape(1, 2 * slots)], axis=1
    )
    notes = jnp.pad(notes, ((0, 0), (0, LANES - 3 * slots)))
    filtered, row = pl.pallas_call(
        filter_kernel,
        name="filtered_sensor",
        out_shape=(
            jax.ShapeDtypeStruct(sensor.shape, jnp.float32),
            jax.ShapeDtypeStruct((1, LANES), jnp.float32),
        ),
        in_specs=[smem()] + [vmem] * 5,
        out_specs=(vmem, vmem),
        compiler_params=params(32),
        cost_estimate=pl.CostEstimate(flops=0, bytes_accessed=4 << 20, transcendentals=0),
    )(flame_flags, jnp.asarray(banded(brick, brick)), sensor, below, above, notes)
    owner, lane = tile_ids // slots, tile_ids % slots
    tile_place = jnp.stack([owner % peers, owner // peers * LANES + lane], axis=1)
    speed = jnp.pad(velocity.T, ((0, 0), (0, 5)))

    rows = gathered(row, ("pen",))
    rows, outgoing = lax.optimization_barrier((rows, outgoing))
    arrived = lax.all_to_all(outgoing, TEAM, split_axis=0, concat_axis=0, tiled=True)
    table = gathered(rows, ("grp", "mig"))
    arrived = arrived.astype(jnp.float32)

    weights = jnp.asarray(plane_weights(), jnp.bfloat16)
    left = pltpu.VMEM((2 * species * slots, 6 * LANES), jnp.bfloat16)
    sums = pltpu.VMEM((2 * species * slots, 3 * FACE), jnp.float32)
    new_fields, new_tend = pl.pallas_call(
        main_kernel,
        name="updates",
        out_shape=(shape, jax.ShapeDtypeStruct(shape.shape, jnp.bfloat16)),
        in_specs=[smem()] * 2 + [vmem] * 3 + [anywhere] * 5,
        out_specs=(anywhere, anywhere),
        scratch_shapes=[
            pltpu.VMEM(weights.shape, jnp.bfloat16),
            pltpu.VMEM((species, slots, cells + 2 * FACE), jnp.float32),
            pltpu.VMEM(rims.shape, jnp.bfloat16),
            pltpu.VMEM(shape.shape, jnp.float32),
            pltpu.VMEM(shape.shape, jnp.bfloat16),
            pltpu.VMEM((species * species, 8, LANES), jnp.float32),
            pltpu.VMEM((5, slots, LANES), jnp.float32),
            left,
            left,
            sums,
            sums,
            pltpu.SemaphoreType.DMA((4, TE // PLANES)),
            pltpu.SemaphoreType.DMA((2, TE // PLANES)),
        ],
        compiler_params=params(58),
        cost_estimate=pl.CostEstimate(flops=0, bytes_accessed=40 << 20, transcendentals=0),
    )(live_counts, rate_matrix, table, tile_place, speed, weights, fields, ghosts, rims, base)

    new_fields = pl.pallas_call(
        add_kernel,
        name="arrived_histories",
        out_shape=shape,
        in_specs=[smem(), smem(), vmem, anywhere, anywhere],
        out_specs=anywhere,
        scratch_shapes=[
            pltpu.VMEM(shape.shape, jnp.float32),
            pltpu.VMEM((species, peers, ROWS, LANES), jnp.float32),
            pltpu.SemaphoreType.DMA((2, species)),
            pltpu.SemaphoreType.DMA((species,)),
        ],
        compiler_params=params(58),
        cost_estimate=pl.CostEstimate(flops=0, bytes_accessed=12 << 20, transcendentals=0),
    )(me, live_counts, table, new_fields, arrived)
    return new_fields.transpose(1, 0, 2), new_tend.transpose(1, 0, 2), filtered


def gathered(row, axes):
    for axis in axes:
        count = lax.axis_size(axis)
        here = lax.axis_index(axis)
        rows = [row] + [passed_along(row, axis, by) for by in range(1, count)]
        height, width = row.shape
        if axis == "grp":
            table = jnp.zeros((height, count * width), row.dtype)
        else:
            table = jnp.zeros((count * height, width), row.dtype)
        for by, part in enumerate(rows):
            place = (here - by) % count
            place = (0, place * width) if axis == "grp" else (place * height, 0)
            table = lax.dynamic_update_slice(table, part, place)
        row = table
    return row


def solution(mesh):
    split = P(EVERY, None, None)
    return jax.shard_map(
        local,
        mesh=mesh,
        in_specs=(
            split,
            split,
            P(None, EVERY),
            P(),
            split,
            split,
            P(EVERY),
            P(EVERY),
            P(EVERY),
            P(EVERY),
            P("pen", ("grp", "mig")),
            P("pen", ("grp", "mig")),
        ),
        out_specs=(split, split, P("pen", ("grp", "mig"))),
        check_vma=False,
    )
```

profile of v0, /device:TPU:0, one launch (start us, length us, event | category | flops | bytes accessed | tf_op | source)
XLA Modules:
  0.0 76.8 jit_solution(14242497949156042678)
XLA Ops:
  0.6 1.8 %raw_sensor.1 = bf16[32,4096]{1,0:T(8,128)(2,1)} custom-call(s32[2,16]{1,0:T(2,128)} %flags_ref.3, f32[32,4096]{1,0:T(8,128)} %sensor_ref.3), custom_call_target="tpu_custom_call" | custom-call | tf_op jit(solution)/shard_map/raw_sensor/pallas_call | solution.py:471
  2.4 5.0 %collective-permute-start.1 = (bf16[32,4096]{1,0:T(8,128)(2,1)}, bf16[32,4096]{1,0:T(8,128)(2,1)S(1)}, u32[]{:S(2)}, u32[]{:S(2)}) collective-permute-start(bf16[32,4096]{1,0:T(8,128)(2,1)} %raw_sensor.1), channel_id=1, source_target_pairs={{0,3},{1,0},{2,1},{3,2},{4,7},{5,4},{6,5},{7,6},{8,11},{9,8},{10,9... | collective-permute-start | bytes 786440 | tf_op jit(solution)/shard_map/ppermute | solution.py:30
  8.1 1.2 %fusion.3 = (f32[2,32]{1,0:T(2,128)S(1)}, s32[2,32]{1,0:T(2,128)}) fusion(s32[1,32]{1,0:T(1,128)} %bitcast.27, s32[1,32]{1,0:T(1,128)} %bitcast.15), kind=kLoop, calls=%fused_computation.22 | loop fusion | flops 128 | bytes 768 | tf_op jit(solution)/shard_map/convert_element_type | solution.py:526
  9.5 0.7 copy-done.4
  10.2 4.9 %outgoing_histories.1 = f32[16,288,128]{2,1,0:T(8,128)S(1)} custom-call(s32[2]{0:T(128)S(1)} %pad_add_fusion.2.me_ref, s32[1,32]{1,0:T(1,128)S(1)} %bitcast.16, bf16[9,32,4096]{2,1,0:T(8,128)(2,1)} %bitcast.19, bf16[9,32,4096]{2,1,0:T(8,128)(2,1)} %bitcast.21), custom_call_target="tpu_custom_call" | custom-call | bytes 8388608 | tf_op jit(solution)/shard_map/outgoing_histories/pallas_call | solution.py:485
  15.1 1.2 %convert_element_type.23 = f16[16,288,128]{2,1,0:T(8,128)(2,1)} convert(f32[16,288,128]{2,1,0:T(8,128)S(1)} %outgoing_histories.1) | non-fusion elementwise | flops 589824 | bytes 3538944 | tf_op jit(solution)/shard_map/convert_element_type | solution.py:499
  16.4 8.0 %base_and_rims.1 = (f32[9,32,4096]{2,1,0:T(8,128)}, bf16[9,32,2048]{2,1,0:T(8,128)(2,1)}) custom-call(s32[2]{0:T(128)} %copy-done.2, s32[1]{0:T(128)S(6)} %copy.32.live_ref, s32[2,32]{1,0:T(2,128)} %get-tuple-element.32.moves_ref, f32[9,32,4096]{2,1,0:T(8,128)} %bitcast.17, bf16[9,32,4096]{2,1,0:T(8,128)(2,1)} %bitcast.20, bf16[9,32,4096]{2,1,0:T(8,128)(2,1)} %bitcast.22, ...), custom_call_target="tpu_custom_call" | custom-call | bytes 25165824 | tf_op jit(solution)/shard_map/base_and_rims/pallas_call | solution.py:503
  24.4 2.2 %filtered_sensor.1 = (f32[32,4096]{1,0:T(8,128)}, f32[1,128]{1,0:T(1,128)S(1)}) custom-call(s32[2,16]{1,0:T(2,128)S(1)} %copy-done.3, f32[32,96]{1,0:T(8,128)S(1)} %copy-done.1, f32[32,4096]{1,0:T(8,128)S(1)} %copy-done, bf16[32,4096]{1,0:T(8,128)(2,1)S(1)} %collective-permute-done.below_ref, bf16[32,4096]{1,0:T(8,128)(2,1)S(1)} %collective-permute-done.1.above_ref, ...), custom_call_target="tpu_custom_call" | custom-call | bytes 4194304 | tf_op jit(solution)/shard_map/filtered_sensor/pallas_call | solution.py:529
  26.6 4.4 %collective-permute-start.3 = (f32[1,128]{1,0:T(1,128)S(1)}, f32[1,128]{1,0:T(1,128)S(1)}, u32[]{:S(2)}, u32[]{:S(2)}) collective-permute-start(f32[1,128]{1,0:T(1,128)S(1)} %get-tuple-element.20), channel_id=1, source_target_pairs={{0,2},{1,3},{2,0},{3,1},{4,6},{5,7},{6,4},{7,5},{8,10},{9,11},{10,... | collective-permute-start | bytes 1544 | tf_op jit(solution)/shard_map/ppermute | solution.py:30
  31.0 0.9 %collective-permute-done.2 = f32[1,128]{1,0:T(1,128)S(1)} collective-permute-done((f32[1,128]{1,0:T(1,128)S(1)}, f32[1,128]{1,0:T(1,128)S(1)}, u32[]{:S(2)}, u32[]{:S(2)}) %collective-permute-start.2) | collective-permute-done | bytes 544 | tf_op jit(solution)/shard_map/ppermute | solution.py:30
  32.5 2.0 %collective-permute-done.4 = f32[1,128]{1,0:T(1,128)S(1)} collective-permute-done((f32[1,128]{1,0:T(1,128)S(1)}, f32[1,128]{1,0:T(1,128)S(1)}, u32[]{:S(2)}, u32[]{:S(2)}) %collective-permute-start.4) | collective-permute-done | bytes 544 | tf_op jit(solution)/shard_map/ppermute | solution.py:30
  34.6 4.1 %all-to-all-start = ((f16[16,288,128]{2,1,0:T(8,128)(2,1)}), f16[16,288,128]{2,1,0:T(8,128)(2,1)S(1)}, u32[]{:S(2)}, u32[]{:S(2)}) async-start(f16[16,288,128]{2,1,0:T(8,128)(2,1)} %convert_element_type.23), calls=%async_computation | async-start | bytes 2359296 | tf_op jit(solution)/shard_map/all_to_all | solution.py:547
  38.9 0.7 copy.21.tile_ref
  39.6 0.6 pad.10.speed_ref
  40.2 1.5 %collective-permute-start.5 = (f32[4,128]{1,0:T(4,128)S(1)}, f32[4,128]{1,0:T(4,128)S(1)}, u32[]{:S(2)}, u32[]{:S(2)}) collective-permute-start(f32[4,128]{1,0:T(4,128)S(1)} %dynamic_update_slice.33), channel_id=1, source_target_pairs={{0,16},{16,0},{1,17},{17,1},{2,18},{18,2},{3,19},{19,3},{4,20},{20... | collective-permute-start | bytes 6152 | tf_op jit(solution)/shard_map/ppermute | solution.py:30
  41.8 2.1 %collective-permute-done.5 = f32[4,128]{1,0:T(4,128)S(1)} collective-permute-done((f32[4,128]{1,0:T(4,128)S(1)}, f32[4,128]{1,0:T(4,128)S(1)}, u32[]{:S(2)}, u32[]{:S(2)}) %collective-permute-start.5) | collective-permute-done | bytes 2080 | tf_op jit(solution)/shard_map/ppermute | solution.py:30
  43.8 0.7 collective-permute-start.8
  44.5 1.1 %collective-permute-start.7 = (f32[4,256]{1,0:T(4,128)S(1)}, f32[4,256]{1,0:T(4,128)S(1)}, u32[]{:S(2)}, u32[]{:S(2)}) collective-permute-start(f32[4,256]{1,0:T(4,128)S(1)} %constant_dynamic-update-slice_fusion.4), channel_id=1, source_target_pairs={{0,8},{4,12},{8,0},{12,4},{1,9},{5,13},{9,1},{13,5},{2,10},{6,14},... | collective-permute-start | bytes 12296 | tf_op jit(solution)/shard_map/ppermute | solution.py:30
  45.9 3.1 %collective-permute-done.6 = f32[4,256]{1,0:T(4,128)S(1)} collective-permute-done((f32[4,256]{1,0:T(4,128)S(1)}, f32[4,256]{1,0:T(4,128)S(1)}, u32[]{:S(2)}, u32[]{:S(2)}) %collective-permute-start.6) | collective-permute-done | bytes 4128 | tf_op jit(solution)/shard_map/ppermute | solution.py:30
  49.0 0.7 collective-permute-done.7
  49.8 0.6 copy-done.5
  50.3 18.6 %updates.1 = (f32[9,32,4096]{2,1,0:T(8,128)}, bf16[9,32,4096]{2,1,0:T(8,128)(2,1)}) custom-call(s32[1]{0:T(128)S(6)} %copy.32.live_ref, f32[9,9]{1,0:T(8,128)} %rate_ref.1, f32[16,256]{1,0:T(8,128)} %copy-done.5, s32[32,2]{1,0:T(8,128)} %copy.21.tile_ref, f32[32,8]{1,0:T(8,128)} %pad.10.speed_ref, bf16[768,768]{1,0:T(8,128)(2,1)} %constant.141.clone.weights_hbm, ...), custom_call_target="tpu_custom_call" | custom-call | bytes 41943040 | tf_op jit(solution)/shard_map/updates/pallas_call | solution.py:554
  68.9 1.7 %convert_element_type.26.arrived_hbm = f32[16,288,128]{2,1,0:T(8,128)} convert(f16[16,288,128]{2,1,0:T(8,128)(2,1)S(1)} %all-to-all-done) | non-fusion elementwise | flops 589824 | bytes 3538944 | tf_op jit(solution)/shard_map/convert_element_type | solution.py:549
  70.6 6.2 %arrived_histories.1 = f32[9,32,4096]{2,1,0:T(8,128)} custom-call(s32[2]{0:T(128)} %copy-done.2, s32[1]{0:T(128)S(6)} %copy.32.live_ref, f32[16,256]{1,0:T(8,128)} %copy-done.5, f32[9,32,4096]{2,1,0:T(8,128)} %get-tuple-element.25.fields_hbm, f32[16,288,128]{2,1,0:T(8,128)} %convert_element_type.26.arrived_hbm), custom_call_target="tpu_custom_call" | custom-call | bytes 12582912 | tf_op jit(solution)/shard_map/arrived_histories/pallas_call | solution.py:579
  (43 shorter events, 1.3 us)
Async XLA Ops:
  2.4 22.0 %collective-permute-start.1 = (bf16[32,4096]{1,0:T(8,128)(2,1)}, bf16[32,4096]{1,0:T(8,128)(2,1)S(1)}, u32[]{:S(2)}, u32[]{:S(2)}) collective-permute-start(bf16[32,4096]{1,0:T(8,128)(2,1)} %raw_sensor.1), channel_id=1, source_target_pairs={{0,3},{1,0},{2,1},{3,2},{4,7},{5,4},{6,5},{7,6},{8,11},{9,8},{10,9... | collective-permute-start | bytes 786440 | tf_op jit(solution)/shard_map/ppermute | solution.py:30
  7.5 16.9 %collective-permute-start = (bf16[32,4096]{1,0:T(8,128)(2,1)}, bf16[32,4096]{1,0:T(8,128)(2,1)S(1)}, u32[]{:S(2)}, u32[]{:S(2)}) collective-permute-start(bf16[32,4096]{1,0:T(8,128)(2,1)} %raw_sensor.1), channel_id=1, source_target_pairs={{0,1},{1,2},{2,3},{3,0},{4,5},{5,6},{6,7},{7,4},{8,9},{9,10},{10,1... | collective-permute-start | bytes 786440 | tf_op jit(solution)/shard_map/ppermute | solution.py:30
  9.5 5.6 %copy-start.2 = (s32[2]{0:T(128)}, s32[2]{0:T(128)S(1)}, u32[]{:S(2)}) copy-start(s32[2]{0:T(128)S(1)} %pad_add_fusion.2.me_ref) | copy-start | bytes 28
  9.5 0.7 copy-start.4
  16.4 8.0 %copy-start = (f32[32,4096]{1,0:T(8,128)S(1)}, f32[32,4096]{1,0:T(8,128)}, u32[]{:S(2)}) copy-start(f32[32,4096]{1,0:T(8,128)} %sensor_ref.3) | copy-start | bytes 1572868
  16.4 8.0 %copy-start.1 = (f32[32,96]{1,0:T(8,128)S(1)}, f32[32,96]{1,0:T(8,128)}, u32[]{:S(2)}) copy-start(f32[32,96]{1,0:T(8,128)} %constant.140.clone.weights_ref) | copy-start | bytes 36868
  16.4 8.0 %copy-start.3 = (s32[2,16]{1,0:T(2,128)S(1)}, s32[2,16]{1,0:T(2,128)}, u32[]{:S(2)}) copy-start(s32[2,16]{1,0:T(2,128)} %flags_ref.3) | copy-start | bytes 388
  24.4 14.4 %copy-start.7 = (s32[32]{0:T(128)S(1)}, s32[32]{0:T(128)}, u32[]{:S(2)}) copy-start(s32[32]{0:T(128)} %param.23) | copy-start | bytes 388
  24.4 15.2 %copy-start.6 = (f32[3,32]{1,0:T(4,128)S(1)}, f32[3,32]{1,0:T(4,128)}, u32[]{:S(2)}) copy-start(f32[3,32]{1,0:T(4,128)} %param.16) | copy-start | bytes 1156
  26.6 5.3 %collective-permute-start.2 = (f32[1,128]{1,0:T(1,128)S(1)}, f32[1,128]{1,0:T(1,128)S(1)}, u32[]{:S(2)}, u32[]{:S(2)}) collective-permute-start(f32[1,128]{1,0:T(1,128)S(1)} %get-tuple-element.20), channel_id=1, source_target_pairs={{0,1},{1,2},{2,3},{3,0},{4,5},{5,6},{6,7},{7,4},{8,9},{9,10},{10,1... | collective-permute-start | bytes 1544 | tf_op jit(solution)/shard_map/ppermute | solution.py:30
  26.6 5.9 %collective-permute-start.3 = (f32[1,128]{1,0:T(1,128)S(1)}, f32[1,128]{1,0:T(1,128)S(1)}, u32[]{:S(2)}, u32[]{:S(2)}) collective-permute-start(f32[1,128]{1,0:T(1,128)S(1)} %get-tuple-element.20), channel_id=1, source_target_pairs={{0,2},{1,3},{2,0},{3,1},{4,6},{5,7},{6,4},{7,5},{8,10},{9,11},{10,... | collective-permute-start | bytes 1544 | tf_op jit(solution)/shard_map/ppermute | solution.py:30
  31.0 3.5 %collective-permute-start.4 = (f32[1,128]{1,0:T(1,128)S(1)}, f32[1,128]{1,0:T(1,128)S(1)}, u32[]{:S(2)}, u32[]{:S(2)}) collective-permute-start(f32[1,128]{1,0:T(1,128)S(1)} %get-tuple-element.20), channel_id=1, source_target_pairs={{0,3},{1,0},{2,1},{3,2},{4,7},{5,4},{6,5},{7,6},{8,11},{9,8},{10,9... | collective-permute-start | bytes 1544 | tf_op jit(solution)/shard_map/ppermute | solution.py:30
  34.6 34.4 %all-to-all-start = ((f16[16,288,128]{2,1,0:T(8,128)(2,1)}), f16[16,288,128]{2,1,0:T(8,128)(2,1)S(1)}, u32[]{:S(2)}, u32[]{:S(2)}) async-start(f16[16,288,128]{2,1,0:T(8,128)(2,1)} %convert_element_type.23), calls=%async_computation | async-start | bytes 2359296 | tf_op jit(solution)/shard_map/all_to_all | solution.py:547
  40.2 3.6 %collective-permute-start.5 = (f32[4,128]{1,0:T(4,128)S(1)}, f32[4,128]{1,0:T(4,128)S(1)}, u32[]{:S(2)}, u32[]{:S(2)}) collective-permute-start(f32[4,128]{1,0:T(4,128)S(1)} %dynamic_update_slice.33), channel_id=1, source_target_pairs={{0,16},{16,0},{1,17},{17,1},{2,18},{18,2},{3,19},{19,3},{4,20},{20... | collective-permute-start | bytes 6152 | tf_op jit(solution)/shard_map/ppermute | solution.py:30
  43.8 5.9 %collective-permute-start.8 = (f32[4,256]{1,0:T(4,128)S(1)}, f32[4,256]{1,0:T(4,128)S(1)}, u32[]{:S(2)}, u32[]{:S(2)}) collective-permute-start(f32[4,256]{1,0:T(4,128)S(1)} %constant_dynamic-update-slice_fusion.4), channel_id=1, source_target_pairs={{0,12},{4,0},{8,4},{12,8},{1,13},{5,1},{9,5},{13,9},{2,14},{6,2},{... | collective-permute-start | bytes 12296 | tf_op jit(solution)/shard_map/ppermute | solution.py:30
  44.5 5.2 %collective-permute-start.7 = (f32[4,256]{1,0:T(4,128)S(1)}, f32[4,256]{1,0:T(4,128)S(1)}, u32[]{:S(2)}, u32[]{:S(2)}) collective-permute-start(f32[4,256]{1,0:T(4,128)S(1)} %constant_dynamic-update-slice_fusion.4), channel_id=1, source_target_pairs={{0,8},{4,12},{8,0},{12,4},{1,9},{5,13},{9,1},{13,5},{2,10},{6,14},... | collective-permute-start | bytes 12296 | tf_op jit(solution)/shard_map/ppermute | solution.py:30
  45.7 3.3 %collective-permute-start.6 = (f32[4,256]{1,0:T(4,128)S(1)}, f32[4,256]{1,0:T(4,128)S(1)}, u32[]{:S(2)}, u32[]{:S(2)}) collective-permute-start(f32[4,256]{1,0:T(4,128)S(1)} %constant_dynamic-update-slice_fusion.4), channel_id=1, source_target_pairs={{0,4},{4,8},{8,12},{12,0},{1,5},{5,9},{9,13},{13,1},{2,6},{6,10},{... | collective-permute-start | bytes 12296 | tf_op jit(solution)/shard_map/ppermute | solution.py:30
  49.7 0.6 copy-start.5
where the time goes:
time: 77.2 us; the launch traced here: 76.8 us
  Pallas kernels  41.6 us (54%)
  starting transfers between devices  17.1 us (22%)
  waiting for transfers between devices  9.32 us (12%)
  other arithmetic  4.24 us (5%)
  local copies, waits for them, and re-layouts  2.99 us (4%)
  between operations  1.54 us (2%)
    pallas_call x1, Pallas kernels, local(): pl.pallas_call(main_kernel, name='updates', out_shape=(shape, jax.ShapeDt...  18.6 us
    ppermute x9, starting transfers between devices, passed_along(): return lax.ppermute(x, axis, [(i, (i + by) % peers) for i in range(peers)])  13 us
    ppermute x9, waiting for transfers between devices, passed_along(): return lax.ppermute(x, axis, [(i, (i + by) % peers) for i in range(peers)])  9.32 us
    pallas_call x1, Pallas kernels, local(): pl.pallas_call(prepare_kernel, name='base_and_rims', out_shape=(shape, ri...  7.96 us
    pallas_call x1, Pallas kernels, local(): pl.pallas_call(add_kernel, name='arrived_histories', out_shape=shape, in_...  6.18 us
    pallas_call x1, Pallas kernels, local(): pl.pallas_call(send_kernel, name='outgoing_histories', out_shape=jax.Shap...  4.91 us
    all_to_all x1, starting transfers between devices, local(): lax.all_to_all(outgoing, TEAM, split_axis=0, concat_axis=0, tiled=True)  4.11 us
    pallas_call x1, Pallas kernels, local(): pl.pallas_call(filter_kernel, name='filtered_sensor', out_shape=(jax.Shap...  2.16 us
  transfers between devices with their start and end apart: 10, of which 6 were waited for; matrix products, arithmetic and copies ran while one was open for 6% of the time, Pallas kernels for 41%

commit v1 on v0

--- a/solution.py
+++ b/solution.py
@@ -20,6 +20,7 @@
 
 SCALE = 4096.0
 PLANES = 4
+AHEAD = 4
 
 EVERY = ("grp", "mig", "pen")
 TEAM = ("mig", "pen")
@@ -49,9 +50,28 @@
             raw_ref[rows, cols] = (sensor_ref[rows, cols] * flag).astype(jnp.bfloat16)
 
 
-def filter_kernel(flags_ref, weights_ref, sensor_ref, below_ref, above_ref, notes_ref, filtered_ref, row_ref):
+def filter_kernel(
+    flags_ref,
+    weights_ref,
+    sensor_ref,
+    below_ref,
+    above_ref,
+    destination_ref,
+    target_ref,
+    filtered_ref,
+    row_ref,
+):
     lane = lax.broadcasted_iota(jnp.int32, (1, LANES), 1)
-    row = notes_ref[...]
+    slots = destination_ref.shape[1]
+    row = jnp.concatenate(
+        [
+            jnp.zeros((1, slots), jnp.float32),
+            destination_ref[...].astype(jnp.float32),
+            target_ref[...].astype(jnp.float32),
+            jnp.zeros((1, LANES - 3 * slots), jnp.float32),
+        ],
+        axis=1,
+    )
     brick = sensor_ref.shape[0]
     for k in range(TCOL):
         cols = slice(k * FACE, (k + 1) * FACE)
@@ -81,7 +101,7 @@
 
 
 def send_kernel(
-    me_ref, destination_ref, recent_hbm, older_hbm, out_ref, recent_ref, older_ref, got
+    destination_ref, recent_hbm, older_hbm, out_ref, recent_ref, older_ref, got
 ):
     species, slots, _ = recent_ref.shape
     peers = out_ref.shape[0]
@@ -92,13 +112,16 @@
             pltpu.make_async_copy(older_hbm.at[s], older_ref.at[s], got.at[1, s]),
         )
 
-    for s in range(species):
+    for s in range(AHEAD):
         for copy in fetches(s):
             copy.start()
     peer = lax.broadcasted_iota(jnp.int32, (peers, slots), 0)
-    hot = ((destination_ref[...] == peer) & (peer != me_ref[0])).astype(jnp.bfloat16)
+    hot = ((destination_ref[...] == peer) & (peer != lax.axis_index(TEAM))).astype(jnp.bfloat16)
     flat = out_ref.reshape(peers * species * ROWS, LANES)
     for s in range(species):
+        if s + AHEAD < species:
+            for copy in fetches(s + AHEAD):
+                copy.start()
         for copy in fetches(s):
             copy.wait()
         recent = jnp.dot(hot, recent_ref[s], preferred_element_type=jnp.float32)
@@ -111,9 +134,9 @@
 
 
 def prepare_kernel(
-    me_ref,
     live_ref,
-    moves_ref,
+    destination_ref,
+    target_ref,
     fields_hbm,
     recent_hbm,
     older_hbm,
@@ -148,17 +171,22 @@
             pltpu.make_async_copy(rims_ref.at[s], rims_hbm.at[s], sent.at[1, s]),
         )
 
-    for s in range(species):
+    for s in range(AHEAD):
         for copy in fetches(s):
             copy.start()
     slot = lax.broadcasted_iota(jnp.int32, (slots, slots), 0)
-    keep = (moves_ref[0:1, :] == me_ref[0]) & (moves_ref[1:2, :] == slot)
+    keep = (destination_ref[...] == lax.axis_index(TEAM)) & (target_ref[...] == slot)
     keep = keep.astype(jnp.bfloat16)
     live = lax.broadcasted_iota(jnp.int32, (slots, 1), 0) < live_ref[0]
     live = jnp.where(live, 1.0, 0.0)
     quarter = lax.broadcasted_iota(jnp.int32, (slots, LANES), 1) // (2 * TE)
 
     def one(s, carry):
+        @pl.when(s + AHEAD < species)
+        def _():
+            for copy in fetches(s + AHEAD):
+                copy.start()
+
         for copy in fetches(s):
             copy.wait()
         recent = jnp.dot(keep, recent_ref[s], preferred_element_type=jnp.float32)
@@ -212,8 +240,8 @@
     live_ref,
     rate_ref,
     table_ref,
-    tile_ref,
-    speed_ref,
+    tiles_ref,
+    velocity_ref,
     weights_hbm,
     fields_hbm,
     ghosts_hbm,
@@ -286,11 +314,16 @@
 
     for copy in ends():
         copy.start()
-    for c in range(chunks):
+    for c in range(2):
         for copy in (*cells_in(c), bases(c)):
             copy.start()
 
-    wanted = lax.broadcasted_iota(jnp.int32, (slots, peers), 1) == tile_ref[:, 0:1]
+    marks = jnp.concatenate(
+        [velocity_ref[...], tiles_ref[...].astype(jnp.float32), jnp.zeros((4, slots), jnp.float32)], axis=0
+    ).T
+    tiles = marks[:, 3:4].astype(jnp.int32)
+    owner = tiles // slots
+    wanted = lax.broadcasted_iota(jnp.int32, (slots, peers), 1) == owner % peers
     picked = jnp.dot(
         wanted.astype(jnp.float32),
         table_ref[...],
@@ -298,11 +331,12 @@
         preferred_element_type=jnp.float32,
     )
     lane = lax.broadcasted_iota(jnp.int32, picked.shape, 1)
-    thick = jnp.sum(jnp.where(lane == tile_ref[:, 1:2], picked, 0.0), axis=1, keepdims=True)
+    spot = owner // peers * LANES + tiles % slots
+    thick = jnp.sum(jnp.where(lane == spot, picked, 0.0), axis=1, keepdims=True)
     live = lax.broadcasted_iota(jnp.int32, (slots, 1), 0) < live_ref[0]
     live = jnp.where(live, 1.0, 0.0)
     parts = [viscous * thick * live, live / thick]
-    parts += [0.5 * live * speed_ref[:, d : d + 1] for d in range(3)]
+    parts += [0.5 * live * marks[:, d : d + 1] for d in range(3)]
     for n, part in enumerate(parts):
         wide_ref[n] = jnp.broadcast_to(part, (slots, LANES))
     for s in range(species):
@@ -363,6 +397,11 @@
     sums(0, 0)
 
     def four(c, carry):
+        @pl.when(c + 2 < chunks)
+        def _():
+            for copy in (*cells_in(c + 2), bases(c + 2)):
+                copy.start()
+
         bases(c).wait()
         sums(2 * c + 1, 1)
         finish(2 * c, 0)
@@ -385,7 +424,7 @@
 
 
 def add_kernel(
-    me_ref, live_ref, table_ref, fields_hbm, arrived_hbm, out_hbm, fields_ref, arrived_ref, got, sent
+    live_ref, table_ref, fields_hbm, arrived_hbm, out_hbm, fields_ref, arrived_ref, got, sent
 ):
     species, peers = arrived_ref.shape[:2]
     slots = fields_ref.shape[1]
@@ -400,10 +439,10 @@
     def store(s):
         return pltpu.make_async_copy(fields_ref.at[s], out_hbm.at[s], sent.at[s])
 
-    for s in range(species):
+    for s in range(AHEAD):
         for copy in fetches(s):
             copy.start()
-    me, first = me_ref[0], pl.multiple_of(me_ref[1] * LANES, LANES)
+    me, first = lax.axis_index(TEAM), pl.multiple_of(lax.axis_index("grp") * LANES, LANES)
     notes = table_ref[:, pl.ds(first, LANES)]
     destination = notes[:, slots : 2 * slots]
     target = notes[:, 2 * slots : 3 * slots]
@@ -415,6 +454,9 @@
     hot = jnp.where(hot, step_size / SCALE, 0.0)
     hot = jnp.concatenate([hot, hot], axis=0).T.astype(jnp.bfloat16)
     for s in range(species):
+        if s + AHEAD < species:
+            for copy in fetches(s + AHEAD):
+                copy.start()
         for copy in fetches(s):
             copy.wait()
         flat = arrived_ref.at[s].reshape(peers * ROWS, LANES)
@@ -462,11 +504,10 @@
     slots, species, cells = fields.shape
     peers = lax.axis_size(TEAM)
     brick = sensor.shape[0]
-    me = jnp.stack([lax.axis_index(TEAM), lax.axis_index("grp")]).astype(jnp.int32)
     fields, ghosts, recent, older = (
         a.transpose(1, 0, 2) for a in (fields, ghosts, recent_tend, older_tend)
     )
-    moves = jnp.stack([destination, target_slot])
+    moves = (destination.reshape(1, slots), target_slot.reshape(1, slots))
 
     raw = pl.pallas_call(
         raw_kernel,
@@ -486,7 +527,7 @@
         send_kernel,
         name="outgoing_histories",
         out_shape=jax.ShapeDtypeStruct((peers, species * ROWS, LANES), jnp.float32),
-        in_specs=[smem(), vmem, in_hbm, in_hbm],
+        in_specs=[vmem, in_hbm, in_hbm],
         out_specs=vmem,
         scratch_shapes=[
             pltpu.VMEM(recent.shape, jnp.bfloat16),
@@ -495,7 +536,7 @@
         ],
         compiler_params=params(50),
         cost_estimate=pl.CostEstimate(flops=0, bytes_accessed=8 << 20, transcendentals=0),
-    )(me, destination.reshape(1, slots), recent, older)
+    )(destination.reshape(1, slots), recent, older)
     outgoing = outgoing.astype(jnp.float16)
 
     shape = jax.ShapeDtypeStruct((species, slots, cells), jnp.float32)
@@ -504,7 +545,7 @@
         prepare_kernel,
         name="base_and_rims",
         out_shape=(shape, rims),
-        in_specs=[smem(), smem(), vmem] + [anywhere] * 4,
+        in_specs=[smem(), vmem, vmem] + [anywhere] * 4,
         out_specs=(anywhere, anywhere),
         scratch_shapes=[
             pltpu.VMEM(shape.shape, jnp.float32),
@@ -517,15 +558,8 @@
         ],
         compiler_params=params(58),
         cost_estimate=pl.CostEstimate(flops=0, bytes_accessed=24 << 20, transcendentals=0),
-    )(me, live_counts, moves, fields, recent, older, ghosts)
-    below, above, base, rims, outgoing = lax.optimization_barrier(
-        (below, above, base, rims, outgoing)
-    )
-
-    notes = jnp.concatenate(
-        [jnp.zeros((1, slots), jnp.float32), moves.astype(jnp.float32).reshape(1, 2 * slots)], axis=1
-    )
-    notes = jnp.pad(notes, ((0, 0), (0, LANES - 3 * slots)))
+    )(live_counts, *moves, fields, recent, older, ghosts)
+
     filtered, row = pl.pallas_call(
         filter_kernel,
         name="filtered_sensor",
@@ -533,17 +567,13 @@
             jax.ShapeDtypeStruct(sensor.shape, jnp.float32),
             jax.ShapeDtypeStruct((1, LANES), jnp.float32),
         ),
-        in_specs=[smem()] + [vmem] * 5,
+        in_specs=[smem()] + [vmem] * 6,
         out_specs=(vmem, vmem),
         compiler_params=params(32),
         cost_estimate=pl.CostEstimate(flops=0, bytes_accessed=4 << 20, transcendentals=0),
-    )(flame_flags, jnp.asarray(banded(brick, brick)), sensor, below, above, notes)
-    owner, lane = tile_ids // slots, tile_ids % slots
-    tile_place = jnp.stack([owner % peers, owner // peers * LANES + lane], axis=1)
-    speed = jnp.pad(velocity.T, ((0, 0), (0, 5)))
-
+    )(flame_flags, jnp.asarray(banded(brick, brick)), sensor, below, above, *moves)
     rows = gathered(row, ("pen",))
-    rows, outgoing = lax.optimization_barrier((rows, outgoing))
+    rows, outgoing, base, rims = lax.optimization_barrier((rows, outgoing, base, rims))
     arrived = lax.all_to_all(outgoing, TEAM, split_axis=0, concat_axis=0, tiled=True)
     table = gathered(rows, ("grp", "mig"))
     arrived = arrived.astype(jnp.float32)
@@ -574,13 +604,24 @@
         ],
         compiler_params=params(58),
         cost_estimate=pl.CostEstimate(flops=0, bytes_accessed=40 << 20, transcendentals=0),
-    )(live_counts, rate_matrix, table, tile_place, speed, weights, fields, ghosts, rims, base)
+    )(
+        live_counts,
+        rate_matrix,
+        table,
+        tile_ids.reshape(1, slots),
+        velocity,
+        weights,
+        fields,
+        ghosts,
+        rims,
+        base,
+    )
 
     new_fields = pl.pallas_call(
         add_kernel,
         name="arrived_histories",
         out_shape=shape,
-        in_specs=[smem(), smem(), vmem, anywhere, anywhere],
+        in_specs=[smem(), vmem, anywhere, anywhere],
         out_specs=anywhere,
         scratch_shapes=[
             pltpu.VMEM(shape.shape, jnp.float32),
@@ -590,7 +631,7 @@
         ],
         compiler_params=params(58),
         cost_estimate=pl.CostEstimate(flops=0, bytes_accessed=12 << 20, transcendentals=0),
-    )(me, live_counts, table, new_fields, arrived)
+    )(live_counts, table, new_fields, arrived)
     return new_fields.transpose(1, 0, 2), new_tend.transpose(1, 0, 2), filtered
 
 

time: 77.2 us -> 75.9 us (0.983)
  local copies, waits for them, and re-layouts: 2.99 us -> 1.48 us
  other arithmetic: 4.24 us -> 2.9 us
  waiting for transfers between devices: 9.32 us -> 10.6 us
  starting transfers between devices: 17.1 us -> 18 us
    ppermute x9, waiting for transfers between devices: 9.32 us -> 10.6 us  [passed_along(): return lax.ppermute(x, axis, [(i, (i + by) % peers) for i in range(peers)])]
    convert_element_type x1 -> x0, other arithmetic: 1.24 us -> none  [local(): moves.astype(jnp.float32).reshape(1, 2 * slots)]
    ppermute x9, starting transfers between devices: 13 us -> 14.1 us  [passed_along(): return lax.ppermute(x, axis, [(i, (i + by) % peers) for i in range(peers)])]
  transfers between devices with their start and end apart: 10 -> 10, of which waited for: 6 -> 5; matrix products, arithmetic and copies ran while one was open for 6% -> 2% of each run, Pallas kernels for 41% -> 41%
where the time goes in v1:
time: 75.9 us; the launch traced here: 75.5 us
  Pallas kernels  40.9 us (54%)
  starting transfers between devices  18 us (24%)
  waiting for transfers between devices  10.6 us (14%)
  other arithmetic  2.9 us (4%)
  between operations  1.53 us (2%)
  local copies, waits for them, and re-layouts  1.48 us (2%)
    pallas_call x1, Pallas kernels, local(): pl.pallas_call(main_kernel, name='updates', out_shape=(shape, jax.ShapeDt...  18.6 us
    ppermute x9, starting transfers between devices, passed_along(): return lax.ppermute(x, axis, [(i, (i + by) % peers) for i in range(peers)])  14.1 us
    ppermute x9, waiting for transfers between devices, passed_along(): return lax.ppermute(x, axis, [(i, (i + by) % peers) for i in range(peers)])  10.6 us
    pallas_call x1, Pallas kernels, local(): pl.pallas_call(prepare_kernel, name='base_and_rims', out_shape=(shape, ri...  7.75 us
    pallas_call x1, Pallas kernels, local(): pl.pallas_call(add_kernel, name='arrived_histories', out_shape=shape, in_...  6.23 us
    pallas_call x1, Pallas kernels, local(): pl.pallas_call(send_kernel, name='outgoing_histories', out_shape=jax.Shap...  4.37 us
    all_to_all x1, starting transfers between devices, local(): lax.all_to_all(outgoing, TEAM, split_axis=0, concat_axis=0, tiled=True)  3.93 us
    pallas_call x1, Pallas kernels, local(): pl.pallas_call(filter_kernel, name='filtered_sensor', out_shape=(jax.Shap...  2.17 us
  transfers between devices with their start and end apart: 10, of which 5 were waited for; matrix products, arithmetic and copies ran while one was open for 2% of the time, Pallas kernels for 41%

profile of v1, /device:TPU:0, one launch (start us, length us, event | category | flops | bytes accessed | tf_op | source)
XLA Modules:
  0.0 75.5 jit_solution(8092079164516086175)
XLA Ops:
  0.6 1.8 %raw_sensor.1 = bf16[32,4096]{1,0:T(8,128)(2,1)} custom-call(s32[2,16]{1,0:T(2,128)} %flags_ref.3, f32[32,4096]{1,0:T(8,128)} %sensor_ref.3), custom_call_target="tpu_custom_call" | custom-call | tf_op jit(solution)/shard_map/raw_sensor/pallas_call | solution.py:512
  2.4 3.0 %collective-permute-start = (bf16[32,4096]{1,0:T(8,128)(2,1)}, bf16[32,4096]{1,0:T(8,128)(2,1)S(1)}, u32[]{:S(2)}, u32[]{:S(2)}) collective-permute-start(bf16[32,4096]{1,0:T(8,128)(2,1)} %raw_sensor.1), channel_id=1, source_target_pairs={{0,1},{1,2},{2,3},{3,0},{4,5},{5,6},{6,7},{7,4},{8,9},{9,10},{10,1... | collective-permute-start | bytes 786440 | tf_op jit(solution)/shard_map/ppermute | solution.py:31
  5.4 2.0 %collective-permute-start.1 = (bf16[32,4096]{1,0:T(8,128)(2,1)}, bf16[32,4096]{1,0:T(8,128)(2,1)S(1)}, u32[]{:S(2)}, u32[]{:S(2)}) collective-permute-start(bf16[32,4096]{1,0:T(8,128)(2,1)} %raw_sensor.1), channel_id=1, source_target_pairs={{0,3},{1,0},{2,1},{3,2},{4,7},{5,4},{6,5},{7,6},{8,11},{9,8},{10,9... | collective-permute-start | bytes 786440 | tf_op jit(solution)/shard_map/ppermute | solution.py:31
  8.1 0.6 copy-done.2
  8.8 4.4 %outgoing_histories.1 = f32[16,288,128]{2,1,0:T(8,128)S(1)} custom-call(s32[1,32]{1,0:T(1,128)S(1)} %bitcast.10, bf16[9,32,4096]{2,1,0:T(8,128)(2,1)} %bitcast.16, bf16[9,32,4096]{2,1,0:T(8,128)(2,1)} %bitcast.18), custom_call_target="tpu_custom_call" | custom-call | bytes 8388608 | tf_op jit(solution)/shard_map/outgoing_histories/pallas_call | solution.py:526
  13.2 1.2 %convert_element_type.6 = f16[16,288,128]{2,1,0:T(8,128)(2,1)} convert(f32[16,288,128]{2,1,0:T(8,128)S(1)} %outgoing_histories.1) | non-fusion elementwise | flops 589824 | bytes 3538944 | tf_op jit(solution)/shard_map/convert_element_type | solution.py:540
  14.4 0.4 collective-permute-done.below_ref
  14.9 4.2 %collective-permute-done.1.above_ref = bf16[32,4096]{1,0:T(8,128)(2,1)S(1)} collective-permute-done((bf16[32,4096]{1,0:T(8,128)(2,1)}, bf16[32,4096]{1,0:T(8,128)(2,1)S(1)}, u32[]{:S(2)}, u32[]{:S(2)}) %collective-permute-start.1) | collective-permute-done | bytes 262176 | tf_op jit(solution)/shard_map/ppermute | solution.py:31
  19.1 2.2 %filtered_sensor.1 = (f32[32,4096]{1,0:T(8,128)}, f32[1,128]{1,0:T(1,128)S(1)}) custom-call(s32[2,16]{1,0:T(2,128)S(1)} %copy-done.4, f32[32,96]{1,0:T(8,128)S(1)} %copy-done.1, f32[32,4096]{1,0:T(8,128)S(1)} %copy-done, bf16[32,4096]{1,0:T(8,128)(2,1)S(1)} %collective-permute-done.below_ref, bf16[32,4096]{1,0:T(8,128)(2,1)S(1)} %collective-permute-done.1.above_ref, ...), custom_call_target="tpu_custom_call" | custom-call | bytes 4194304 | tf_op jit(solution)/shard_map/filtered_sensor/pallas_call | solution.py:563
  21.2 1.1 %collective-permute-start.2 = (f32[1,128]{1,0:T(1,128)S(1)}, f32[1,128]{1,0:T(1,128)S(1)}, u32[]{:S(2)}, u32[]{:S(2)}) collective-permute-start(f32[1,128]{1,0:T(1,128)S(1)} %get-tuple-element.13), channel_id=1, source_target_pairs={{0,1},{1,2},{2,3},{3,0},{4,5},{5,6},{6,7},{7,4},{8,9},{9,10},{10,1... | collective-permute-start | bytes 1544 | tf_op jit(solution)/shard_map/ppermute | solution.py:31
  22.4 1.8 %collective-permute-start.3 = (f32[1,128]{1,0:T(1,128)S(1)}, f32[1,128]{1,0:T(1,128)S(1)}, u32[]{:S(2)}, u32[]{:S(2)}) collective-permute-start(f32[1,128]{1,0:T(1,128)S(1)} %get-tuple-element.13), channel_id=1, source_target_pairs={{0,2},{1,3},{2,0},{3,1},{4,6},{5,7},{6,4},{7,5},{8,10},{9,11},{10,... | collective-permute-start | bytes 1544 | tf_op jit(solution)/shard_map/ppermute | solution.py:31
  24.1 1.3 %collective-permute-start.4 = (f32[1,128]{1,0:T(1,128)S(1)}, f32[1,128]{1,0:T(1,128)S(1)}, u32[]{:S(2)}, u32[]{:S(2)}) collective-permute-start(f32[1,128]{1,0:T(1,128)S(1)} %get-tuple-element.13), channel_id=1, source_target_pairs={{0,3},{1,0},{2,1},{3,2},{4,7},{5,4},{6,5},{7,6},{8,11},{9,8},{10,9... | collective-permute-start | bytes 1544 | tf_op jit(solution)/shard_map/ppermute | solution.py:31
  25.5 7.8 %base_and_rims.1 = (f32[9,32,4096]{2,1,0:T(8,128)}, bf16[9,32,2048]{2,1,0:T(8,128)(2,1)}) custom-call(s32[1]{0:T(128)S(6)} %copy.27.live_ref, s32[1,32]{1,0:T(1,128)} %bitcast.9, s32[1,32]{1,0:T(1,128)} %bitcast.12, f32[9,32,4096]{2,1,0:T(8,128)} %bitcast.14, bf16[9,32,4096]{2,1,0:T(8,128)(2,1)} %bitcast.17, bf16[9,32,4096]{2,1,0:T(8,128)(2,1)} %bitcast.19, ...), custom_call_target="tpu_custom_call" | custom-call | bytes 25165824 | tf_op jit(solution)/shard_map/base_and_rims/pallas_call | solution.py:544
  33.4 3.9 %all-to-all-start = ((f16[16,288,128]{2,1,0:T(8,128)(2,1)}), f16[16,288,128]{2,1,0:T(8,128)(2,1)S(1)}, u32[]{:S(2)}, u32[]{:S(2)}) async-start(f16[16,288,128]{2,1,0:T(8,128)(2,1)} %convert_element_type.6), calls=%async_computation | async-start | bytes 2359296 | tf_op jit(solution)/shard_map/all_to_all | solution.py:577
  37.5 1.6 %collective-permute-start.5 = (f32[4,128]{1,0:T(4,128)S(1)}, f32[4,128]{1,0:T(4,128)S(1)}, u32[]{:S(2)}, u32[]{:S(2)}) collective-permute-start(f32[4,128]{1,0:T(4,128)S(1)} %dynamic_update_slice.33), channel_id=1, source_target_pairs={{0,16},{16,0},{1,17},{17,1},{2,18},{18,2},{3,19},{19,3},{4,20},{20... | collective-permute-start | bytes 6152 | tf_op jit(solution)/shard_map/ppermute | solution.py:31
  39.0 2.1 %collective-permute-done.5 = f32[4,128]{1,0:T(4,128)S(1)} collective-permute-done((f32[4,128]{1,0:T(4,128)S(1)}, f32[4,128]{1,0:T(4,128)S(1)}, u32[]{:S(2)}, u32[]{:S(2)}) %collective-permute-start.5) | collective-permute-done | bytes 2080 | tf_op jit(solution)/shard_map/ppermute | solution.py:31
  41.1 1.8 %collective-permute-start.7 = (f32[4,256]{1,0:T(4,128)S(1)}, f32[4,256]{1,0:T(4,128)S(1)}, u32[]{:S(2)}, u32[]{:S(2)}) collective-permute-start(f32[4,256]{1,0:T(4,128)S(1)} %constant_dynamic-update-slice_fusion.4), channel_id=1, source_target_pairs={{0,8},{4,12},{8,0},{12,4},{1,9},{5,13},{9,1},{13,5},{2,10},{6,14},... | collective-permute-start | bytes 12296 | tf_op jit(solution)/shard_map/ppermute | solution.py:31
  42.9 1.4 %collective-permute-start.8 = (f32[4,256]{1,0:T(4,128)S(1)}, f32[4,256]{1,0:T(4,128)S(1)}, u32[]{:S(2)}, u32[]{:S(2)}) collective-permute-start(f32[4,256]{1,0:T(4,128)S(1)} %constant_dynamic-update-slice_fusion.4), channel_id=1, source_target_pairs={{0,12},{4,0},{8,4},{12,8},{1,13},{5,1},{9,5},{13,9},{2,14},{6,2},{... | collective-permute-start | bytes 12296 | tf_op jit(solution)/shard_map/ppermute | solution.py:31
  44.4 2.8 %collective-permute-done.6 = f32[4,256]{1,0:T(4,128)S(1)} collective-permute-done((f32[4,256]{1,0:T(4,128)S(1)}, f32[4,256]{1,0:T(4,128)S(1)}, u32[]{:S(2)}, u32[]{:S(2)}) %collective-permute-start.6) | collective-permute-done | bytes 4128 | tf_op jit(solution)/shard_map/ppermute | solution.py:31
  47.2 1.1 %collective-permute-done.7 = f32[4,256]{1,0:T(4,128)S(1)} collective-permute-done((f32[4,256]{1,0:T(4,128)S(1)}, f32[4,256]{1,0:T(4,128)S(1)}, u32[]{:S(2)}, u32[]{:S(2)}) %collective-permute-start.7) | collective-permute-done | bytes 4128 | tf_op jit(solution)/shard_map/ppermute | solution.py:31
  48.3 0.6 copy-done.6
  48.9 18.6 %updates.1 = (f32[9,32,4096]{2,1,0:T(8,128)}, bf16[9,32,4096]{2,1,0:T(8,128)(2,1)}) custom-call(s32[1]{0:T(128)S(6)} %copy.27.live_ref, f32[9,9]{1,0:T(8,128)} %rate_ref.1, f32[16,256]{1,0:T(8,128)} %copy-done.6, s32[1,32]{1,0:T(1,128)} %bitcast.23, f32[3,32]{1,0:T(4,128)} %velocity_ref.1, bf16[768,768]{1,0:T(8,128)(2,1)} %constant.96.clone.weights_hbm, ...), custom_call_target="tpu_custom_call" | custom-call | bytes 41943040 | tf_op jit(solution)/shard_map/updates/pallas_call | solution.py:584
  67.5 1.7 %convert_element_type.7.arrived_hbm = f32[16,288,128]{2,1,0:T(8,128)} convert(f16[16,288,128]{2,1,0:T(8,128)(2,1)S(1)} %all-to-all-done) | non-fusion elementwise | flops 589824 | bytes 3538944 | tf_op jit(solution)/shard_map/convert_element_type | solution.py:579
  69.2 6.2 %arrived_histories.1 = f32[9,32,4096]{2,1,0:T(8,128)} custom-call(s32[1]{0:T(128)S(6)} %copy.27.live_ref, f32[16,256]{1,0:T(8,128)} %copy-done.6, f32[9,32,4096]{2,1,0:T(8,128)} %get-tuple-element.19.fields_hbm, f32[16,288,128]{2,1,0:T(8,128)} %convert_element_type.7.arrived_hbm), custom_call_target="tpu_custom_call" | custom-call | bytes 12582912 | tf_op jit(solution)/shard_map/arrived_histories/pallas_call | solution.py:620
  (31 shorter events, 0.3 us)
Async XLA Ops:
  2.4 12.4 %collective-permute-start = (bf16[32,4096]{1,0:T(8,128)(2,1)}, bf16[32,4096]{1,0:T(8,128)(2,1)S(1)}, u32[]{:S(2)}, u32[]{:S(2)}) collective-permute-start(bf16[32,4096]{1,0:T(8,128)(2,1)} %raw_sensor.1), channel_id=1, source_target_pairs={{0,1},{1,2},{2,3},{3,0},{4,5},{5,6},{6,7},{7,4},{8,9},{9,10},{10,1... | collective-permute-start | bytes 786440 | tf_op jit(solution)/shard_map/ppermute | solution.py:31
  5.4 13.6 %collective-permute-start.1 = (bf16[32,4096]{1,0:T(8,128)(2,1)}, bf16[32,4096]{1,0:T(8,128)(2,1)S(1)}, u32[]{:S(2)}, u32[]{:S(2)}) collective-permute-start(bf16[32,4096]{1,0:T(8,128)(2,1)} %raw_sensor.1), channel_id=1, source_target_pairs={{0,3},{1,0},{2,1},{3,2},{4,7},{5,4},{6,5},{7,6},{8,11},{9,8},{10,9... | collective-permute-start | bytes 786440 | tf_op jit(solution)/shard_map/ppermute | solution.py:31
  8.1 0.7 copy-start.2
  13.2 5.9 %copy-start = (f32[32,4096]{1,0:T(8,128)S(1)}, f32[32,4096]{1,0:T(8,128)}, u32[]{:S(2)}) copy-start(f32[32,4096]{1,0:T(8,128)} %sensor_ref.3) | copy-start | bytes 1572868
  13.2 5.9 %copy-start.1 = (f32[32,96]{1,0:T(8,128)S(1)}, f32[32,96]{1,0:T(8,128)}, u32[]{:S(2)}) copy-start(f32[32,96]{1,0:T(8,128)} %constant.95.clone.weights_ref) | copy-start | bytes 36868
  13.2 5.9 %copy-start.3 = (s32[32]{0:T(128)S(1)}, s32[32]{0:T(128)}, u32[]{:S(2)}) copy-start(s32[32]{0:T(128)} %param.20) | copy-start | bytes 388
  13.2 5.9 %copy-start.4 = (s32[2,16]{1,0:T(2,128)S(1)}, s32[2,16]{1,0:T(2,128)}, u32[]{:S(2)}) copy-start(s32[2,16]{1,0:T(2,128)} %flags_ref.3) | copy-start | bytes 388
  13.2 5.9 %copy-start.5 = (s32[32]{0:T(128)S(1)}, s32[32]{0:T(128)}, u32[]{:S(2)}) copy-start(s32[32]{0:T(128)} %param.21) | copy-start | bytes 388
  21.2 12.0 %collective-permute-start.2 = (f32[1,128]{1,0:T(1,128)S(1)}, f32[1,128]{1,0:T(1,128)S(1)}, u32[]{:S(2)}, u32[]{:S(2)}) collective-permute-start(f32[1,128]{1,0:T(1,128)S(1)} %get-tuple-element.13), channel_id=1, source_target_pairs={{0,1},{1,2},{2,3},{3,0},{4,5},{5,6},{6,7},{7,4},{8,9},{9,10},{10,1... | collective-permute-start | bytes 1544 | tf_op jit(solution)/shard_map/ppermute | solution.py:31
  22.4 11.0 %collective-permute-start.3 = (f32[1,128]{1,0:T(1,128)S(1)}, f32[1,128]{1,0:T(1,128)S(1)}, u32[]{:S(2)}, u32[]{:S(2)}) collective-permute-start(f32[1,128]{1,0:T(1,128)S(1)} %get-tuple-element.13), channel_id=1, source_target_pairs={{0,2},{1,3},{2,0},{3,1},{4,6},{5,7},{6,4},{7,5},{8,10},{9,11},{10,... | collective-permute-start | bytes 1544 | tf_op jit(solution)/shard_map/ppermute | solution.py:31
  24.1 9.2 %collective-permute-start.4 = (f32[1,128]{1,0:T(1,128)S(1)}, f32[1,128]{1,0:T(1,128)S(1)}, u32[]{:S(2)}, u32[]{:S(2)}) collective-permute-start(f32[1,128]{1,0:T(1,128)S(1)} %get-tuple-element.13), channel_id=1, source_target_pairs={{0,3},{1,0},{2,1},{3,2},{4,7},{5,4},{6,5},{7,6},{8,11},{9,8},{10,9... | collective-permute-start | bytes 1544 | tf_op jit(solution)/shard_map/ppermute | solution.py:31
  33.4 34.1 %all-to-all-start = ((f16[16,288,128]{2,1,0:T(8,128)(2,1)}), f16[16,288,128]{2,1,0:T(8,128)(2,1)S(1)}, u32[]{:S(2)}, u32[]{:S(2)}) async-start(f16[16,288,128]{2,1,0:T(8,128)(2,1)} %convert_element_type.6), calls=%async_computation | async-start | bytes 2359296 | tf_op jit(solution)/shard_map/all_to_all | solution.py:577
  37.5 3.7 %collective-permute-start.5 = (f32[4,128]{1,0:T(4,128)S(1)}, f32[4,128]{1,0:T(4,128)S(1)}, u32[]{:S(2)}, u32[]{:S(2)}) collective-permute-start(f32[4,128]{1,0:T(4,128)S(1)} %dynamic_update_slice.33), channel_id=1, source_target_pairs={{0,16},{16,0},{1,17},{17,1},{2,18},{18,2},{3,19},{19,3},{4,20},{20... | collective-permute-start | bytes 6152 | tf_op jit(solution)/shard_map/ppermute | solution.py:31
  41.1 6.1 %collective-permute-start.6 = (f32[4,256]{1,0:T(4,128)S(1)}, f32[4,256]{1,0:T(4,128)S(1)}, u32[]{:S(2)}, u32[]{:S(2)}) collective-permute-start(f32[4,256]{1,0:T(4,128)S(1)} %constant_dynamic-update-slice_fusion.4), channel_id=1, source_target_pairs={{0,4},{4,8},{8,12},{12,0},{1,5},{5,9},{9,13},{13,1},{2,6},{6,10},{... | collective-permute-start | bytes 12296 | tf_op jit(solution)/shard_map/ppermute | solution.py:31
  41.1 7.2 %collective-permute-start.7 = (f32[4,256]{1,0:T(4,128)S(1)}, f32[4,256]{1,0:T(4,128)S(1)}, u32[]{:S(2)}, u32[]{:S(2)}) collective-permute-start(f32[4,256]{1,0:T(4,128)S(1)} %constant_dynamic-update-slice_fusion.4), channel_id=1, source_target_pairs={{0,8},{4,12},{8,0},{12,4},{1,9},{5,13},{9,1},{13,5},{2,10},{6,14},... | collective-permute-start | bytes 12296 | tf_op jit(solution)/shard_map/ppermute | solution.py:31
  42.9 5.4 %collective-permute-start.8 = (f32[4,256]{1,0:T(4,128)S(1)}, f32[4,256]{1,0:T(4,128)S(1)}, u32[]{:S(2)}, u32[]{:S(2)}) collective-permute-start(f32[4,256]{1,0:T(4,128)S(1)} %constant_dynamic-update-slice_fusion.4), channel_id=1, source_target_pairs={{0,12},{4,0},{8,4},{12,8},{1,13},{5,1},{9,5},{13,9},{2,14},{6,2},{... | collective-permute-start | bytes 12296 | tf_op jit(solution)/shard_map/ppermute | solution.py:31
  48.3 0.6 copy-start.6

commit v2 on v1

--- a/solution.py
+++ b/solution.py
@@ -133,66 +133,21 @@
             ]
 
 
-def prepare_kernel(
-    live_ref,
-    destination_ref,
-    target_ref,
-    fields_hbm,
-    recent_hbm,
-    older_hbm,
-    ghosts_hbm,
-    base_hbm,
-    rims_hbm,
-    fields_ref,
-    recent_ref,
-    older_ref,
-    ghosts_ref,
-    rims_ref,
-    got,
-    sent,
-):
-    species, slots, _ = fields_ref.shape
-
-    def fetches(s):
-        pairs = (
-            (fields_hbm, fields_ref),
-            (recent_hbm, recent_ref),
-            (older_hbm, older_ref),
-            (ghosts_hbm, ghosts_ref),
-        )
-        return [
-            pltpu.make_async_copy(here.at[s], there.at[s], got.at[n, s])
-            for n, (here, there) in enumerate(pairs)
-        ]
-
-    def stores(s):
-        return (
-            pltpu.make_async_copy(fields_ref.at[s], base_hbm.at[s], sent.at[0, s]),
-            pltpu.make_async_copy(rims_ref.at[s], rims_hbm.at[s], sent.at[1, s]),
-        )
-
-    for s in range(AHEAD):
-        for copy in fetches(s):
-            copy.start()
-    slot = lax.broadcasted_iota(jnp.int32, (slots, slots), 0)
-    keep = (destination_ref[...] == lax.axis_index(TEAM)) & (target_ref[...] == slot)
-    keep = keep.astype(jnp.bfloat16)
-    live = lax.broadcasted_iota(jnp.int32, (slots, 1), 0) < live_ref[0]
-    live = jnp.where(live, 1.0, 0.0)
+def rims_kernel(ghosts_hbm, rims_hbm, ghosts_ref, rims_ref, got, sent):
+    species, slots, _ = ghosts_ref.shape
+
+    def fetch(s):
+        return pltpu.make_async_copy(ghosts_hbm.at[s], ghosts_ref.at[s], got.at[s])
+
+    def store(s):
+        return pltpu.make_async_copy(rims_ref.at[s], rims_hbm.at[s], sent.at[s])
+
+    for s in range(species):
+        fetch(s).start()
     quarter = lax.broadcasted_iota(jnp.int32, (slots, LANES), 1) // (2 * TE)
 
     def one(s, carry):
-        @pl.when(s + AHEAD < species)
-        def _():
-            for copy in fetches(s + AHEAD):
-                copy.start()
-
-        for copy in fetches(s):
-            copy.wait()
-        recent = jnp.dot(keep, recent_ref[s], preferred_element_type=jnp.float32)
-        older = jnp.dot(keep, older_ref[s], preferred_element_type=jnp.float32)
-        kept = recent * (-16.0 / 12.0 * step_size) + older * (5.0 / 12.0 * step_size)
-        fields_ref[s] = (fields_ref[s] + kept) * live
+        fetch(s).wait()
         for block in range(2):
             faces = [
                 ghosts_ref[s, :, w * FACE + block * LANES : w * FACE + (block + 1) * LANES]
@@ -208,14 +163,62 @@
                 start = (block * 4 + q) * 2 * LANES
                 rims_ref[s, :, start : start + LANES] = high
                 rims_ref[s, :, start + LANES : start + 2 * LANES] = low
-        for copy in stores(s):
-            copy.start()
+        store(s).start()
         return carry
 
     lax.fori_loop(0, species, one, 0)
     for s in range(species):
-        for copy in stores(s):
+        store(s).wait()
+
+
+def base_kernel(
+    live_ref,
+    destination_ref,
+    target_ref,
+    fields_hbm,
+    recent_hbm,
+    older_hbm,
+    base_hbm,
+    fields_ref,
+    recent_ref,
+    older_ref,
+    got,
+    sent,
+):
+    species, slots, _ = fields_ref.shape
+
+    def fetches(s):
+        pairs = ((fields_hbm, fields_ref), (recent_hbm, recent_ref), (older_hbm, older_ref))
+        return [
+            pltpu.make_async_copy(here.at[s], there.at[s], got.at[n, s])
+            for n, (here, there) in enumerate(pairs)
+        ]
+
+    def store(s):
+        return pltpu.make_async_copy(fields_ref.at[s], base_hbm.at[s], sent.at[s])
+
+    for s in range(species):
+        for copy in fetches(s):
+            copy.start()
+    slot = lax.broadcasted_iota(jnp.int32, (slots, slots), 0)
+    keep = (destination_ref[...] == lax.axis_index(TEAM)) & (target_ref[...] == slot)
+    keep = keep.astype(jnp.bfloat16)
+    live = lax.broadcasted_iota(jnp.int32, (slots, 1), 0) < live_ref[0]
+    live = jnp.where(live, 1.0, 0.0)
+
+    def one(s, carry):
+        for copy in fetches(s):
             copy.wait()
+        recent = jnp.dot(keep, recent_ref[s], preferred_element_type=jnp.float32)
+        older = jnp.dot(keep, older_ref[s], preferred_element_type=jnp.float32)
+        kept = recent * (-16.0 / 12.0 * step_size) + older * (5.0 / 12.0 * step_size)
+        fields_ref[s] = (fields_ref[s] + kept) * live
+        store(s).start()
+        return carry
+
+    lax.fori_loop(0, species, one, 0)
+    for s in range(species):
+        store(s).wait()
 
 
 def plane_weights():
@@ -254,12 +257,16 @@
     rims_ref,
     base_ref,
     new_tend_ref,
-    rates_ref,
+    mix_ref,
     wide_ref,
     left_even_ref,
     left_odd_ref,
+    fuel_even_ref,
+    fuel_odd_ref,
     sums_even_ref,
     sums_odd_ref,
+    react_even_ref,
+    react_odd_ref,
     got,
     sent,
 ):
@@ -339,9 +346,28 @@
     parts += [0.5 * live * marks[:, d : d + 1] for d in range(3)]
     for n, part in enumerate(parts):
         wide_ref[n] = jnp.broadcast_to(part, (slots, LANES))
+    main = (species - 1) * slots
+    tail = lax.broadcasted_iota(jnp.int32, (slots, LANES), 1)
+    main_lane = lax.broadcasted_iota(jnp.int32, (slots, main), 1)
+    main_slot = lax.broadcasted_iota(jnp.int32, (slots, main), 0) == main_lane % slots
+    tail_slot = lax.broadcasted_iota(jnp.int32, (slots, LANES), 0) == tail % slots
     for s in range(species):
-        for k in range(species):
-            rates_ref[s * species + k] = jnp.full((8, LANES), rate_ref[s, k], jnp.float32)
+        rows = slice(s * slots, (s + 1) * slots)
+        rate = jnp.zeros((slots, main), jnp.float32)
+        for k in range(species - 1):
+            rate = jnp.where(main_lane // slots == k, rate_ref[s, k], rate)
+        rate = jnp.where(main_slot, rate, 0.0)
+        high = rate.astype(jnp.bfloat16)
+        mix_ref[rows, 0:main] = high
+        mix_ref[rows, main : 2 * main] = (rate - high.astype(jnp.float32)).astype(jnp.bfloat16)
+        mix_ref[rows, 2 * main : 3 * main] = high
+        rate = jnp.where(tail_slot & (tail < 3 * slots), rate_ref[s, species - 1], 0.0)
+        high = rate.astype(jnp.bfloat16).astype(jnp.float32)
+        rate = jnp.where(tail // slots == 1, rate - high, high)
+        mix_ref[rows, 3 * main :] = rate.astype(jnp.bfloat16)
+    for fuel_ref in (fuel_even_ref, fuel_odd_ref):
+        fuel_ref[3 * main + 3 * slots :, :] = jnp.zeros((LANES - 3 * slots, 2 * FACE), jnp.bfloat16)
+
     parity = lax.broadcasted_iota(jnp.int32, (slots, 2 * LANES), 1) // TE % 2
 
     def sums(pair, odd):
@@ -359,38 +385,42 @@
                 left_ref[rows, 2 * FACE :] = jnp.where(parity == p, both, jnp.zeros_like(both))
         sums_ref[...] = jnp.dot(left_ref[...], weights_ref[...], preferred_element_type=jnp.float32)
 
+        fuel_ref, react_ref = ((fuel_even_ref, react_even_ref), (fuel_odd_ref, react_odd_ref))[odd]
+        both = pl.ds(pl.multiple_of((2 * pair + 1) * FACE, FACE), 2 * FACE)
+        over = jnp.concatenate([wide_ref[1]] * 4, axis=1)
+        burning = fields_ref[0, :, both] * fields_ref[1, :, both] * over
+        for k in range(species):
+            fuel = fields_ref[k, :, both] * burning
+            high = fuel.astype(jnp.bfloat16)
+            low = (fuel - high.astype(jnp.float32)).astype(jnp.bfloat16)
+            for n, part in enumerate((high, high, low)):
+                start = n * main + k * slots if k < species - 1 else 3 * main + n * slots
+                fuel_ref[start : start + slots, :] = part
+        react_ref[...] = jnp.dot(mix_ref[...], fuel_ref[...], preferred_element_type=jnp.float32)
+
     def finish(pair, odd):
-        sums_ref = (sums_even_ref, sums_odd_ref)[odd]
+        sums_ref, react_ref = ((sums_even_ref, react_even_ref), (sums_odd_ref, react_odd_ref))[odd]
         for p in range(2):
             inner, before, here, after = (
                 pl.ds(pl.multiple_of((2 * pair + p + n) * FACE, FACE), FACE) for n in (0, 0, 1, 2)
             )
-            for g in range(slots // 8):
-                rows = slice(g * 8, (g + 1) * 8)
-                smooth, over, vx, vy, vz = (
-                    jnp.concatenate([wide_ref[n, rows, :]] * 2, axis=1) for n in range(5)
+            for g in range(slots // 16):
+                rows = slice(g * 16, (g + 1) * 16)
+                smooth, vx, vy, vz = (
+                    jnp.concatenate([wide_ref[n, rows, :]] * 2, axis=1) for n in (0, 2, 3, 4)
                 )
-                fuel = [fields_ref[s, rows, here] for s in range(species)]
-                burning = fuel[0] * fuel[1] * over
-                fuel = [f * burning for f in fuel]
                 for s in range(species):
-                    react = None
-                    for k in range(species):
-                        rate = rates_ref[s * species + k]
-                        term = jnp.concatenate([rate, rate], axis=1) * fuel[k]
-                        react = term if react is None else react + term
                     low, high = fields_ref[s, rows, before], fields_ref[s, rows, after]
-                    line = (p * species + s) * slots + g * 8
+                    line = s * slots + g * 16
+                    react = react_ref[line : line + 16, p * FACE : (p + 1) * FACE]
+                    line += p * species * slots
                     total, along_y, along_z = (
-                        sums_ref[line : line + 8, d * FACE : (d + 1) * FACE] for d in range(3)
+                        sums_ref[line : line + 16, d * FACE : (d + 1) * FACE] for d in range(3)
                     )
                     tend = smooth * (total + (low + high)) - vx * (high - low)
                     tend = (tend - vy * along_y) + (react - vz * along_z)
                     base_ref[s, rows, inner] += (step_size * 23.0 / 12.0) * tend
-                    sums_ref[line : line + 8, 0:FACE] = tend
-            for s in range(species):
-                line = (p * species + s) * slots
-                new_tend_ref[s, :, inner] = sums_ref[line : line + slots, 0:FACE].astype(jnp.bfloat16)
+                    new_tend_ref[s, rows, inner] = tend.astype(jnp.bfloat16)
 
     for copy in (*ends(), *cells_in(0)):
         copy.wait()
@@ -541,24 +571,38 @@
 
     shape = jax.ShapeDtypeStruct((species, slots, cells), jnp.float32)
     rims = jax.ShapeDtypeStruct((species, slots, TE * LANES), jnp.bfloat16)
-    base, rims = pl.pallas_call(
-        prepare_kernel,
-        name="base_and_rims",
-        out_shape=(shape, rims),
-        in_specs=[smem(), vmem, vmem] + [anywhere] * 4,
-        out_specs=(anywhere, anywhere),
+    base = pl.pallas_call(
+        base_kernel,
+        name="kept_histories",
+        out_shape=shape,
+        in_specs=[smem(), vmem, vmem] + [anywhere] * 3,
+        out_specs=anywhere,
         scratch_shapes=[
             pltpu.VMEM(shape.shape, jnp.float32),
             pltpu.VMEM(shape.shape, jnp.bfloat16),
             pltpu.VMEM(shape.shape, jnp.bfloat16),
+            pltpu.SemaphoreType.DMA((3, species)),
+            pltpu.SemaphoreType.DMA((species,)),
+        ],
+        compiler_params=params(58),
+        cost_estimate=pl.CostEstimate(flops=0, bytes_accessed=18 << 20, transcendentals=0),
+    )(live_counts, *moves, fields, recent, older)
+    rims = pl.pallas_call(
+        rims_kernel,
+        name="rims",
+        out_shape=rims,
+        in_specs=[anywhere],
+        out_specs=anywhere,
+        scratch_shapes=[
             pltpu.VMEM(ghosts.shape, jnp.float32),
             pltpu.VMEM(rims.shape, jnp.bfloat16),
-            pltpu.SemaphoreType.DMA((4, species)),
-            pltpu.SemaphoreType.DMA((2, species)),
+            pltpu.SemaphoreType.DMA((species,)),
+            pltpu.SemaphoreType.DMA((species,)),
         ],
         compiler_params=params(58),
-        cost_estimate=pl.CostEstimate(flops=0, bytes_accessed=24 << 20, transcendentals=0),
-    )(live_counts, *moves, fields, recent, older, ghosts)
+        cost_estimate=pl.CostEstimate(flops=0, bytes_accessed=8 << 20, transcendentals=0),
+    )(ghosts)
+    below, above, rims = lax.optimization_barrier((below, above, rims))
 
     filtered, row = pl.pallas_call(
         filter_kernel,
@@ -573,7 +617,7 @@
         cost_estimate=pl.CostEstimate(flops=0, bytes_accessed=4 << 20, transcendentals=0),
     )(flame_flags, jnp.asarray(banded(brick, brick)), sensor, below, above, *moves)
     rows = gathered(row, ("pen",))
-    rows, outgoing, base, rims = lax.optimization_barrier((rows, outgoing, base, rims))
+    rows, outgoing, base = lax.optimization_barrier((rows, outgoing, base))
     arrived = lax.all_to_all(outgoing, TEAM, split_axis=0, concat_axis=0, tiled=True)
     table = gathered(rows, ("grp", "mig"))
     arrived = arrived.astype(jnp.float32)
@@ -581,6 +625,9 @@
     weights = jnp.asarray(plane_weights(), jnp.bfloat16)
     left = pltpu.VMEM((2 * species * slots, 6 * LANES), jnp.bfloat16)
     sums = pltpu.VMEM((2 * species * slots, 3 * FACE), jnp.float32)
+    depth = 3 * (species - 1) * slots + LANES
+    fuel = pltpu.VMEM((depth, 2 * FACE), jnp.bfloat16)
+    react = pltpu.VMEM((species * slots, 2 * FACE), jnp.float32)
     new_fields, new_tend = pl.pallas_call(
         main_kernel,
         name="updates",
@@ -593,12 +640,16 @@
             pltpu.VMEM(rims.shape, jnp.bfloat16),
             pltpu.VMEM(shape.shape, jnp.float32),
             pltpu.VMEM(shape.shape, jnp.bfloat16),
-            pltpu.VMEM((species * species, 8, LANES), jnp.float32),
+            pltpu.VMEM((species * slots, depth), jnp.bfloat16),
             pltpu.VMEM((5, slots, LANES), jnp.float32),
             left,
             left,
+            fuel,
+            fuel,
             sums,
             sums,
+            react,
+            react,
             pltpu.SemaphoreType.DMA((4, TE // PLANES)),
             pltpu.SemaphoreType.DMA((2, TE // PLANES)),
         ],

time: 75.9 us -> 75.9 us (level)
  Pallas kernels: 40.9 us -> 44.1 us
  waiting for transfers between devices: 10.6 us -> 7.9 us
    ppermute x9, waiting for transfers between devices: 10.6 us -> 7.9 us  [passed_along(): return lax.ppermute(x, axis, [(i, (i + by) % peers) for i in range(peers)])]
    pallas_call x1 -> x2, Pallas kernels: 7.75 us -> 10.2 us  [the longest x1 6.87 us: local(): pl.pallas_call(base_kernel, name='kept_histories', out_shape=shape, in_sp...]
  transfers between devices with their start and end apart: 10 -> 10, of which waited for: 5 -> 4; matrix products, arithmetic and copies ran while one was open for 2% -> 2% of each run, Pallas kernels for 41% -> 45%
where the time goes in v2:
time: 75.9 us; the launch traced here: 75.4 us
  Pallas kernels  44.1 us (58%)
  starting transfers between devices  18 us (24%)
  waiting for transfers between devices  7.9 us (10%)
  other arithmetic  2.88 us (4%)
  between operations  1.69 us (2%)
  local copies, waits for them, and re-layouts  0.83 us (1%)
    pallas_call x1, Pallas kernels, local(): pl.pallas_call(main_kernel, name='updates', out_shape=(shape, jax.ShapeDt...  19.3 us
    ppermute x9, starting transfers between devices, passed_along(): return lax.ppermute(x, axis, [(i, (i + by) % peers) for i in range(peers)])  14.1 us
    ppermute x9, waiting for transfers between devices, passed_along(): return lax.ppermute(x, axis, [(i, (i + by) % peers) for i in range(peers)])  7.9 us
    pallas_call x1, Pallas kernels, local(): pl.pallas_call(base_kernel, name='kept_histories', out_shape=shape, in_sp...  6.87 us
    pallas_call x1, Pallas kernels, local(): pl.pallas_call(add_kernel, name='arrived_histories', out_shape=shape, in_...  6.23 us
    pallas_call x1, Pallas kernels, local(): pl.pallas_call(send_kernel, name='outgoing_histories', out_shape=jax.Shap...  4.37 us
    all_to_all x1, starting transfers between devices, local(): lax.all_to_all(outgoing, TEAM, split_axis=0, concat_axis=0, tiled=True)  3.89 us
    pallas_call x1, Pallas kernels, local(): pl.pallas_call(rims_kernel, name='rims', out_shape=rims, in_specs=[anywhe...  3.34 us
  transfers between devices with their start and end apart: 10, of which 4 were waited for; matrix products, arithmetic and copies ran while one was open for 2% of the time, Pallas kernels for 45%

profile of v2, /device:TPU:0, one launch (start us, length us, event | category | flops | bytes accessed | tf_op | source)
XLA Modules:
  0.0 75.4 jit_solution(15717619702428566860)
XLA Ops:
  0.6 1.8 %raw_sensor.1 = bf16[32,4096]{1,0:T(8,128)(2,1)} custom-call(s32[2,16]{1,0:T(2,128)} %flags_ref.3, f32[32,4096]{1,0:T(8,128)} %sensor_ref.3), custom_call_target="tpu_custom_call" | custom-call | tf_op jit(solution)/shard_map/raw_sensor/pallas_call | solution.py:542
  2.4 3.0 %collective-permute-start = (bf16[32,4096]{1,0:T(8,128)(2,1)}, bf16[32,4096]{1,0:T(8,128)(2,1)S(1)}, u32[]{:S(2)}, u32[]{:S(2)}) collective-permute-start(bf16[32,4096]{1,0:T(8,128)(2,1)} %raw_sensor.1), channel_id=1, source_target_pairs={{0,1},{1,2},{2,3},{3,0},{4,5},{5,6},{6,7},{7,4},{8,9},{9,10},{10,1... | collective-permute-start | bytes 786440 | tf_op jit(solution)/shard_map/ppermute | solution.py:31
  5.5 2.0 %collective-permute-start.1 = (bf16[32,4096]{1,0:T(8,128)(2,1)}, bf16[32,4096]{1,0:T(8,128)(2,1)S(1)}, u32[]{:S(2)}, u32[]{:S(2)}) collective-permute-start(bf16[32,4096]{1,0:T(8,128)(2,1)} %raw_sensor.1), channel_id=1, source_target_pairs={{0,3},{1,0},{2,1},{3,2},{4,7},{5,4},{6,5},{7,6},{8,11},{9,8},{10,9... | collective-permute-start | bytes 786440 | tf_op jit(solution)/shard_map/ppermute | solution.py:31
  7.5 3.3 %rims.1.rims_hbm = bf16[9,32,2048]{2,1,0:T(8,128)(2,1)} custom-call(f32[9,32,1536]{2,1,0:T(8,128)} %bitcast.20), custom_call_target="tpu_custom_call" | custom-call | bytes 8388608 | tf_op jit(solution)/shard_map/rims/pallas_call | solution.py:590
  11.5 4.4 %outgoing_histories.1 = f32[16,288,128]{2,1,0:T(8,128)S(1)} custom-call(s32[1,32]{1,0:T(1,128)S(1)} %bitcast.10, bf16[9,32,4096]{2,1,0:T(8,128)(2,1)} %bitcast.16, bf16[9,32,4096]{2,1,0:T(8,128)(2,1)} %bitcast.18), custom_call_target="tpu_custom_call" | custom-call | bytes 8388608 | tf_op jit(solution)/shard_map/outgoing_histories/pallas_call | solution.py:556
  15.9 0.0 copy-start.1
  15.9 1.2 %convert_element_type.6 = f16[16,288,128]{2,1,0:T(8,128)(2,1)} convert(f32[16,288,128]{2,1,0:T(8,128)S(1)} %outgoing_histories.1) | non-fusion elementwise | flops 589824 | bytes 3538944 | tf_op jit(solution)/shard_map/convert_element_type | solution.py:570
  17.1 1.9 %collective-permute-done.1.above_ref = bf16[32,4096]{1,0:T(8,128)(2,1)S(1)} collective-permute-done((bf16[32,4096]{1,0:T(8,128)(2,1)}, bf16[32,4096]{1,0:T(8,128)(2,1)S(1)}, u32[]{:S(2)}, u32[]{:S(2)}) %collective-permute-start.1) | collective-permute-done | bytes 262176 | tf_op jit(solution)/shard_map/ppermute | solution.py:31
  19.1 2.2 %filtered_sensor.1 = (f32[32,4096]{1,0:T(8,128)}, f32[1,128]{1,0:T(1,128)S(1)}) custom-call(s32[2,16]{1,0:T(2,128)S(1)} %copy-done.3, f32[32,96]{1,0:T(8,128)S(1)} %copy-done.1, f32[32,4096]{1,0:T(8,128)S(1)} %copy-done, bf16[32,4096]{1,0:T(8,128)(2,1)S(1)} %collective-permute-done.below_ref, bf16[32,4096]{1,0:T(8,128)(2,1)S(1)} %collective-permute-done.1.above_ref, ...), custom_call_target="tpu_custom_call" | custom-call | bytes 4194304 | tf_op jit(solution)/shard_map/filtered_sensor/pallas_call | solution.py:607
  21.2 1.1 %collective-permute-start.2 = (f32[1,128]{1,0:T(1,128)S(1)}, f32[1,128]{1,0:T(1,128)S(1)}, u32[]{:S(2)}, u32[]{:S(2)}) collective-permute-start(f32[1,128]{1,0:T(1,128)S(1)} %get-tuple-element.15), channel_id=1, source_target_pairs={{0,1},{1,2},{2,3},{3,0},{4,5},{5,6},{6,7},{7,4},{8,9},{9,10},{10,1... | collective-permute-start | bytes 1544 | tf_op jit(solution)/shard_map/ppermute | solution.py:31
  22.4 1.8 %collective-permute-start.3 = (f32[1,128]{1,0:T(1,128)S(1)}, f32[1,128]{1,0:T(1,128)S(1)}, u32[]{:S(2)}, u32[]{:S(2)}) collective-permute-start(f32[1,128]{1,0:T(1,128)S(1)} %get-tuple-element.15), channel_id=1, source_target_pairs={{0,2},{1,3},{2,0},{3,1},{4,6},{5,7},{6,4},{7,5},{8,10},{9,11},{10,... | collective-permute-start | bytes 1544 | tf_op jit(solution)/shard_map/ppermute | solution.py:31
  24.1 1.3 %collective-permute-start.4 = (f32[1,128]{1,0:T(1,128)S(1)}, f32[1,128]{1,0:T(1,128)S(1)}, u32[]{:S(2)}, u32[]{:S(2)}) collective-permute-start(f32[1,128]{1,0:T(1,128)S(1)} %get-tuple-element.15), channel_id=1, source_target_pairs={{0,3},{1,0},{2,1},{3,2},{4,7},{5,4},{6,5},{7,6},{8,11},{9,8},{10,9... | collective-permute-start | bytes 1544 | tf_op jit(solution)/shard_map/ppermute | solution.py:31
  25.5 6.9 %kept_histories.1.base_hbm = f32[9,32,4096]{2,1,0:T(8,128)} custom-call(s32[1]{0:T(128)S(6)} %copy.27.live_ref, s32[1,32]{1,0:T(1,128)} %bitcast.9, s32[1,32]{1,0:T(1,128)} %bitcast.12, f32[9,32,4096]{2,1,0:T(8,128)} %bitcast.14, bf16[9,32,4096]{2,1,0:T(8,128)(2,1)} %bitcast.17, bf16[9,32,4096]{2,1,0:T(8,128)(2,1)} %bitcast.19), custom_call_target="tpu_custom_call" | custom-call | bytes 18874368 | tf_op jit(solution)/shard_map/kept_histories/pallas_call | solution.py:574
  32.5 3.9 %all-to-all-start = ((f16[16,288,128]{2,1,0:T(8,128)(2,1)}), f16[16,288,128]{2,1,0:T(8,128)(2,1)S(1)}, u32[]{:S(2)}, u32[]{:S(2)}) async-start(f16[16,288,128]{2,1,0:T(8,128)(2,1)} %convert_element_type.6), calls=%async_computation | async-start | bytes 2359296 | tf_op jit(solution)/shard_map/all_to_all | solution.py:621
  36.5 1.6 %collective-permute-start.5 = (f32[4,128]{1,0:T(4,128)S(1)}, f32[4,128]{1,0:T(4,128)S(1)}, u32[]{:S(2)}, u32[]{:S(2)}) collective-permute-start(f32[4,128]{1,0:T(4,128)S(1)} %dynamic_update_slice.33), channel_id=1, source_target_pairs={{0,16},{16,0},{1,17},{17,1},{2,18},{18,2},{3,19},{19,3},{4,20},{20... | collective-permute-start | bytes 6152 | tf_op jit(solution)/shard_map/ppermute | solution.py:31
  38.2 2.0 %collective-permute-done.5 = f32[4,128]{1,0:T(4,128)S(1)} collective-permute-done((f32[4,128]{1,0:T(4,128)S(1)}, f32[4,128]{1,0:T(4,128)S(1)}, u32[]{:S(2)}, u32[]{:S(2)}) %collective-permute-start.5) | collective-permute-done | bytes 2080 | tf_op jit(solution)/shard_map/ppermute | solution.py:31
  40.2 1.8 %collective-permute-start.7 = (f32[4,256]{1,0:T(4,128)S(1)}, f32[4,256]{1,0:T(4,128)S(1)}, u32[]{:S(2)}, u32[]{:S(2)}) collective-permute-start(f32[4,256]{1,0:T(4,128)S(1)} %constant_dynamic-update-slice_fusion.4), channel_id=1, source_target_pairs={{0,8},{4,12},{8,0},{12,4},{1,9},{5,13},{9,1},{13,5},{2,10},{6,14},... | collective-permute-start | bytes 12296 | tf_op jit(solution)/shard_map/ppermute | solution.py:31
  42.0 1.4 %collective-permute-start.8 = (f32[4,256]{1,0:T(4,128)S(1)}, f32[4,256]{1,0:T(4,128)S(1)}, u32[]{:S(2)}, u32[]{:S(2)}) collective-permute-start(f32[4,256]{1,0:T(4,128)S(1)} %constant_dynamic-update-slice_fusion.4), channel_id=1, source_target_pairs={{0,12},{4,0},{8,4},{12,8},{1,13},{5,1},{9,5},{13,9},{2,14},{6,2},{... | collective-permute-start | bytes 12296 | tf_op jit(solution)/shard_map/ppermute | solution.py:31
  43.4 2.8 %collective-permute-done.6 = f32[4,256]{1,0:T(4,128)S(1)} collective-permute-done((f32[4,256]{1,0:T(4,128)S(1)}, f32[4,256]{1,0:T(4,128)S(1)}, u32[]{:S(2)}, u32[]{:S(2)}) %collective-permute-start.6) | collective-permute-done | bytes 4128 | tf_op jit(solution)/shard_map/ppermute | solution.py:31
  46.3 1.1 %collective-permute-done.7 = f32[4,256]{1,0:T(4,128)S(1)} collective-permute-done((f32[4,256]{1,0:T(4,128)S(1)}, f32[4,256]{1,0:T(4,128)S(1)}, u32[]{:S(2)}, u32[]{:S(2)}) %collective-permute-start.7) | collective-permute-done | bytes 4128 | tf_op jit(solution)/shard_map/ppermute | solution.py:31
  47.4 0.6 copy-done.5
  48.0 19.3 %updates.1 = (f32[9,32,4096]{2,1,0:T(8,128)}, bf16[9,32,4096]{2,1,0:T(8,128)(2,1)}) custom-call(s32[1]{0:T(128)S(6)} %copy.27.live_ref, f32[9,9]{1,0:T(8,128)} %rate_ref.1, f32[16,256]{1,0:T(8,128)} %copy-done.5, s32[1,32]{1,0:T(1,128)} %bitcast.23, f32[3,32]{1,0:T(4,128)} %velocity_ref.1, bf16[768,768]{1,0:T(8,128)(2,1)} %constant.96.clone.weights_hbm, ...), custom_call_target="tpu_custom_call" | custom-call | bytes 41943040 | tf_op jit(solution)/shard_map/updates/pallas_call | solution.py:631
  67.3 1.7 %convert_element_type.7.arrived_hbm = f32[16,288,128]{2,1,0:T(8,128)} convert(f16[16,288,128]{2,1,0:T(8,128)(2,1)S(1)} %all-to-all-done) | non-fusion elementwise | flops 589824 | bytes 3538944 | tf_op jit(solution)/shard_map/convert_element_type | solution.py:623
  69.0 6.2 %arrived_histories.1 = f32[9,32,4096]{2,1,0:T(8,128)} custom-call(s32[1]{0:T(128)S(6)} %copy.27.live_ref, f32[16,256]{1,0:T(8,128)} %copy-done.5, f32[9,32,4096]{2,1,0:T(8,128)} %get-tuple-element.19.fields_hbm, f32[16,288,128]{2,1,0:T(8,128)} %convert_element_type.7.arrived_hbm), custom_call_target="tpu_custom_call" | custom-call | bytes 12582912 | tf_op jit(solution)/shard_map/arrived_histories/pallas_call | solution.py:671
  (30 shorter events, 0.2 us)
Async XLA Ops:
  0.6 10.9 %copy-start.2 = (s32[32]{0:T(128)S(1)}, s32[32]{0:T(128)}, u32[]{:S(2)}) copy-start(s32[32]{0:T(128)} %param.20) | copy-start | bytes 388
  2.4 14.7 %collective-permute-start = (bf16[32,4096]{1,0:T(8,128)(2,1)}, bf16[32,4096]{1,0:T(8,128)(2,1)S(1)}, u32[]{:S(2)}, u32[]{:S(2)}) collective-permute-start(bf16[32,4096]{1,0:T(8,128)(2,1)} %raw_sensor.1), channel_id=1, source_target_pairs={{0,1},{1,2},{2,3},{3,0},{4,5},{5,6},{6,7},{7,4},{8,9},{9,10},{10,1... | collective-permute-start | bytes 786440 | tf_op jit(solution)/shard_map/ppermute | solution.py:31
  5.5 13.6 %collective-permute-start.1 = (bf16[32,4096]{1,0:T(8,128)(2,1)}, bf16[32,4096]{1,0:T(8,128)(2,1)S(1)}, u32[]{:S(2)}, u32[]{:S(2)}) collective-permute-start(bf16[32,4096]{1,0:T(8,128)(2,1)} %raw_sensor.1), channel_id=1, source_target_pairs={{0,3},{1,0},{2,1},{3,2},{4,7},{5,4},{6,5},{7,6},{8,11},{9,8},{10,9... | collective-permute-start | bytes 786440 | tf_op jit(solution)/shard_map/ppermute | solution.py:31
  15.9 3.2 %copy-start = (f32[32,4096]{1,0:T(8,128)S(1)}, f32[32,4096]{1,0:T(8,128)}, u32[]{:S(2)}) copy-start(f32[32,4096]{1,0:T(8,128)} %sensor_ref.3) | copy-start | bytes 1572868
  15.9 3.2 %copy-start.1 = (f32[32,96]{1,0:T(8,128)S(1)}, f32[32,96]{1,0:T(8,128)}, u32[]{:S(2)}) copy-start(f32[32,96]{1,0:T(8,128)} %constant.95.clone.weights_ref) | copy-start | bytes 36868
  15.9 3.2 %copy-start.3 = (s32[2,16]{1,0:T(2,128)S(1)}, s32[2,16]{1,0:T(2,128)}, u32[]{:S(2)}) copy-start(s32[2,16]{1,0:T(2,128)} %flags_ref.3) | copy-start | bytes 388
  15.9 3.2 %copy-start.4 = (s32[32]{0:T(128)S(1)}, s32[32]{0:T(128)}, u32[]{:S(2)}) copy-start(s32[32]{0:T(128)} %param.21) | copy-start | bytes 388
  21.2 11.2 %collective-permute-start.2 = (f32[1,128]{1,0:T(1,128)S(1)}, f32[1,128]{1,0:T(1,128)S(1)}, u32[]{:S(2)}, u32[]{:S(2)}) collective-permute-start(f32[1,128]{1,0:T(1,128)S(1)} %get-tuple-element.15), channel_id=1, source_target_pairs={{0,1},{1,2},{2,3},{3,0},{4,5},{5,6},{6,7},{7,4},{8,9},{9,10},{10,1... | collective-permute-start | bytes 1544 | tf_op jit(solution)/shard_map/ppermute | solution.py:31
  22.4 10.1 %collective-permute-start.3 = (f32[1,128]{1,0:T(1,128)S(1)}, f32[1,128]{1,0:T(1,128)S(1)}, u32[]{:S(2)}, u32[]{:S(2)}) collective-permute-start(f32[1,128]{1,0:T(1,128)S(1)} %get-tuple-element.15), channel_id=1, source_target_pairs={{0,2},{1,3},{2,0},{3,1},{4,6},{5,7},{6,4},{7,5},{8,10},{9,11},{10,... | collective-permute-start | bytes 1544 | tf_op jit(solution)/shard_map/ppermute | solution.py:31
  24.1 8.4 %collective-permute-start.4 = (f32[1,128]{1,0:T(1,128)S(1)}, f32[1,128]{1,0:T(1,128)S(1)}, u32[]{:S(2)}, u32[]{:S(2)}) collective-permute-start(f32[1,128]{1,0:T(1,128)S(1)} %get-tuple-element.15), channel_id=1, source_target_pairs={{0,3},{1,0},{2,1},{3,2},{4,7},{5,4},{6,5},{7,6},{8,11},{9,8},{10,9... | collective-permute-start | bytes 1544 | tf_op jit(solution)/shard_map/ppermute | solution.py:31
  32.5 34.8 %all-to-all-start = ((f16[16,288,128]{2,1,0:T(8,128)(2,1)}), f16[16,288,128]{2,1,0:T(8,128)(2,1)S(1)}, u32[]{:S(2)}, u32[]{:S(2)}) async-start(f16[16,288,128]{2,1,0:T(8,128)(2,1)} %convert_element_type.6), calls=%async_computation | async-start | bytes 2359296 | tf_op jit(solution)/shard_map/all_to_all | solution.py:621
  36.5 3.7 %collective-permute-start.5 = (f32[4,128]{1,0:T(4,128)S(1)}, f32[4,128]{1,0:T(4,128)S(1)}, u32[]{:S(2)}, u32[]{:S(2)}) collective-permute-start(f32[4,128]{1,0:T(4,128)S(1)} %dynamic_update_slice.33), channel_id=1, source_target_pairs={{0,16},{16,0},{1,17},{17,1},{2,18},{18,2},{3,19},{19,3},{4,20},{20... | collective-permute-start | bytes 6152 | tf_op jit(solution)/shard_map/ppermute | solution.py:31
  40.2 6.1 %collective-permute-start.6 = (f32[4,256]{1,0:T(4,128)S(1)}, f32[4,256]{1,0:T(4,128)S(1)}, u32[]{:S(2)}, u32[]{:S(2)}) collective-permute-start(f32[4,256]{1,0:T(4,128)S(1)} %constant_dynamic-update-slice_fusion.4), channel_id=1, source_target_pairs={{0,4},{4,8},{8,12},{12,0},{1,5},{5,9},{9,13},{13,1},{2,6},{6,10},{... | collective-permute-start | bytes 12296 | tf_op jit(solution)/shard_map/ppermute | solution.py:31
  40.2 7.2 %collective-permute-start.7 = (f32[4,256]{1,0:T(4,128)S(1)}, f32[4,256]{1,0:T(4,128)S(1)}, u32[]{:S(2)}, u32[]{:S(2)}) collective-permute-start(f32[4,256]{1,0:T(4,128)S(1)} %constant_dynamic-update-slice_fusion.4), channel_id=1, source_target_pairs={{0,8},{4,12},{8,0},{12,4},{1,9},{5,13},{9,1},{13,5},{2,10},{6,14},... | collective-permute-start | bytes 12296 | tf_op jit(solution)/shard_map/ppermute | solution.py:31
  42.0 5.4 %collective-permute-start.8 = (f32[4,256]{1,0:T(4,128)S(1)}, f32[4,256]{1,0:T(4,128)S(1)}, u32[]{:S(2)}, u32[]{:S(2)}) collective-permute-start(f32[4,256]{1,0:T(4,128)S(1)} %constant_dynamic-update-slice_fusion.4), channel_id=1, source_target_pairs={{0,12},{4,0},{8,4},{12,8},{1,13},{5,1},{9,5},{13,9},{2,14},{6,2},{... | collective-permute-start | bytes 12296 | tf_op jit(solution)/shard_map/ppermute | solution.py:31
  47.4 0.6 copy-start.5

commit v3 on v2

--- a/solution.py
+++ b/solution.py
@@ -259,12 +259,8 @@
     new_tend_ref,
     mix_ref,
     wide_ref,
-    left_even_ref,
-    left_odd_ref,
     fuel_even_ref,
     fuel_odd_ref,
-    sums_even_ref,
-    sums_odd_ref,
     react_even_ref,
     react_odd_ref,
     got,
@@ -370,21 +366,7 @@
 
     parity = lax.broadcasted_iota(jnp.int32, (slots, 2 * LANES), 1) // TE % 2
 
-    def sums(pair, odd):
-        left_ref, sums_ref = ((left_even_ref, sums_even_ref), (left_odd_ref, sums_odd_ref))[odd]
-        rims = pl.ds(pl.multiple_of(pair * FACE, FACE), FACE)
-        for s in range(species):
-            both = rims_ref[s, :, rims]
-            for p in range(2):
-                lanes = pl.ds(pl.multiple_of((2 * pair + p + 1) * FACE, FACE), FACE)
-                rows = slice((p * species + s) * slots, (p * species + s + 1) * slots)
-                f = fields_ref[s, :, lanes]
-                high = f.astype(jnp.bfloat16)
-                left_ref[rows, 0:FACE] = high
-                left_ref[rows, FACE : 2 * FACE] = (f - high.astype(jnp.float32)).astype(jnp.bfloat16)
-                left_ref[rows, 2 * FACE :] = jnp.where(parity == p, both, jnp.zeros_like(both))
-        sums_ref[...] = jnp.dot(left_ref[...], weights_ref[...], preferred_element_type=jnp.float32)
-
+    def burn(pair, odd):
         fuel_ref, react_ref = ((fuel_even_ref, react_even_ref), (fuel_odd_ref, react_odd_ref))[odd]
         both = pl.ds(pl.multiple_of((2 * pair + 1) * FACE, FACE), 2 * FACE)
         over = jnp.concatenate([wide_ref[1]] * 4, axis=1)
@@ -399,32 +381,42 @@
         react_ref[...] = jnp.dot(mix_ref[...], fuel_ref[...], preferred_element_type=jnp.float32)
 
     def finish(pair, odd):
-        sums_ref, react_ref = ((sums_even_ref, react_even_ref), (sums_odd_ref, react_odd_ref))[odd]
-        for p in range(2):
-            inner, before, here, after = (
-                pl.ds(pl.multiple_of((2 * pair + p + n) * FACE, FACE), FACE) for n in (0, 0, 1, 2)
+        react_ref = (react_even_ref, react_odd_ref)[odd]
+        rims = pl.ds(pl.multiple_of(pair * FACE, FACE), FACE)
+        planes = [pl.ds(pl.multiple_of((2 * pair + n) * FACE, FACE), FACE) for n in range(4)]
+        for s in range(species):
+            both = rims_ref[s, :, rims]
+            none = jnp.zeros_like(both)
+            rim = jnp.concatenate([jnp.where(parity == p, both, none) for p in range(2)], axis=0)
+            f = jnp.concatenate([fields_ref[s, :, planes[1 + p]] for p in range(2)], axis=0)
+            high = f.astype(jnp.bfloat16)
+            low = (f - high.astype(jnp.float32)).astype(jnp.bfloat16)
+            sums = jnp.dot(
+                jnp.concatenate([high, low, rim], axis=1),
+                weights_ref[...],
+                preferred_element_type=jnp.float32,
             )
-            for g in range(slots // 16):
-                rows = slice(g * 16, (g + 1) * 16)
-                smooth, vx, vy, vz = (
-                    jnp.concatenate([wide_ref[n, rows, :]] * 2, axis=1) for n in (0, 2, 3, 4)
-                )
-                for s in range(species):
-                    low, high = fields_ref[s, rows, before], fields_ref[s, rows, after]
+            for p in range(2):
+                for g in range(slots // 16):
+                    rows = slice(g * 16, (g + 1) * 16)
+                    smooth, vx, vy, vz = (
+                        jnp.concatenate([wide_ref[n, rows, :]] * 2, axis=1) for n in (0, 2, 3, 4)
+                    )
+                    before, after = (fields_ref[s, rows, planes[p + n]] for n in (0, 2))
+                    line = p * slots + g * 16
+                    total, along_y, along_z = (
+                        sums[line : line + 16, d * FACE : (d + 1) * FACE] for d in range(3)
+                    )
                     line = s * slots + g * 16
                     react = react_ref[line : line + 16, p * FACE : (p + 1) * FACE]
-                    line += p * species * slots
-                    total, along_y, along_z = (
-                        sums_ref[line : line + 16, d * FACE : (d + 1) * FACE] for d in range(3)
-                    )
-                    tend = smooth * (total + (low + high)) - vx * (high - low)
+                    tend = smooth * (total + (before + after)) - vx * (after - before)
                     tend = (tend - vy * along_y) + (react - vz * along_z)
-                    base_ref[s, rows, inner] += (step_size * 23.0 / 12.0) * tend
-                    new_tend_ref[s, rows, inner] = tend.astype(jnp.bfloat16)
+                    base_ref[s, rows, planes[p]] += (step_size * 23.0 / 12.0) * tend
+                    new_tend_ref[s, rows, planes[p]] = tend.astype(jnp.bfloat16)
 
     for copy in (*ends(), *cells_in(0)):
         copy.wait()
-    sums(0, 0)
+    burn(0, 0)
 
     def four(c, carry):
         @pl.when(c + 2 < chunks)
@@ -433,7 +425,7 @@
                 copy.start()
 
         bases(c).wait()
-        sums(2 * c + 1, 1)
+        burn(2 * c + 1, 1)
         finish(2 * c, 0)
 
         @pl.when(c + 1 < chunks)
@@ -441,7 +433,7 @@
             for copy in cells_in(c + 1):
                 copy.wait()
 
-        sums(jnp.minimum(2 * c + 2, 2 * (chunks - 1)), 0)
+        burn(jnp.minimum(2 * c + 2, 2 * (chunks - 1)), 0)
         finish(2 * c + 1, 1)
         for copy in stores(c):
             copy.start()
@@ -571,22 +563,6 @@
 
     shape = jax.ShapeDtypeStruct((species, slots, cells), jnp.float32)
     rims = jax.ShapeDtypeStruct((species, slots, TE * LANES), jnp.bfloat16)
-    base = pl.pallas_call(
-        base_kernel,
-        name="kept_histories",
-        out_shape=shape,
-        in_specs=[smem(), vmem, vmem] + [anywhere] * 3,
-        out_specs=anywhere,
-        scratch_shapes=[
-            pltpu.VMEM(shape.shape, jnp.float32),
-            pltpu.VMEM(shape.shape, jnp.bfloat16),
-            pltpu.VMEM(shape.shape, jnp.bfloat16),
-            pltpu.SemaphoreType.DMA((3, species)),
-            pltpu.SemaphoreType.DMA((species,)),
-        ],
-        compiler_params=params(58),
-        cost_estimate=pl.CostEstimate(flops=0, bytes_accessed=18 << 20, transcendentals=0),
-    )(live_counts, *moves, fields, recent, older)
     rims = pl.pallas_call(
         rims_kernel,
         name="rims",
@@ -617,14 +593,28 @@
         cost_estimate=pl.CostEstimate(flops=0, bytes_accessed=4 << 20, transcendentals=0),
     )(flame_flags, jnp.asarray(banded(brick, brick)), sensor, below, above, *moves)
     rows = gathered(row, ("pen",))
-    rows, outgoing, base = lax.optimization_barrier((rows, outgoing, base))
+    rows, outgoing, live = lax.optimization_barrier((rows, outgoing, live_counts))
     arrived = lax.all_to_all(outgoing, TEAM, split_axis=0, concat_axis=0, tiled=True)
     table = gathered(rows, ("grp", "mig"))
     arrived = arrived.astype(jnp.float32)
+    base = pl.pallas_call(
+        base_kernel,
+        name="kept_histories",
+        out_shape=shape,
+        in_specs=[smem(), vmem, vmem] + [anywhere] * 3,
+        out_specs=anywhere,
+        scratch_shapes=[
+            pltpu.VMEM(shape.shape, jnp.float32),
+            pltpu.VMEM(shape.shape, jnp.bfloat16),
+            pltpu.VMEM(shape.shape, jnp.bfloat16),
+            pltpu.SemaphoreType.DMA((3, species)),
+            pltpu.SemaphoreType.DMA((species,)),
+        ],
+        compiler_params=params(58),
+        cost_estimate=pl.CostEstimate(flops=0, bytes_accessed=18 << 20, transcendentals=0),
+    )(live, *moves, fields, recent, older)
 
     weights = jnp.asarray(plane_weights(), jnp.bfloat16)
-    left = pltpu.VMEM((2 * species * slots, 6 * LANES), jnp.bfloat16)
-    sums = pltpu.VMEM((2 * species * slots, 3 * FACE), jnp.float32)
     depth = 3 * (species - 1) * slots + LANES
     fuel = pltpu.VMEM((depth, 2 * FACE), jnp.bfloat16)
     react = pltpu.VMEM((species * slots, 2 * FACE), jnp.float32)
@@ -642,12 +632,8 @@
             pltpu.VMEM(shape.shape, jnp.bfloat16),
             pltpu.VMEM((species * slots, depth), jnp.bfloat16),
             pltpu.VMEM((5, slots, LANES), jnp.float32),
-            left,
-            left,
             fuel,
             fuel,
-            sums,
-            sums,
             react,
             react,
             pltpu.SemaphoreType.DMA((4, TE // PLANES)),

time: 75.9 us -> 84 us (1.11)
  Pallas kernels: 44.1 us -> 49.2 us
  starting transfers between devices: 18 us -> 19.6 us
  waiting for transfers between devices: 7.9 us -> 9.17 us
    pallas_call x1, Pallas kernels: 19.3 us -> 24.4 us  [local(): pl.pallas_call(main_kernel, name='updates', out_shape=(shape, jax.ShapeDt...]
    all_to_all x1, starting transfers between devices: 3.89 us -> 5.46 us  [local(): lax.all_to_all(outgoing, TEAM, split_axis=0, concat_axis=0, tiled=True)]
    ppermute x9, waiting for transfers between devices: 7.9 us -> 9.17 us  [passed_along(): return lax.ppermute(x, axis, [(i, (i + by) % peers) for i in range(peers)])]
  transfers between devices with their start and end apart: 10 -> 10, of which waited for: 4 -> 6; matrix products, arithmetic and copies ran while one was open for 2% -> 2% of each run, Pallas kernels for 45% -> 47%
where the time goes in v3:
time: 84 us; the launch traced here: 83.3 us
  Pallas kernels  49.2 us (59%)
  starting transfers between devices  19.6 us (23%)
  waiting for transfers between devices  9.17 us (11%)
  other arithmetic  2.88 us (3%)
  between operations  1.69 us (2%)
    pallas_call x1, Pallas kernels, local(): pl.pallas_call(main_kernel, name='updates', out_shape=(shape, jax.ShapeDt...  24.4 us
    ppermute x9, starting transfers between devices, passed_along(): return lax.ppermute(x, axis, [(i, (i + by) % peers) for i in range(peers)])  14.1 us
    ppermute x9, waiting for transfers between devices, passed_along(): return lax.ppermute(x, axis, [(i, (i + by) % peers) for i in range(peers)])  9.17 us
    pallas_call x1, Pallas kernels, local(): pl.pallas_call(base_kernel, name='kept_histories', out_shape=shape, in_sp...  6.88 us
    pallas_call x1, Pallas kernels, local(): pl.pallas_call(add_kernel, name='arrived_histories', out_shape=shape, in_...  6.23 us
    all_to_all x1, starting transfers between devices, local(): lax.all_to_all(outgoing, TEAM, split_axis=0, concat_axis=0, tiled=True)  5.46 us
    pallas_call x1, Pallas kernels, local(): pl.pallas_call(send_kernel, name='outgoing_histories', out_shape=jax.Shap...  4.42 us
    pallas_call x1, Pallas kernels, local(): pl.pallas_call(rims_kernel, name='rims', out_shape=rims, in_specs=[anywhe...  3.34 us
  transfers between devices with their start and end apart: 10, of which 6 were waited for; matrix products, arithmetic and copies ran while one was open for 2% of the time, Pallas kernels for 47%

profile of v3, /device:TPU:0, one launch (start us, length us, event | category | flops | bytes accessed | tf_op | source)
XLA Modules:
  0.0 83.3 jit_solution(1528880377536636310)
XLA Ops:
  0.6 1.8 %raw_sensor.1 = bf16[32,4096]{1,0:T(8,128)(2,1)} custom-call(s32[2,16]{1,0:T(2,128)} %flags_ref.3, f32[32,4096]{1,0:T(8,128)} %sensor_ref.3), custom_call_target="tpu_custom_call" | custom-call | tf_op jit(solution)/shard_map/raw_sensor/pallas_call | solution.py:534
  2.4 3.0 %collective-permute-start = (bf16[32,4096]{1,0:T(8,128)(2,1)}, bf16[32,4096]{1,0:T(8,128)(2,1)S(1)}, u32[]{:S(2)}, u32[]{:S(2)}) collective-permute-start(bf16[32,4096]{1,0:T(8,128)(2,1)} %raw_sensor.1), channel_id=1, source_target_pairs={{0,1},{1,2},{2,3},{3,0},{4,5},{5,6},{6,7},{7,4},{8,9},{9,10},{10,1... | collective-permute-start | bytes 786440 | tf_op jit(solution)/shard_map/ppermute | solution.py:31
  5.5 2.0 %collective-permute-start.1 = (bf16[32,4096]{1,0:T(8,128)(2,1)}, bf16[32,4096]{1,0:T(8,128)(2,1)S(1)}, u32[]{:S(2)}, u32[]{:S(2)}) collective-permute-start(bf16[32,4096]{1,0:T(8,128)(2,1)} %raw_sensor.1), channel_id=1, source_target_pairs={{0,3},{1,0},{2,1},{3,2},{4,7},{5,4},{6,5},{7,6},{8,11},{9,8},{10,9... | collective-permute-start | bytes 786440 | tf_op jit(solution)/shard_map/ppermute | solution.py:31
  7.5 3.3 %rims.1.rims_hbm = bf16[9,32,2048]{2,1,0:T(8,128)(2,1)} custom-call(f32[9,32,1536]{2,1,0:T(8,128)} %bitcast.20), custom_call_target="tpu_custom_call" | custom-call | bytes 8388608 | tf_op jit(solution)/shard_map/rims/pallas_call | solution.py:566
  10.9 4.4 %outgoing_histories.1 = f32[16,288,128]{2,1,0:T(8,128)S(1)} custom-call(s32[1,32]{1,0:T(1,128)S(1)} %bitcast.10, bf16[9,32,4096]{2,1,0:T(8,128)(2,1)} %bitcast.16, bf16[9,32,4096]{2,1,0:T(8,128)(2,1)} %bitcast.18), custom_call_target="tpu_custom_call" | custom-call | bytes 8388608 | tf_op jit(solution)/shard_map/outgoing_histories/pallas_call | solution.py:548
  15.3 3.7 %collective-permute-done.1.above_ref = bf16[32,4096]{1,0:T(8,128)(2,1)S(1)} collective-permute-done((bf16[32,4096]{1,0:T(8,128)(2,1)}, bf16[32,4096]{1,0:T(8,128)(2,1)S(1)}, u32[]{:S(2)}, u32[]{:S(2)}) %collective-permute-start.1) | collective-permute-done | bytes 262176 | tf_op jit(solution)/shard_map/ppermute | solution.py:31
  19.1 2.2 %filtered_sensor.1 = (f32[32,4096]{1,0:T(8,128)}, f32[1,128]{1,0:T(1,128)S(1)}) custom-call(s32[2,16]{1,0:T(2,128)S(1)} %copy-done.3, f32[32,96]{1,0:T(8,128)S(1)} %copy-done.1, f32[32,4096]{1,0:T(8,128)S(1)} %copy-done, bf16[32,4096]{1,0:T(8,128)(2,1)S(1)} %collective-permute-done.below_ref, bf16[32,4096]{1,0:T(8,128)(2,1)S(1)} %collective-permute-done.1.above_ref, ...), custom_call_target="tpu_custom_call" | custom-call | bytes 4194304 | tf_op jit(solution)/shard_map/filtered_sensor/pallas_call | solution.py:583
  21.2 1.1 %collective-permute-start.2 = (f32[1,128]{1,0:T(1,128)S(1)}, f32[1,128]{1,0:T(1,128)S(1)}, u32[]{:S(2)}, u32[]{:S(2)}) collective-permute-start(f32[1,128]{1,0:T(1,128)S(1)} %get-tuple-element.15), channel_id=1, source_target_pairs={{0,1},{1,2},{2,3},{3,0},{4,5},{5,6},{6,7},{7,4},{8,9},{9,10},{10,1... | collective-permute-start | bytes 1544 | tf_op jit(solution)/shard_map/ppermute | solution.py:31
  22.4 1.2 %convert_element_type.6 = f16[16,288,128]{2,1,0:T(8,128)(2,1)} convert(f32[16,288,128]{2,1,0:T(8,128)S(1)} %outgoing_histories.1) | non-fusion elementwise | flops 589824 | bytes 3538944 | tf_op jit(solution)/shard_map/convert_element_type | solution.py:562
  23.6 1.8 %collective-permute-start.3 = (f32[1,128]{1,0:T(1,128)S(1)}, f32[1,128]{1,0:T(1,128)S(1)}, u32[]{:S(2)}, u32[]{:S(2)}) collective-permute-start(f32[1,128]{1,0:T(1,128)S(1)} %get-tuple-element.15), channel_id=1, source_target_pairs={{0,2},{1,3},{2,0},{3,1},{4,6},{5,7},{6,4},{7,5},{8,10},{9,11},{10,... | collective-permute-start | bytes 1544 | tf_op jit(solution)/shard_map/ppermute | solution.py:31
  25.3 1.3 %collective-permute-start.4 = (f32[1,128]{1,0:T(1,128)S(1)}, f32[1,128]{1,0:T(1,128)S(1)}, u32[]{:S(2)}, u32[]{:S(2)}) collective-permute-start(f32[1,128]{1,0:T(1,128)S(1)} %get-tuple-element.15), channel_id=1, source_target_pairs={{0,3},{1,0},{2,1},{3,2},{4,7},{5,4},{6,5},{7,6},{8,11},{9,8},{10,9... | collective-permute-start | bytes 1544 | tf_op jit(solution)/shard_map/ppermute | solution.py:31
  26.7 1.3 %collective-permute-done.3 = f32[1,128]{1,0:T(1,128)S(1)} collective-permute-done((f32[1,128]{1,0:T(1,128)S(1)}, f32[1,128]{1,0:T(1,128)S(1)}, u32[]{:S(2)}, u32[]{:S(2)}) %collective-permute-start.3) | collective-permute-done | bytes 544 | tf_op jit(solution)/shard_map/ppermute | solution.py:31
  28.0 0.8 collective-permute-done.4
  28.9 5.5 %all-to-all-start = ((f16[16,288,128]{2,1,0:T(8,128)(2,1)}), f16[16,288,128]{2,1,0:T(8,128)(2,1)S(1)}, u32[]{:S(2)}, u32[]{:S(2)}) async-start(f16[16,288,128]{2,1,0:T(8,128)(2,1)} %convert_element_type.6), calls=%async_computation | async-start | bytes 2359296 | tf_op jit(solution)/shard_map/all_to_all | solution.py:597
  35.1 6.9 %kept_histories.1.base_hbm = f32[9,32,4096]{2,1,0:T(8,128)} custom-call(s32[1]{0:T(128)S(6)} %copy.27.live_ref, s32[1,32]{1,0:T(1,128)} %bitcast.9, s32[1,32]{1,0:T(1,128)} %bitcast.12, f32[9,32,4096]{2,1,0:T(8,128)} %bitcast.14, bf16[9,32,4096]{2,1,0:T(8,128)(2,1)} %bitcast.17, bf16[9,32,4096]{2,1,0:T(8,128)(2,1)} %bitcast.19), custom_call_target="tpu_custom_call" | custom-call | bytes 18874368 | tf_op jit(solution)/shard_map/kept_histories/pallas_call | solution.py:600
  42.0 1.6 %collective-permute-start.5 = (f32[4,128]{1,0:T(4,128)S(1)}, f32[4,128]{1,0:T(4,128)S(1)}, u32[]{:S(2)}, u32[]{:S(2)}) collective-permute-start(f32[4,128]{1,0:T(4,128)S(1)} %dynamic_update_slice.33), channel_id=1, source_target_pairs={{0,16},{16,0},{1,17},{17,1},{2,18},{18,2},{3,19},{19,3},{4,20},{20... | collective-permute-start | bytes 6152 | tf_op jit(solution)/shard_map/ppermute | solution.py:31
  43.6 2.1 %collective-permute-done.5 = f32[4,128]{1,0:T(4,128)S(1)} collective-permute-done((f32[4,128]{1,0:T(4,128)S(1)}, f32[4,128]{1,0:T(4,128)S(1)}, u32[]{:S(2)}, u32[]{:S(2)}) %collective-permute-start.5) | collective-permute-done | bytes 2080 | tf_op jit(solution)/shard_map/ppermute | solution.py:31
  45.7 1.8 %collective-permute-start.7 = (f32[4,256]{1,0:T(4,128)S(1)}, f32[4,256]{1,0:T(4,128)S(1)}, u32[]{:S(2)}, u32[]{:S(2)}) collective-permute-start(f32[4,256]{1,0:T(4,128)S(1)} %constant_dynamic-update-slice_fusion.4), channel_id=1, source_target_pairs={{0,8},{4,12},{8,0},{12,4},{1,9},{5,13},{9,1},{13,5},{2,10},{6,14},... | collective-permute-start | bytes 12296 | tf_op jit(solution)/shard_map/ppermute | solution.py:31
  47.5 1.4 %collective-permute-start.8 = (f32[4,256]{1,0:T(4,128)S(1)}, f32[4,256]{1,0:T(4,128)S(1)}, u32[]{:S(2)}, u32[]{:S(2)}) collective-permute-start(f32[4,256]{1,0:T(4,128)S(1)} %constant_dynamic-update-slice_fusion.4), channel_id=1, source_target_pairs={{0,12},{4,0},{8,4},{12,8},{1,13},{5,1},{9,5},{13,9},{2,14},{6,2},{... | collective-permute-start | bytes 12296 | tf_op jit(solution)/shard_map/ppermute | solution.py:31
  49.0 0.7 collective-permute-done.7
  49.7 0.6 collective-permute-done.8
  50.9 24.4 %updates.1 = (f32[9,32,4096]{2,1,0:T(8,128)}, bf16[9,32,4096]{2,1,0:T(8,128)(2,1)}) custom-call(s32[1]{0:T(128)S(6)} %copy.27.live_ref, f32[9,9]{1,0:T(8,128)} %rate_ref.1, f32[16,256]{1,0:T(8,128)} %copy-done.5, s32[1,32]{1,0:T(1,128)} %bitcast.23, f32[3,32]{1,0:T(4,128)} %velocity_ref.1, bf16[768,768]{1,0:T(8,128)(2,1)} %constant.96.clone.weights_hbm, ...), custom_call_target="tpu_custom_call" | custom-call | bytes 41943040 | tf_op jit(solution)/shard_map/updates/pallas_call | solution.py:621
  75.3 1.7 %convert_element_type.7.arrived_hbm = f32[16,288,128]{2,1,0:T(8,128)} convert(f16[16,288,128]{2,1,0:T(8,128)(2,1)S(1)} %all-to-all-done) | non-fusion elementwise | flops 589824 | bytes 3538944 | tf_op jit(solution)/shard_map/convert_element_type | solution.py:599
  76.9 6.2 %arrived_histories.1 = f32[9,32,4096]{2,1,0:T(8,128)} custom-call(s32[1]{0:T(128)S(6)} %copy.27.live_ref, f32[16,256]{1,0:T(8,128)} %copy-done.5, f32[9,32,4096]{2,1,0:T(8,128)} %get-tuple-element.19.fields_hbm, f32[16,288,128]{2,1,0:T(8,128)} %convert_element_type.7.arrived_hbm), custom_call_target="tpu_custom_call" | custom-call | bytes 12582912 | tf_op jit(solution)/shard_map/arrived_histories/pallas_call | solution.py:657
  (30 shorter events, 0.8 us)
Async XLA Ops:
  0.6 10.2 %copy-start.2 = (s32[32]{0:T(128)S(1)}, s32[32]{0:T(128)}, u32[]{:S(2)}) copy-start(s32[32]{0:T(128)} %param.20) | copy-start | bytes 388
  2.4 12.9 %collective-permute-start = (bf16[32,4096]{1,0:T(8,128)(2,1)}, bf16[32,4096]{1,0:T(8,128)(2,1)S(1)}, u32[]{:S(2)}, u32[]{:S(2)}) collective-permute-start(bf16[32,4096]{1,0:T(8,128)(2,1)} %raw_sensor.1), channel_id=1, source_target_pairs={{0,1},{1,2},{2,3},{3,0},{4,5},{5,6},{6,7},{7,4},{8,9},{9,10},{10,1... | collective-permute-start | bytes 786440 | tf_op jit(solution)/shard_map/ppermute | solution.py:31
  5.5 13.6 %collective-permute-start.1 = (bf16[32,4096]{1,0:T(8,128)(2,1)}, bf16[32,4096]{1,0:T(8,128)(2,1)S(1)}, u32[]{:S(2)}, u32[]{:S(2)}) collective-permute-start(bf16[32,4096]{1,0:T(8,128)(2,1)} %raw_sensor.1), channel_id=1, source_target_pairs={{0,3},{1,0},{2,1},{3,2},{4,7},{5,4},{6,5},{7,6},{8,11},{9,8},{10,9... | collective-permute-start | bytes 786440 | tf_op jit(solution)/shard_map/ppermute | solution.py:31
  10.8 8.2 %copy-start = (f32[32,4096]{1,0:T(8,128)S(1)}, f32[32,4096]{1,0:T(8,128)}, u32[]{:S(2)}) copy-start(f32[32,4096]{1,0:T(8,128)} %sensor_ref.3) | copy-start | bytes 1572868
  10.9 8.2 %copy-start.1 = (f32[32,96]{1,0:T(8,128)S(1)}, f32[32,96]{1,0:T(8,128)}, u32[]{:S(2)}) copy-start(f32[32,96]{1,0:T(8,128)} %constant.95.clone.weights_ref) | copy-start | bytes 36868
  10.9 8.2 %copy-start.3 = (s32[2,16]{1,0:T(2,128)S(1)}, s32[2,16]{1,0:T(2,128)}, u32[]{:S(2)}) copy-start(s32[2,16]{1,0:T(2,128)} %flags_ref.3) | copy-start | bytes 388
  10.9 8.2 %copy-start.4 = (s32[32]{0:T(128)S(1)}, s32[32]{0:T(128)}, u32[]{:S(2)}) copy-start(s32[32]{0:T(128)} %param.21) | copy-start | bytes 388
  21.2 5.5 %collective-permute-start.2 = (f32[1,128]{1,0:T(1,128)S(1)}, f32[1,128]{1,0:T(1,128)S(1)}, u32[]{:S(2)}, u32[]{:S(2)}) collective-permute-start(f32[1,128]{1,0:T(1,128)S(1)} %get-tuple-element.15), channel_id=1, source_target_pairs={{0,1},{1,2},{2,3},{3,0},{4,5},{5,6},{6,7},{7,4},{8,9},{9,10},{10,1... | collective-permute-start | bytes 1544 | tf_op jit(solution)/shard_map/ppermute | solution.py:31
  23.6 4.4 %collective-permute-start.3 = (f32[1,128]{1,0:T(1,128)S(1)}, f32[1,128]{1,0:T(1,128)S(1)}, u32[]{:S(2)}, u32[]{:S(2)}) collective-permute-start(f32[1,128]{1,0:T(1,128)S(1)} %get-tuple-element.15), channel_id=1, source_target_pairs={{0,2},{1,3},{2,0},{3,1},{4,6},{5,7},{6,4},{7,5},{8,10},{9,11},{10,... | collective-permute-start | bytes 1544 | tf_op jit(solution)/shard_map/ppermute | solution.py:31
  25.3 3.5 %collective-permute-start.4 = (f32[1,128]{1,0:T(1,128)S(1)}, f32[1,128]{1,0:T(1,128)S(1)}, u32[]{:S(2)}, u32[]{:S(2)}) collective-permute-start(f32[1,128]{1,0:T(1,128)S(1)} %get-tuple-element.15), channel_id=1, source_target_pairs={{0,3},{1,0},{2,1},{3,2},{4,7},{5,4},{6,5},{7,6},{8,11},{9,8},{10,9... | collective-permute-start | bytes 1544 | tf_op jit(solution)/shard_map/ppermute | solution.py:31
  28.9 46.4 %all-to-all-start = ((f16[16,288,128]{2,1,0:T(8,128)(2,1)}), f16[16,288,128]{2,1,0:T(8,128)(2,1)S(1)}, u32[]{:S(2)}, u32[]{:S(2)}) async-start(f16[16,288,128]{2,1,0:T(8,128)(2,1)} %convert_element_type.6), calls=%async_computation | async-start | bytes 2359296 | tf_op jit(solution)/shard_map/all_to_all | solution.py:597
  42.0 3.7 %collective-permute-start.5 = (f32[4,128]{1,0:T(4,128)S(1)}, f32[4,128]{1,0:T(4,128)S(1)}, u32[]{:S(2)}, u32[]{:S(2)}) collective-permute-start(f32[4,128]{1,0:T(4,128)S(1)} %dynamic_update_slice.33), channel_id=1, source_target_pairs={{0,16},{16,0},{1,17},{17,1},{2,18},{18,2},{3,19},{19,3},{4,20},{20... | collective-permute-start | bytes 6152 | tf_op jit(solution)/shard_map/ppermute | solution.py:31
  45.7 3.3 %collective-permute-start.6 = (f32[4,256]{1,0:T(4,128)S(1)}, f32[4,256]{1,0:T(4,128)S(1)}, u32[]{:S(2)}, u32[]{:S(2)}) collective-permute-start(f32[4,256]{1,0:T(4,128)S(1)} %constant_dynamic-update-slice_fusion.4), channel_id=1, source_target_pairs={{0,4},{4,8},{8,12},{12,0},{1,5},{5,9},{9,13},{13,1},{2,6},{6,10},{... | collective-permute-start | bytes 12296 | tf_op jit(solution)/shard_map/ppermute | solution.py:31
  45.7 4.0 %collective-permute-start.7 = (f32[4,256]{1,0:T(4,128)S(1)}, f32[4,256]{1,0:T(4,128)S(1)}, u32[]{:S(2)}, u32[]{:S(2)}) collective-permute-start(f32[4,256]{1,0:T(4,128)S(1)} %constant_dynamic-update-slice_fusion.4), channel_id=1, source_target_pairs={{0,8},{4,12},{8,0},{12,4},{1,9},{5,13},{9,1},{13,5},{2,10},{6,14},... | collective-permute-start | bytes 12296 | tf_op jit(solution)/shard_map/ppermute | solution.py:31
  47.5 2.8 %collective-permute-start.8 = (f32[4,256]{1,0:T(4,128)S(1)}, f32[4,256]{1,0:T(4,128)S(1)}, u32[]{:S(2)}, u32[]{:S(2)}) collective-permute-start(f32[4,256]{1,0:T(4,128)S(1)} %constant_dynamic-update-slice_fusion.4), channel_id=1, source_target_pairs={{0,12},{4,0},{8,4},{12,8},{1,13},{5,1},{9,5},{13,9},{2,14},{6,2},{... | collective-permute-start | bytes 12296 | tf_op jit(solution)/shard_map/ppermute | solution.py:31
  50.3 0.6 copy-start.5

commit v4 on v2

--- a/solution.py
+++ b/solution.py
@@ -97,7 +97,7 @@
             )
             thick = 1.0 + (thicken - 1.0) * (total / float(TE * FACE))
             row = jnp.where(lane == r * TCOL + k, thick, row)
-    row_ref[...] = row
+    row_ref[...] = jnp.broadcast_to(row, row_ref.shape)
 
 
 def send_kernel(
@@ -171,56 +171,6 @@
         store(s).wait()
 
 
-def base_kernel(
-    live_ref,
-    destination_ref,
-    target_ref,
-    fields_hbm,
-    recent_hbm,
-    older_hbm,
-    base_hbm,
-    fields_ref,
-    recent_ref,
-    older_ref,
-    got,
-    sent,
-):
-    species, slots, _ = fields_ref.shape
-
-    def fetches(s):
-        pairs = ((fields_hbm, fields_ref), (recent_hbm, recent_ref), (older_hbm, older_ref))
-        return [
-            pltpu.make_async_copy(here.at[s], there.at[s], got.at[n, s])
-            for n, (here, there) in enumerate(pairs)
-        ]
-
-    def store(s):
-        return pltpu.make_async_copy(fields_ref.at[s], base_hbm.at[s], sent.at[s])
-
-    for s in range(species):
-        for copy in fetches(s):
-            copy.start()
-    slot = lax.broadcasted_iota(jnp.int32, (slots, slots), 0)
-    keep = (destination_ref[...] == lax.axis_index(TEAM)) & (target_ref[...] == slot)
-    keep = keep.astype(jnp.bfloat16)
-    live = lax.broadcasted_iota(jnp.int32, (slots, 1), 0) < live_ref[0]
-    live = jnp.where(live, 1.0, 0.0)
-
-    def one(s, carry):
-        for copy in fetches(s):
-            copy.wait()
-        recent = jnp.dot(keep, recent_ref[s], preferred_element_type=jnp.float32)
-        older = jnp.dot(keep, older_ref[s], preferred_element_type=jnp.float32)
-        kept = recent * (-16.0 / 12.0 * step_size) + older * (5.0 / 12.0 * step_size)
-        fields_ref[s] = (fields_ref[s] + kept) * live
-        store(s).start()
-        return carry
-
-    lax.fori_loop(0, species, one, 0)
-    for s in range(species):
-        store(s).wait()
-
-
 def plane_weights():
     weights = np.zeros((6 * LANES, 3 * FACE), np.float32)
     for cell in range(FACE):
@@ -245,17 +195,22 @@
     table_ref,
     tiles_ref,
     velocity_ref,
+    destination_ref,
+    target_ref,
     weights_hbm,
     fields_hbm,
     ghosts_hbm,
     rims_hbm,
-    base_hbm,
+    recent_hbm,
+    older_hbm,
     new_fields_hbm,
     new_tend_hbm,
     weights_ref,
     fields_ref,
     rims_ref,
-    base_ref,
+    recent_ref,
+    older_ref,
+    new_fields_ref,
     new_tend_ref,
     mix_ref,
     wide_ref,
@@ -267,22 +222,18 @@
     sums_odd_ref,
     react_even_ref,
     react_odd_ref,
+    kept_even_ref,
+    kept_odd_ref,
     got,
     sent,
 ):
-    species, slots, cells = base_ref.shape
-    peers = table_ref.shape[0]
+    species, slots, cells = new_fields_ref.shape
+    devices = table_ref.shape[0]
     chunk = PLANES * FACE
     chunks = cells // chunk
 
     def span(c, length, skipped=0):
         return pl.ds(pl.multiple_of(skipped + c * length, LANES), length)
-
-    def bases(c):
-        lanes = span(c, chunk)
-        return pltpu.make_async_copy(
-            base_hbm.at[:, :, lanes], base_ref.at[:, :, lanes], got.at[2, c]
-        )
 
     def cells_in(c):
         lanes, rims, inner = span(c, chunk), span(c, chunk // 2), span(c, chunk, FACE)
@@ -293,18 +244,24 @@
             pltpu.make_async_copy(
                 rims_hbm.at[:, :, rims], rims_ref.at[:, :, rims], got.at[1, c]
             ),
+            pltpu.make_async_copy(
+                recent_hbm.at[:, :, lanes], recent_ref.at[:, :, lanes], got.at[2, c]
+            ),
+            pltpu.make_async_copy(
+                older_hbm.at[:, :, lanes], older_ref.at[:, :, lanes], got.at[3, c]
+            ),
         )
 
     def ends():
         return (
-            pltpu.make_async_copy(weights_hbm, weights_ref, got.at[3, 0]),
-            pltpu.make_async_copy(
-                ghosts_hbm.at[:, :, pl.ds(0, FACE)], fields_ref.at[:, :, pl.ds(0, FACE)], got.at[3, 1]
+            pltpu.make_async_copy(weights_hbm, weights_ref, got.at[4, 0]),
+            pltpu.make_async_copy(
+                ghosts_hbm.at[:, :, pl.ds(0, FACE)], fields_ref.at[:, :, pl.ds(0, FACE)], got.at[4, 1]
             ),
             pltpu.make_async_copy(
                 ghosts_hbm.at[:, :, pl.ds(FACE, FACE)],
                 fields_ref.at[:, :, pl.ds(FACE + cells, FACE)],
-                got.at[3, 2],
+                got.at[4, 2],
             ),
         )
 
@@ -312,7 +269,7 @@
         lanes = span(c, chunk)
         return (
             pltpu.make_async_copy(
-                base_ref.at[:, :, lanes], new_fields_hbm.at[:, :, lanes], sent.at[0, c]
+                new_fields_ref.at[:, :, lanes], new_fields_hbm.at[:, :, lanes], sent.at[0, c]
             ),
             pltpu.make_async_copy(
                 new_tend_ref.at[:, :, lanes], new_tend_hbm.at[:, :, lanes], sent.at[1, c]
@@ -322,15 +279,14 @@
     for copy in ends():
         copy.start()
     for c in range(2):
-        for copy in (*cells_in(c), bases(c)):
+        for copy in cells_in(c):
             copy.start()
 
     marks = jnp.concatenate(
         [velocity_ref[...], tiles_ref[...].astype(jnp.float32), jnp.zeros((4, slots), jnp.float32)], axis=0
     ).T
     tiles = marks[:, 3:4].astype(jnp.int32)
-    owner = tiles // slots
-    wanted = lax.broadcasted_iota(jnp.int32, (slots, peers), 1) == owner % peers
+    wanted = lax.broadcasted_iota(jnp.int32, (slots, devices), 1) == tiles // slots
     picked = jnp.dot(
         wanted.astype(jnp.float32),
         table_ref[...],
@@ -338,12 +294,11 @@
         preferred_element_type=jnp.float32,
     )
     lane = lax.broadcasted_iota(jnp.int32, picked.shape, 1)
-    spot = owner // peers * LANES + tiles % slots
-    thick = jnp.sum(jnp.where(lane == spot, picked, 0.0), axis=1, keepdims=True)
+    thick = jnp.sum(jnp.where(lane == tiles % slots, picked, 0.0), axis=1, keepdims=True)
     live = lax.broadcasted_iota(jnp.int32, (slots, 1), 0) < live_ref[0]
     live = jnp.where(live, 1.0, 0.0)
     parts = [viscous * thick * live, live / thick]
-    parts += [0.5 * live * marks[:, d : d + 1] for d in range(3)]
+    parts += [0.5 * live * marks[:, d : d + 1] for d in range(3)] + [live]
     for n, part in enumerate(parts):
         wide_ref[n] = jnp.broadcast_to(part, (slots, LANES))
     main = (species - 1) * slots
@@ -369,6 +324,9 @@
         fuel_ref[3 * main + 3 * slots :, :] = jnp.zeros((LANES - 3 * slots, 2 * FACE), jnp.bfloat16)
 
     parity = lax.broadcasted_iota(jnp.int32, (slots, 2 * LANES), 1) // TE % 2
+    slot = lax.broadcasted_iota(jnp.int32, (slots, slots), 0)
+    keep = (destination_ref[...] == lax.axis_index(TEAM)) & (target_ref[...] == slot)
+    keep = keep.astype(jnp.bfloat16)
 
     def sums(pair, odd):
         left_ref, sums_ref = ((left_even_ref, sums_even_ref), (left_odd_ref, sums_odd_ref))[odd]
@@ -385,6 +343,13 @@
                 left_ref[rows, 2 * FACE :] = jnp.where(parity == p, both, jnp.zeros_like(both))
         sums_ref[...] = jnp.dot(left_ref[...], weights_ref[...], preferred_element_type=jnp.float32)
 
+        kept_ref = (kept_even_ref, kept_odd_ref)[odd]
+        both = pl.ds(pl.multiple_of(2 * pair * FACE, FACE), 2 * FACE)
+        for s in range(species):
+            recent = jnp.dot(keep, recent_ref[s, :, both], preferred_element_type=jnp.float32)
+            older = jnp.dot(keep, older_ref[s, :, both], preferred_element_type=jnp.float32)
+            kept_ref[s] = recent * (-16.0 / 12.0 * step_size) + older * (5.0 / 12.0 * step_size)
+
         fuel_ref, react_ref = ((fuel_even_ref, react_even_ref), (fuel_odd_ref, react_odd_ref))[odd]
         both = pl.ds(pl.multiple_of((2 * pair + 1) * FACE, FACE), 2 * FACE)
         over = jnp.concatenate([wide_ref[1]] * 4, axis=1)
@@ -399,6 +364,7 @@
         react_ref[...] = jnp.dot(mix_ref[...], fuel_ref[...], preferred_element_type=jnp.float32)
 
     def finish(pair, odd):
+        kept_ref = (kept_even_ref, kept_odd_ref)[odd]
         sums_ref, react_ref = ((sums_even_ref, react_even_ref), (sums_odd_ref, react_odd_ref))[odd]
         for p in range(2):
             inner, before, here, after = (
@@ -406,8 +372,8 @@
             )
             for g in range(slots // 16):
                 rows = slice(g * 16, (g + 1) * 16)
-                smooth, vx, vy, vz = (
-                    jnp.concatenate([wide_ref[n, rows, :]] * 2, axis=1) for n in (0, 2, 3, 4)
+                smooth, vx, vy, vz, live = (
+                    jnp.concatenate([wide_ref[n, rows, :]] * 2, axis=1) for n in (0, 2, 3, 4, 5)
                 )
                 for s in range(species):
                     low, high = fields_ref[s, rows, before], fields_ref[s, rows, after]
@@ -419,7 +385,9 @@
                     )
                     tend = smooth * (total + (low + high)) - vx * (high - low)
                     tend = (tend - vy * along_y) + (react - vz * along_z)
-                    base_ref[s, rows, inner] += (step_size * 23.0 / 12.0) * tend
+                    kept = kept_ref[s, rows, p * FACE : (p + 1) * FACE]
+                    new = (fields_ref[s, rows, here] + kept) * live
+                    new_fields_ref[s, rows, inner] = new + (step_size * 23.0 / 12.0) * tend
                     new_tend_ref[s, rows, inner] = tend.astype(jnp.bfloat16)
 
     for copy in (*ends(), *cells_in(0)):
@@ -429,10 +397,9 @@
     def four(c, carry):
         @pl.when(c + 2 < chunks)
         def _():
-            for copy in (*cells_in(c + 2), bases(c + 2)):
+            for copy in cells_in(c + 2):
                 copy.start()
 
-        bases(c).wait()
         sums(2 * c + 1, 1)
         finish(2 * c, 0)
 
@@ -472,8 +439,8 @@
     for s in range(AHEAD):
         for copy in fetches(s):
             copy.start()
-    me, first = lax.axis_index(TEAM), pl.multiple_of(lax.axis_index("grp") * LANES, LANES)
-    notes = table_ref[:, pl.ds(first, LANES)]
+    me, first = lax.axis_index(TEAM), pl.multiple_of(lax.axis_index("grp") * peers, peers)
+    notes = table_ref[pl.ds(first, peers), :]
     destination = notes[:, slots : 2 * slots]
     target = notes[:, 2 * slots : 3 * slots]
     peer = lax.broadcasted_iota(jnp.int32, (peers, slots), 0)
@@ -533,6 +500,7 @@
 ):
     slots, species, cells = fields.shape
     peers = lax.axis_size(TEAM)
+    devices = lax.axis_size(EVERY)
     brick = sensor.shape[0]
     fields, ghosts, recent, older = (
         a.transpose(1, 0, 2) for a in (fields, ghosts, recent_tend, older_tend)
@@ -571,22 +539,6 @@
 
     shape = jax.ShapeDtypeStruct((species, slots, cells), jnp.float32)
     rims = jax.ShapeDtypeStruct((species, slots, TE * LANES), jnp.bfloat16)
-    base = pl.pallas_call(
-        base_kernel,
-        name="kept_histories",
-        out_shape=shape,
-        in_specs=[smem(), vmem, vmem] + [anywhere] * 3,
-        out_specs=anywhere,
-        scratch_shapes=[
-            pltpu.VMEM(shape.shape, jnp.float32),
-            pltpu.VMEM(shape.shape, jnp.bfloat16),
-            pltpu.VMEM(shape.shape, jnp.bfloat16),
-            pltpu.SemaphoreType.DMA((3, species)),
-            pltpu.SemaphoreType.DMA((species,)),
-        ],
-        compiler_params=params(58),
-        cost_estimate=pl.CostEstimate(flops=0, bytes_accessed=18 << 20, transcendentals=0),
-    )(live_counts, *moves, fields, recent, older)
     rims = pl.pallas_call(
         rims_kernel,
         name="rims",
@@ -604,22 +556,21 @@
     )(ghosts)
     below, above, rims = lax.optimization_barrier((below, above, rims))
 
-    filtered, row = pl.pallas_call(
+    filtered, rows = pl.pallas_call(
         filter_kernel,
         name="filtered_sensor",
         out_shape=(
             jax.ShapeDtypeStruct(sensor.shape, jnp.float32),
-            jax.ShapeDtypeStruct((1, LANES), jnp.float32),
+            jax.ShapeDtypeStruct((devices, LANES), jnp.float32),
         ),
         in_specs=[smem()] + [vmem] * 6,
         out_specs=(vmem, vmem),
         compiler_params=params(32),
         cost_estimate=pl.CostEstimate(flops=0, bytes_accessed=4 << 20, transcendentals=0),
     )(flame_flags, jnp.asarray(banded(brick, brick)), sensor, below, above, *moves)
-    rows = gathered(row, ("pen",))
-    rows, outgoing, base = lax.optimization_barrier((rows, outgoing, base))
+    table = lax.all_to_all(rows, EVERY, split_axis=0, concat_axis=0, tiled=True)
+    table, outgoing = lax.optimization_barrier((table, outgoing))
     arrived = lax.all_to_all(outgoing, TEAM, split_axis=0, concat_axis=0, tiled=True)
-    table = gathered(rows, ("grp", "mig"))
     arrived = arrived.astype(jnp.float32)
 
     weights = jnp.asarray(plane_weights(), jnp.bfloat16)
@@ -628,20 +579,23 @@
     depth = 3 * (species - 1) * slots + LANES
     fuel = pltpu.VMEM((depth, 2 * FACE), jnp.bfloat16)
     react = pltpu.VMEM((species * slots, 2 * FACE), jnp.float32)
+    kept = pltpu.VMEM((species, slots, 2 * FACE), jnp.float32)
     new_fields, new_tend = pl.pallas_call(
         main_kernel,
         name="updates",
         out_shape=(shape, jax.ShapeDtypeStruct(shape.shape, jnp.bfloat16)),
-        in_specs=[smem()] * 2 + [vmem] * 3 + [anywhere] * 5,
+        in_specs=[smem()] * 2 + [vmem] * 5 + [anywhere] * 6,
         out_specs=(anywhere, anywhere),
         scratch_shapes=[
             pltpu.VMEM(weights.shape, jnp.bfloat16),
             pltpu.VMEM((species, slots, cells + 2 * FACE), jnp.float32),
             pltpu.VMEM(rims.shape, jnp.bfloat16),
+            pltpu.VMEM(shape.shape, jnp.bfloat16),
+            pltpu.VMEM(shape.shape, jnp.bfloat16),
             pltpu.VMEM(shape.shape, jnp.float32),
             pltpu.VMEM(shape.shape, jnp.bfloat16),
             pltpu.VMEM((species * slots, depth), jnp.bfloat16),
-            pltpu.VMEM((5, slots, LANES), jnp.float32),
+            pltpu.VMEM((6, slots, LANES), jnp.float32),
             left,
             left,
             fuel,
@@ -650,7 +604,9 @@
             sums,
             react,
             react,
-            pltpu.SemaphoreType.DMA((4, TE // PLANES)),
+            kept,
+            kept,
+            pltpu.SemaphoreType.DMA((5, TE // PLANES)),
             pltpu.SemaphoreType.DMA((2, TE // PLANES)),
         ],
         compiler_params=params(58),
@@ -661,11 +617,13 @@
         table,
         tile_ids.reshape(1, slots),
         velocity,
+        *moves,
         weights,
         fields,
         ghosts,
         rims,
-        base,
+        recent,
+        older,
     )
 
     new_fields = pl.pallas_call(
@@ -684,24 +642,6 @@
         cost_estimate=pl.CostEstimate(flops=0, bytes_accessed=12 << 20, transcendentals=0),
     )(live_counts, table, new_fields, arrived)
     return new_fields.transpose(1, 0, 2), new_tend.transpose(1, 0, 2), filtered
-
-
-def gathered(row, axes):
-    for axis in axes:
-        count = lax.axis_size(axis)
-        here = lax.axis_index(axis)
-        rows = [row] + [passed_along(row, axis, by) for by in range(1, count)]
-        height, width = row.shape
-        if axis == "grp":
-            table = jnp.zeros((height, count * width), row.dtype)
-        else:
-            table = jnp.zeros((count * height, width), row.dtype)
-        for by, part in enumerate(rows):
-            place = (here - by) % count
-            place = (0, place * width) if axis == "grp" else (place * height, 0)
-            table = lax.dynamic_update_slice(table, part, place)
-        row = table
-    return row
 
 
 def solution(mesh):

time: 75.9 us -> 75.8 us (level)
  waiting for transfers between devices: 7.9 us -> 19.3 us
  Pallas kernels: 44.1 us -> 38.2 us
  starting transfers between devices: 18 us -> 13.5 us
  local copies, waits for them, and re-layouts: 0.83 us -> 0.03 us
    ppermute x9 -> x2, starting transfers between devices: 14.1 us -> 5.05 us  [passed_along(): return lax.ppermute(x, axis, [(i, (i + by) % peers) for i in range(peers)])]
    all_to_all x1, waiting for transfers between devices: 0.01 us -> 8.85 us  [local(): lax.all_to_all(outgoing, TEAM, split_axis=0, concat_axis=0, tiled=True)]
    pallas_call x1 -> x0, Pallas kernels: 6.87 us -> none  [local(): pl.pallas_call(base_kernel, name='kept_histories', out_shape=shape, in_sp...]
    all_to_all x0 -> x1, starting transfers between devices: none -> 3.99 us  [local(): table = lax.all_to_all(rows, EVERY, split_axis=0, concat_axis=0, tiled=True)]
    all_to_all x0 -> x1, waiting for transfers between devices: none -> 1.51 us  [local(): table = lax.all_to_all(rows, EVERY, split_axis=0, concat_axis=0, tiled=True)]
    ppermute x9 -> x2, waiting for transfers between devices: 7.9 us -> 8.97 us  [passed_along(): return lax.ppermute(x, axis, [(i, (i + by) % peers) for i in range(peers)])]
    pallas_call x1, Pallas kernels: 19.3 us -> 20.3 us  [local(): pl.pallas_call(main_kernel, name='updates', out_shape=(shape, jax.ShapeDt...]
  transfers between devices with their start and end apart: 10 -> 4, of which waited for: 4 -> 4; matrix products, arithmetic and copies ran while one was open for 2% -> 2% of each run, Pallas kernels for 45% -> 37%
where the time goes in v4:
time: 75.8 us; the launch traced here: 75.3 us
  Pallas kernels  38.2 us (50%)
  waiting for transfers between devices  19.3 us (25%)
  starting transfers between devices  13.5 us (18%)
  other arithmetic  2.88 us (4%)
  between operations  1.39 us (2%)
    pallas_call x1, Pallas kernels, local(): pl.pallas_call(main_kernel, name='updates', out_shape=(shape, jax.ShapeDt...  20.3 us
    ppermute x2, waiting for transfers between devices, passed_along(): return lax.ppermute(x, axis, [(i, (i + by) % peers) for i in range(peers)])  8.97 us
    all_to_all x1, waiting for transfers between devices, local(): lax.all_to_all(outgoing, TEAM, split_axis=0, concat_axis=0, tiled=True)  8.85 us
    pallas_call x1, Pallas kernels, local(): pl.pallas_call(add_kernel, name='arrived_histories', out_shape=shape, in_...  6.23 us
    ppermute x2, starting transfers between devices, passed_along(): return lax.ppermute(x, axis, [(i, (i + by) % peers) for i in range(peers)])  5.05 us
    all_to_all x1, starting transfers between devices, local(): lax.all_to_all(outgoing, TEAM, split_axis=0, concat_axis=0, tiled=True)  4.41 us
    pallas_call x1, Pallas kernels, local(): pl.pallas_call(send_kernel, name='outgoing_histories', out_shape=jax.Shap...  4.37 us
    all_to_all x1, starting transfers between devices, local(): table = lax.all_to_all(rows, EVERY, split_axis=0, concat_axis=0, tiled=True)  3.99 us
  transfers between devices with their start and end apart: 4, of which 4 were waited for; matrix products, arithmetic and copies ran while one was open for 2% of the time, Pallas kernels for 37%

profile of v4, /device:TPU:0, one launch (start us, length us, event | category | flops | bytes accessed | tf_op | source)
XLA Modules:
  0.0 75.3 jit_solution(12027122437384897741)
XLA Ops:
  0.6 0.0 copy-start.1
  0.6 0.0 copy-start.3
  0.7 0.0 copy-start
  0.7 0.0 copy-start.4
  0.7 0.0 copy-start.2
  0.7 1.8 %raw_sensor.1 = bf16[32,4096]{1,0:T(8,128)(2,1)} custom-call(s32[2,16]{1,0:T(2,128)} %flags_ref.3, f32[32,4096]{1,0:T(8,128)} %sensor_ref.3), custom_call_target="tpu_custom_call" | custom-call | tf_op jit(solution)/shard_map/raw_sensor/pallas_call | solution.py:510
  2.5 5.0 %collective-permute-start.1 = (bf16[32,4096]{1,0:T(8,128)(2,1)}, bf16[32,4096]{1,0:T(8,128)(2,1)S(1)}, u32[]{:S(2)}, u32[]{:S(2)}) collective-permute-start(bf16[32,4096]{1,0:T(8,128)(2,1)} %raw_sensor.1), channel_id=1, source_target_pairs={{0,3},{1,0},{2,1},{3,2},{4,7},{5,4},{6,5},{7,6},{8,11},{9,8},{10,9... | collective-permute-start | bytes 786440 | tf_op jit(solution)/shard_map/ppermute | solution.py:31
  7.6 0.0 collective-permute-start
  7.6 3.3 %rims.1.rims_hbm = bf16[9,32,2048]{2,1,0:T(8,128)(2,1)} custom-call(f32[9,32,1536]{2,1,0:T(8,128)} %bitcast.22), custom_call_target="tpu_custom_call" | custom-call | bytes 8388608 | tf_op jit(solution)/shard_map/rims/pallas_call | solution.py:542
  10.9 3.7 %collective-permute-done.1.above_ref = bf16[32,4096]{1,0:T(8,128)(2,1)S(1)} collective-permute-done((bf16[32,4096]{1,0:T(8,128)(2,1)}, bf16[32,4096]{1,0:T(8,128)(2,1)S(1)}, u32[]{:S(2)}, u32[]{:S(2)}) %collective-permute-start.1) | collective-permute-done | bytes 262176 | tf_op jit(solution)/shard_map/ppermute | solution.py:31
  14.6 5.3 %collective-permute-done.below_ref = bf16[32,4096]{1,0:T(8,128)(2,1)S(1)} collective-permute-done((bf16[32,4096]{1,0:T(8,128)(2,1)}, bf16[32,4096]{1,0:T(8,128)(2,1)S(1)}, u32[]{:S(2)}, u32[]{:S(2)}) %collective-permute-start) | collective-permute-done | bytes 262176 | tf_op jit(solution)/shard_map/ppermute | solution.py:31
  19.9 0.0 copy-done.1
  19.9 0.0 copy-done.3
  19.9 0.0 copy-done
  19.9 2.2 %filtered_sensor.1 = (f32[32,4096]{1,0:T(8,128)}, f32[32,128]{1,0:T(8,128)}) custom-call(s32[2,16]{1,0:T(2,128)S(1)} %copy-done.3, f32[32,96]{1,0:T(8,128)S(1)} %copy-done.1, f32[32,4096]{1,0:T(8,128)S(1)} %copy-done, bf16[32,4096]{1,0:T(8,128)(2,1)S(1)} %collective-permute-done.below_ref, bf16[32,4096]{1,0:T(8,128)(2,1)S(1)} %collective-permute-done.1.above_ref, ...), custom_call_target="tpu_custom_call" | custom-call | bytes 4194304 | tf_op jit(solution)/shard_map/filtered_sensor/pallas_call | solution.py:559
  22.1 4.0 %all-to-all-start = ((f32[32,1,128]{2,1,0:T(1,128)}), f32[32,1,128]{2,1,0:T(1,128)S(1)}, u32[]{:S(2)}, u32[]{:S(2)}) async-start(f32[32,1,128]{2,1,0:T(1,128)} %bitcast.4), calls=%async_computation | async-start | bytes 32768 | tf_op jit(solution)/shard_map/all_to_all | solution.py:571
  26.1 4.4 %outgoing_histories.1 = f32[16,288,128]{2,1,0:T(8,128)S(1)} custom-call(s32[1,32]{1,0:T(1,128)S(1)} %bitcast.15, bf16[9,32,4096]{2,1,0:T(8,128)(2,1)} %bitcast.18, bf16[9,32,4096]{2,1,0:T(8,128)(2,1)} %bitcast.20), custom_call_target="tpu_custom_call" | custom-call | bytes 8388608 | tf_op jit(solution)/shard_map/outgoing_histories/pallas_call | solution.py:524
  30.5 1.2 %convert_element_type.6 = f16[16,288,128]{2,1,0:T(8,128)(2,1)} convert(f32[16,288,128]{2,1,0:T(8,128)S(1)} %outgoing_histories.1) | non-fusion elementwise | flops 589824 | bytes 3538944 | tf_op jit(solution)/shard_map/convert_element_type | solution.py:538
  31.7 1.5 %all-to-all-done = f32[32,1,128]{2,1,0:T(1,128)S(1)} async-done(((f32[32,1,128]{2,1,0:T(1,128)}), f32[32,1,128]{2,1,0:T(1,128)S(1)}, u32[]{:S(2)}, u32[]{:S(2)}) %all-to-all-start) | async-done | bytes 16416 | tf_op jit(solution)/shard_map/all_to_all | solution.py:571
  33.2 4.4 %all-to-all-start.1 = ((f16[16,288,128]{2,1,0:T(8,128)(2,1)}), f16[16,288,128]{2,1,0:T(8,128)(2,1)S(1)}, u32[]{:S(2)}, u32[]{:S(2)}) async-start(f16[16,288,128]{2,1,0:T(8,128)(2,1)} %convert_element_type.6), calls=%async_computation.1 | async-start | bytes 2359296 | tf_op jit(solution)/shard_map/all_to_all | solution.py:573
  38.3 20.3 %updates.1 = (f32[9,32,4096]{2,1,0:T(8,128)}, bf16[9,32,4096]{2,1,0:T(8,128)(2,1)}) custom-call(s32[1]{0:T(128)S(6)} %copy.18.live_ref, f32[9,9]{1,0:T(8,128)} %rate_ref.1, f32[32,128]{1,0:T(8,128)} %bitcast.26, s32[1,32]{1,0:T(1,128)} %bitcast.28, f32[3,32]{1,0:T(4,128)} %velocity_ref.1, s32[1,32]{1,0:T(1,128)} %bitcast.13, s32[1,32]{1,0:T(1,128)} %bitcast.16, ...), custom_call_target="tpu_custom_call" | custom-call | bytes 41943040 | tf_op jit(solution)/shard_map/updates/pallas_call | solution.py:583
  58.5 8.8 %all-to-all-done.1 = f16[16,288,128]{2,1,0:T(8,128)(2,1)S(1)} async-done(((f16[16,288,128]{2,1,0:T(8,128)(2,1)}), f16[16,288,128]{2,1,0:T(8,128)(2,1)S(1)}, u32[]{:S(2)}, u32[]{:S(2)}) %all-to-all-start.1) | async-done | bytes 1179680 | tf_op jit(solution)/shard_map/all_to_all | solution.py:573
  67.4 1.7 %convert_element_type.7.arrived_hbm = f32[16,288,128]{2,1,0:T(8,128)} convert(f16[16,288,128]{2,1,0:T(8,128)(2,1)S(1)} %all-to-all-done.1) | non-fusion elementwise | flops 589824 | bytes 3538944 | tf_op jit(solution)/shard_map/convert_element_type | solution.py:574
  69.1 6.2 %arrived_histories.1 = f32[9,32,4096]{2,1,0:T(8,128)} custom-call(s32[1]{0:T(128)S(6)} %copy.18.live_ref, f32[32,128]{1,0:T(8,128)} %bitcast.27, f32[9,32,4096]{2,1,0:T(8,128)} %get-tuple-element.17.fields_hbm, f32[16,288,128]{2,1,0:T(8,128)} %convert_element_type.7.arrived_hbm), custom_call_target="tpu_custom_call" | custom-call | bytes 12582912 | tf_op jit(solution)/shard_map/arrived_histories/pallas_call | solution.py:629
  (4 shorter events, 0.0 us)
Async XLA Ops:
  0.6 19.3 %copy-start.1 = (f32[32,96]{1,0:T(8,128)S(1)}, f32[32,96]{1,0:T(8,128)}, u32[]{:S(2)}) copy-start(f32[32,96]{1,0:T(8,128)} %constant.4.clone.weights_ref) | copy-start | bytes 36868
  0.6 19.2 %copy-start.3 = (s32[2,16]{1,0:T(2,128)S(1)}, s32[2,16]{1,0:T(2,128)}, u32[]{:S(2)}) copy-start(s32[2,16]{1,0:T(2,128)} %flags_ref.3) | copy-start | bytes 388
  0.7 19.2 %copy-start = (f32[32,4096]{1,0:T(8,128)S(1)}, f32[32,4096]{1,0:T(8,128)}, u32[]{:S(2)}) copy-start(f32[32,4096]{1,0:T(8,128)} %sensor_ref.3) | copy-start | bytes 1572868
  0.7 19.2 %copy-start.4 = (s32[32]{0:T(128)S(1)}, s32[32]{0:T(128)}, u32[]{:S(2)}) copy-start(s32[32]{0:T(128)} %param.21) | copy-start | bytes 388
  0.7 19.2 %copy-start.2 = (s32[32]{0:T(128)S(1)}, s32[32]{0:T(128)}, u32[]{:S(2)}) copy-start(s32[32]{0:T(128)} %param.20) | copy-start | bytes 388
  2.5 12.1 %collective-permute-start.1 = (bf16[32,4096]{1,0:T(8,128)(2,1)}, bf16[32,4096]{1,0:T(8,128)(2,1)S(1)}, u32[]{:S(2)}, u32[]{:S(2)}) collective-permute-start(bf16[32,4096]{1,0:T(8,128)(2,1)} %raw_sensor.1), channel_id=1, source_target_pairs={{0,3},{1,0},{2,1},{3,2},{4,7},{5,4},{6,5},{7,6},{8,11},{9,8},{10,9... | collective-permute-start | bytes 786440 | tf_op jit(solution)/shard_map/ppermute | solution.py:31
  7.6 12.3 %collective-permute-start = (bf16[32,4096]{1,0:T(8,128)(2,1)}, bf16[32,4096]{1,0:T(8,128)(2,1)S(1)}, u32[]{:S(2)}, u32[]{:S(2)}) collective-permute-start(bf16[32,4096]{1,0:T(8,128)(2,1)} %raw_sensor.1), channel_id=1, source_target_pairs={{0,1},{1,2},{2,3},{3,0},{4,5},{5,6},{6,7},{7,4},{8,9},{9,10},{10,1... | collective-permute-start | bytes 786440 | tf_op jit(solution)/shard_map/ppermute | solution.py:31
  22.1 11.1 %all-to-all-start = ((f32[32,1,128]{2,1,0:T(1,128)}), f32[32,1,128]{2,1,0:T(1,128)S(1)}, u32[]{:S(2)}, u32[]{:S(2)}) async-start(f32[32,1,128]{2,1,0:T(1,128)} %bitcast.4), calls=%async_computation | async-start | bytes 32768 | tf_op jit(solution)/shard_map/all_to_all | solution.py:571
  33.2 5.1 %copy-start.5 = (f32[32,1,128]{2,1,0:T(1,128)}, f32[32,1,128]{2,1,0:T(1,128)S(1)}, u32[]{:S(2)}) copy-start(f32[32,1,128]{2,1,0:T(1,128)S(1)} %all-to-all-done) | copy-start | bytes 49156
  33.2 34.2 %all-to-all-start.1 = ((f16[16,288,128]{2,1,0:T(8,128)(2,1)}), f16[16,288,128]{2,1,0:T(8,128)(2,1)S(1)}, u32[]{:S(2)}, u32[]{:S(2)}) async-start(f16[16,288,128]{2,1,0:T(8,128)(2,1)} %convert_element_type.6), calls=%async_computation.1 | async-start | bytes 2359296 | tf_op jit(solution)/shard_map/all_to_all | solution.py:573

commit v5 on v4

--- a/solution.py
+++ b/solution.py
@@ -421,10 +421,21 @@
 
 
 def add_kernel(
-    live_ref, table_ref, fields_hbm, arrived_hbm, out_hbm, fields_ref, arrived_ref, got, sent
+    live_ref,
+    table_ref,
+    fields_hbm,
+    arrived_hbm,
+    out_hbm,
+    fields_ref,
+    arrived_ref,
+    hot_ref,
+    parts_ref,
+    got,
+    sent,
 ):
     species, peers = arrived_ref.shape[:2]
     slots = fields_ref.shape[1]
+    depth = peers * ROWS
 
     def fetches(s):
         part = arrived_hbm.at[:, pl.ds(s * ROWS, ROWS)]
@@ -436,7 +447,7 @@
     def store(s):
         return pltpu.make_async_copy(fields_ref.at[s], out_hbm.at[s], sent.at[s])
 
-    for s in range(AHEAD):
+    for s in range(species):
         for copy in fetches(s):
             copy.start()
     me, first = lax.axis_index(TEAM), pl.multiple_of(lax.axis_index("grp") * peers, peers)
@@ -448,26 +459,33 @@
     slot = jnp.max(jnp.where(mine, target, -1.0), axis=1, keepdims=True)
     index = lax.broadcasted_iota(jnp.int32, (peers, slots), 1)
     hot = (slot == index.astype(jnp.float32)) & (index < live_ref[0])
-    hot = jnp.where(hot, step_size / SCALE, 0.0)
-    hot = jnp.concatenate([hot, hot], axis=0).T.astype(jnp.bfloat16)
-    for s in range(species):
-        if s + AHEAD < species:
-            for copy in fetches(s + AHEAD):
-                copy.start()
-        for copy in fetches(s):
-            copy.wait()
-        flat = arrived_ref.at[s].reshape(peers * ROWS, LANES)
-        for c in range(ROWS // 2):
-            lanes = slice(c * 2 * LANES, (c + 1) * 2 * LANES)
-            arrived = jnp.concatenate(
-                [flat[pl.ds(2 * c + k, peers, stride=ROWS), :] for k in range(2)], axis=1
-            )
+    hot = jnp.where(hot, step_size / SCALE, 0.0).astype(jnp.bfloat16)
+    spread = lax.broadcasted_iota(jnp.int32, (peers, depth), 1) // ROWS
+    spread = (spread == lax.broadcasted_iota(jnp.int32, (peers, depth), 0)).astype(jnp.bfloat16)
+    wide = lax.dot_general(hot, spread, (((0,), (0,)), ((), ())), preferred_element_type=jnp.float32)
+    part = lax.broadcasted_iota(jnp.int32, (slots, depth), 1) % ROWS
+    for k in range(ROWS):
+        lines = jnp.where(part == k, wide, 0.0).astype(jnp.bfloat16)
+        hot_ref[k * slots : (k + 1) * slots, 0:depth] = lines
+        hot_ref[k * slots : (k + 1) * slots, depth:] = lines
+    for first in range(0, species, 2):
+        here = range(first, min(first + 2, species))
+        for n, s in enumerate(here):
+            for copy in fetches(s):
+                copy.wait()
+            arrived = arrived_ref.at[s].reshape(depth, LANES)[...]
             high = arrived.astype(jnp.bfloat16)
-            low = (arrived - high.astype(jnp.float32)).astype(jnp.bfloat16)
-            fields_ref[s, :, lanes] += jnp.dot(
-                hot, jnp.concatenate([high, low], axis=0), preferred_element_type=jnp.float32
-            )
-        store(s).start()
+            lanes = slice(n * LANES, (n + 1) * LANES)
+            parts_ref[0:depth, lanes] = high
+            parts_ref[depth:, lanes] = (arrived - high.astype(jnp.float32)).astype(jnp.bfloat16)
+        placed = jnp.dot(hot_ref[...], parts_ref[...], preferred_element_type=jnp.float32)
+        for n, s in enumerate(here):
+            for k in range(ROWS):
+                lanes = slice(k * LANES, (k + 1) * LANES)
+                fields_ref[s, :, lanes] += placed[
+                    k * slots : (k + 1) * slots, n * LANES : (n + 1) * LANES
+                ]
+            store(s).start()
     for s in range(species):
         store(s).wait()
 
@@ -554,7 +572,7 @@
         compiler_params=params(58),
         cost_estimate=pl.CostEstimate(flops=0, bytes_accessed=8 << 20, transcendentals=0),
     )(ghosts)
-    below, above, rims = lax.optimization_barrier((below, above, rims))
+    below, above, rims, outgoing = lax.optimization_barrier((below, above, rims, outgoing))
 
     filtered, rows = pl.pallas_call(
         filter_kernel,
@@ -635,6 +653,8 @@
         scratch_shapes=[
             pltpu.VMEM(shape.shape, jnp.float32),
             pltpu.VMEM((species, peers, ROWS, LANES), jnp.float32),
+            pltpu.VMEM((slots * ROWS, 2 * peers * ROWS), jnp.bfloat16),
+            pltpu.VMEM((2 * peers * ROWS, 2 * LANES), jnp.bfloat16),
             pltpu.SemaphoreType.DMA((2, species)),
             pltpu.SemaphoreType.DMA((species,)),
         ],

time: 75.8 us -> 78.1 us (1.030)
  blocking collectives: 0 us -> 11.1 us
  waiting for transfers between devices: 19.3 us -> 11.9 us
  starting transfers between devices: 13.5 us -> 8.93 us
  Pallas kernels: 38.2 us -> 41.3 us
    all_to_all x0 -> x1, blocking collectives: none -> 11.1 us  [local(): table = lax.all_to_all(rows, EVERY, split_axis=0, concat_axis=0, tiled=True)]
    ppermute x2, waiting for transfers between devices: 8.97 us -> 3.31 us  [passed_along(): return lax.ppermute(x, axis, [(i, (i + by) % peers) for i in range(peers)])]
    all_to_all x1 -> x0, starting transfers between devices: 3.99 us -> none  [local(): table = lax.all_to_all(rows, EVERY, split_axis=0, concat_axis=0, tiled=True)]
    pallas_call x1, Pallas kernels: 6.23 us -> 9.37 us  [local(): pl.pallas_call(add_kernel, name='arrived_histories', out_shape=shape, in_...]
    all_to_all x1 -> x0, waiting for transfers between devices: 1.51 us -> none  [local(): table = lax.all_to_all(rows, EVERY, split_axis=0, concat_axis=0, tiled=True)]
  transfers between devices with their start and end apart: 4 -> 3, of which waited for: 4 -> 2; matrix products, arithmetic and copies ran while one was open for 2% -> 2% of each run, Pallas kernels for 37% -> 36%
where the time goes in v5:
time: 78.1 us; the launch traced here: 77.7 us
  Pallas kernels  41.3 us (53%)
  waiting for transfers between devices  11.9 us (15%)
  blocking collectives  11.1 us (14%)
  starting transfers between devices  8.93 us (11%)
  other arithmetic  2.89 us (4%)
  between operations  1.53 us (2%)
    pallas_call x1, Pallas kernels, local(): pl.pallas_call(main_kernel, name='updates', out_shape=(shape, jax.ShapeDt...  20.3 us
    all_to_all x1, blocking collectives, local(): table = lax.all_to_all(rows, EVERY, split_axis=0, concat_axis=0, tiled=True)  11.1 us
    pallas_call x1, Pallas kernels, local(): pl.pallas_call(add_kernel, name='arrived_histories', out_shape=shape, in_...  9.37 us
    all_to_all x1, waiting for transfers between devices, local(): lax.all_to_all(outgoing, TEAM, split_axis=0, concat_axis=0, tiled=True)  8.6 us
    ppermute x2, starting transfers between devices, passed_along(): return lax.ppermute(x, axis, [(i, (i + by) % peers) for i in range(peers)])  5.05 us
    pallas_call x1, Pallas kernels, local(): pl.pallas_call(send_kernel, name='outgoing_histories', out_shape=jax.Shap...  4.37 us
    all_to_all x1, starting transfers between devices, local(): lax.all_to_all(outgoing, TEAM, split_axis=0, concat_axis=0, tiled=True)  3.88 us
    ppermute x2, waiting for transfers between devices, passed_along(): return lax.ppermute(x, axis, [(i, (i + by) % peers) for i in range(peers)])  3.31 us
  transfers between devices with their start and end apart: 3, of which 2 were waited for; matrix products, arithmetic and copies ran while one was open for 2% of the time, Pallas kernels for 36%

profile of v5, /device:TPU:0, one launch (start us, length us, event | category | flops | bytes accessed | tf_op | source)
XLA Modules:
  0.0 77.7 jit_solution(3603305523827354268)
XLA Ops:
  0.6 0.0 copy-start.2
  0.6 1.8 %raw_sensor.1 = bf16[32,4096]{1,0:T(8,128)(2,1)} custom-call(s32[2,16]{1,0:T(2,128)} %flags_ref.3, f32[32,4096]{1,0:T(8,128)} %sensor_ref.3), custom_call_target="tpu_custom_call" | custom-call | tf_op jit(solution)/shard_map/raw_sensor/pallas_call | solution.py:528
  2.4 5.0 %collective-permute-start.1 = (bf16[32,4096]{1,0:T(8,128)(2,1)}, bf16[32,4096]{1,0:T(8,128)(2,1)S(1)}, u32[]{:S(2)}, u32[]{:S(2)}) collective-permute-start(bf16[32,4096]{1,0:T(8,128)(2,1)} %raw_sensor.1), channel_id=1, source_target_pairs={{0,3},{1,0},{2,1},{3,2},{4,7},{5,4},{6,5},{7,6},{8,11},{9,8},{10,9... | collective-permute-start | bytes 786440 | tf_op jit(solution)/shard_map/ppermute | solution.py:31
  7.5 0.0 collective-permute-start
  7.5 3.3 %rims.1.rims_hbm = bf16[9,32,2048]{2,1,0:T(8,128)(2,1)} custom-call(f32[9,32,1536]{2,1,0:T(8,128)} %bitcast.23), custom_call_target="tpu_custom_call" | custom-call | bytes 8388608 | tf_op jit(solution)/shard_map/rims/pallas_call | solution.py:560
  10.8 0.0 copy-done.2
  10.8 4.4 %outgoing_histories.1 = f32[16,288,128]{2,1,0:T(8,128)S(1)} custom-call(s32[1,32]{1,0:T(1,128)S(1)} %bitcast.15, bf16[9,32,4096]{2,1,0:T(8,128)(2,1)} %bitcast.19, bf16[9,32,4096]{2,1,0:T(8,128)(2,1)} %bitcast.21), custom_call_target="tpu_custom_call" | custom-call | bytes 8388608 | tf_op jit(solution)/shard_map/outgoing_histories/pallas_call | solution.py:542
  15.2 0.0 copy-start
  15.2 0.0 copy-start.1
  15.2 0.0 copy-start.3
  15.2 0.0 copy-start.4
  15.2 1.2 %convert_element_type.6 = f16[16,288,128]{2,1,0:T(8,128)(2,1)} convert(f32[16,288,128]{2,1,0:T(8,128)S(1)} %outgoing_histories.1) | non-fusion elementwise | flops 589824 | bytes 3538944 | tf_op jit(solution)/shard_map/convert_element_type | solution.py:556
  16.5 0.0 collective-permute-done.1.above_ref
  16.5 3.3 %collective-permute-done.below_ref = bf16[32,4096]{1,0:T(8,128)(2,1)S(1)} collective-permute-done((bf16[32,4096]{1,0:T(8,128)(2,1)}, bf16[32,4096]{1,0:T(8,128)(2,1)S(1)}, u32[]{:S(2)}, u32[]{:S(2)}) %collective-permute-start) | collective-permute-done | bytes 262176 | tf_op jit(solution)/shard_map/ppermute | solution.py:31
  19.8 0.0 copy-done
  19.8 0.0 copy-done.1
  19.8 0.0 copy-done.3
  19.8 2.2 %filtered_sensor.1 = (f32[32,4096]{1,0:T(8,128)}, f32[32,128]{1,0:T(8,128)S(1)}) custom-call(s32[2,16]{1,0:T(2,128)S(1)} %copy-done.3, f32[32,96]{1,0:T(8,128)S(1)} %copy-done.1, f32[32,4096]{1,0:T(8,128)S(1)} %copy-done, bf16[32,4096]{1,0:T(8,128)(2,1)S(1)} %collective-permute-done.below_ref, bf16[32,4096]{1,0:T(8,128)(2,1)S(1)} %collective-permute-done.1.above_ref, ...), custom_call_target="tpu_custom_call" | custom-call | bytes 4194304 | tf_op jit(solution)/shard_map/filtered_sensor/pallas_call | solution.py:577
  22.0 11.1 %all_to_all.17 = f32[32,1,128]{2,1,0:T(1,128)} all-to-all(f32[32,1,128]{2,1,0:T(1,128)S(1)} %bitcast.13), channel_id=1, replica_groups=mesh['grp'=2,'mig'=4,'pen'=4] {'grp','mig','pen'}, dimensions={0} | all-to-all | bytes 32768 | tf_op jit(solution)/shard_map/all_to_all | solution.py:589
  33.0 3.9 %all-to-all-start.1 = ((f16[16,288,128]{2,1,0:T(8,128)(2,1)}), f16[16,288,128]{2,1,0:T(8,128)(2,1)S(1)}, u32[]{:S(2)}, u32[]{:S(2)}) async-start(f16[16,288,128]{2,1,0:T(8,128)(2,1)} %convert_element_type.6), calls=%async_computation.1 | async-start | bytes 2359296 | tf_op jit(solution)/shard_map/all_to_all | solution.py:591
  37.6 20.3 %updates.1 = (f32[9,32,4096]{2,1,0:T(8,128)}, bf16[9,32,4096]{2,1,0:T(8,128)(2,1)}) custom-call(s32[1]{0:T(128)S(6)} %copy.18.live_ref, f32[9,9]{1,0:T(8,128)} %rate_ref.1, f32[32,128]{1,0:T(8,128)} %bitcast.27, s32[1,32]{1,0:T(1,128)} %bitcast.29, f32[3,32]{1,0:T(4,128)} %velocity_ref.1, s32[1,32]{1,0:T(1,128)} %bitcast.14, s32[1,32]{1,0:T(1,128)} %bitcast.17, ...), custom_call_target="tpu_custom_call" | custom-call | bytes 41943040 | tf_op jit(solution)/shard_map/updates/pallas_call | solution.py:601
  57.9 8.6 %all-to-all-done.1 = f16[16,288,128]{2,1,0:T(8,128)(2,1)S(1)} async-done(((f16[16,288,128]{2,1,0:T(8,128)(2,1)}), f16[16,288,128]{2,1,0:T(8,128)(2,1)S(1)}, u32[]{:S(2)}, u32[]{:S(2)}) %all-to-all-start.1) | async-done | bytes 1179680 | tf_op jit(solution)/shard_map/all_to_all | solution.py:591
  66.5 1.7 %convert_element_type.7.arrived_hbm = f32[16,288,128]{2,1,0:T(8,128)} convert(f16[16,288,128]{2,1,0:T(8,128)(2,1)S(1)} %all-to-all-done.1) | non-fusion elementwise | flops 589824 | bytes 3538944 | tf_op jit(solution)/shard_map/convert_element_type | solution.py:592
  68.1 9.4 %arrived_histories.1 = f32[9,32,4096]{2,1,0:T(8,128)} custom-call(s32[1]{0:T(128)S(6)} %copy.18.live_ref, f32[32,128]{1,0:T(8,128)} %bitcast.28, f32[9,32,4096]{2,1,0:T(8,128)} %get-tuple-element.19.fields_hbm, f32[16,288,128]{2,1,0:T(8,128)} %convert_element_type.7.arrived_hbm), custom_call_target="tpu_custom_call" | custom-call | bytes 12582912 | tf_op jit(solution)/shard_map/arrived_histories/pallas_call | solution.py:647
  (1 shorter events, 0.0 us)
Async XLA Ops:
  0.6 10.2 %copy-start.2 = (s32[32]{0:T(128)S(1)}, s32[32]{0:T(128)}, u32[]{:S(2)}) copy-start(s32[32]{0:T(128)} %param.20) | copy-start | bytes 388
  2.4 14.0 %collective-permute-start.1 = (bf16[32,4096]{1,0:T(8,128)(2,1)}, bf16[32,4096]{1,0:T(8,128)(2,1)S(1)}, u32[]{:S(2)}, u32[]{:S(2)}) collective-permute-start(bf16[32,4096]{1,0:T(8,128)(2,1)} %raw_sensor.1), channel_id=1, source_target_pairs={{0,3},{1,0},{2,1},{3,2},{4,7},{5,4},{6,5},{7,6},{8,11},{9,8},{10,9... | collective-permute-start | bytes 786440 | tf_op jit(solution)/shard_map/ppermute | solution.py:31
  7.5 12.3 %collective-permute-start = (bf16[32,4096]{1,0:T(8,128)(2,1)}, bf16[32,4096]{1,0:T(8,128)(2,1)S(1)}, u32[]{:S(2)}, u32[]{:S(2)}) collective-permute-start(bf16[32,4096]{1,0:T(8,128)(2,1)} %raw_sensor.1), channel_id=1, source_target_pairs={{0,1},{1,2},{2,3},{3,0},{4,5},{5,6},{6,7},{7,4},{8,9},{9,10},{10,1... | collective-permute-start | bytes 786440 | tf_op jit(solution)/shard_map/ppermute | solution.py:31
  15.2 4.6 %copy-start = (f32[32,4096]{1,0:T(8,128)S(1)}, f32[32,4096]{1,0:T(8,128)}, u32[]{:S(2)}) copy-start(f32[32,4096]{1,0:T(8,128)} %sensor_ref.3) | copy-start | bytes 1572868
  15.2 4.6 %copy-start.1 = (f32[32,96]{1,0:T(8,128)S(1)}, f32[32,96]{1,0:T(8,128)}, u32[]{:S(2)}) copy-start(f32[32,96]{1,0:T(8,128)} %constant.4.clone.weights_ref) | copy-start | bytes 36868
  15.2 4.6 %copy-start.3 = (s32[2,16]{1,0:T(2,128)S(1)}, s32[2,16]{1,0:T(2,128)}, u32[]{:S(2)}) copy-start(s32[2,16]{1,0:T(2,128)} %flags_ref.3) | copy-start | bytes 388
  15.2 4.6 %copy-start.4 = (s32[32]{0:T(128)S(1)}, s32[32]{0:T(128)}, u32[]{:S(2)}) copy-start(s32[32]{0:T(128)} %param.21) | copy-start | bytes 388
  33.0 33.4 %all-to-all-start.1 = ((f16[16,288,128]{2,1,0:T(8,128)(2,1)}), f16[16,288,128]{2,1,0:T(8,128)(2,1)S(1)}, u32[]{:S(2)}, u32[]{:S(2)}) async-start(f16[16,288,128]{2,1,0:T(8,128)(2,1)} %convert_element_type.6), calls=%async_computation.1 | async-start | bytes 2359296 | tf_op jit(solution)/shard_map/all_to_all | solution.py:591

commit v6 on v4

--- a/solution.py
+++ b/solution.py
@@ -97,7 +97,7 @@
             )
             thick = 1.0 + (thicken - 1.0) * (total / float(TE * FACE))
             row = jnp.where(lane == r * TCOL + k, thick, row)
-    row_ref[...] = jnp.broadcast_to(row, row_ref.shape)
+    row_ref[...] = row
 
 
 def send_kernel(
@@ -214,6 +214,7 @@
     new_tend_ref,
     mix_ref,
     wide_ref,
+    mask_ref,
     left_even_ref,
     left_odd_ref,
     fuel_even_ref,
@@ -228,7 +229,7 @@
     sent,
 ):
     species, slots, cells = new_fields_ref.shape
-    devices = table_ref.shape[0]
+    peers = table_ref.shape[0]
     chunk = PLANES * FACE
     chunks = cells // chunk
 
@@ -286,7 +287,8 @@
         [velocity_ref[...], tiles_ref[...].astype(jnp.float32), jnp.zeros((4, slots), jnp.float32)], axis=0
     ).T
     tiles = marks[:, 3:4].astype(jnp.int32)
-    wanted = lax.broadcasted_iota(jnp.int32, (slots, devices), 1) == tiles // slots
+    owner = tiles // slots
+    wanted = lax.broadcasted_iota(jnp.int32, (slots, peers), 1) == owner % peers
     picked = jnp.dot(
         wanted.astype(jnp.float32),
         table_ref[...],
@@ -294,7 +296,8 @@
         preferred_element_type=jnp.float32,
     )
     lane = lax.broadcasted_iota(jnp.int32, picked.shape, 1)
-    thick = jnp.sum(jnp.where(lane == tiles % slots, picked, 0.0), axis=1, keepdims=True)
+    spot = owner // peers * LANES + tiles % slots
+    thick = jnp.sum(jnp.where(lane == spot, picked, 0.0), axis=1, keepdims=True)
     live = lax.broadcasted_iota(jnp.int32, (slots, 1), 0) < live_ref[0]
     live = jnp.where(live, 1.0, 0.0)
     parts = [viscous * thick * live, live / thick]
@@ -324,14 +327,16 @@
         fuel_ref[3 * main + 3 * slots :, :] = jnp.zeros((LANES - 3 * slots, 2 * FACE), jnp.bfloat16)
 
     parity = lax.broadcasted_iota(jnp.int32, (slots, 2 * LANES), 1) // TE % 2
+    for p in range(2):
+        mask_ref[p] = jnp.where(parity == p, 1.0, 0.0).astype(jnp.bfloat16)
     slot = lax.broadcasted_iota(jnp.int32, (slots, slots), 0)
     keep = (destination_ref[...] == lax.axis_index(TEAM)) & (target_ref[...] == slot)
     keep = keep.astype(jnp.bfloat16)
 
-    def sums(pair, odd):
-        left_ref, sums_ref = ((left_even_ref, sums_even_ref), (left_odd_ref, sums_odd_ref))[odd]
+    def build(pair, odd, some):
+        left_ref = (left_even_ref, left_odd_ref)[odd]
         rims = pl.ds(pl.multiple_of(pair * FACE, FACE), FACE)
-        for s in range(species):
+        for s in some:
             both = rims_ref[s, :, rims]
             for p in range(2):
                 lanes = pl.ds(pl.multiple_of((2 * pair + p + 1) * FACE, FACE), FACE)
@@ -340,9 +345,16 @@
                 high = f.astype(jnp.bfloat16)
                 left_ref[rows, 0:FACE] = high
                 left_ref[rows, FACE : 2 * FACE] = (f - high.astype(jnp.float32)).astype(jnp.bfloat16)
-                left_ref[rows, 2 * FACE :] = jnp.where(parity == p, both, jnp.zeros_like(both))
-        sums_ref[...] = jnp.dot(left_ref[...], weights_ref[...], preferred_element_type=jnp.float32)
-
+                left_ref[rows, 2 * FACE :] = both * mask_ref[p]
+
+    def multiply(pair, odd, d):
+        left_ref, sums_ref = ((left_even_ref, sums_even_ref), (left_odd_ref, sums_odd_ref))[odd]
+        columns = slice(d * FACE, (d + 1) * FACE)
+        sums_ref[:, columns] = jnp.dot(
+            left_ref[...], weights_ref[:, columns], preferred_element_type=jnp.float32
+        )
+
+    def burn(pair, odd):
         kept_ref = (kept_even_ref, kept_odd_ref)[odd]
         both = pl.ds(pl.multiple_of(2 * pair * FACE, FACE), 2 * FACE)
         for s in range(species):
@@ -363,7 +375,7 @@
                 fuel_ref[start : start + slots, :] = part
         react_ref[...] = jnp.dot(mix_ref[...], fuel_ref[...], preferred_element_type=jnp.float32)
 
-    def finish(pair, odd):
+    def finish(pair, odd, some):
         kept_ref = (kept_even_ref, kept_odd_ref)[odd]
         sums_ref, react_ref = ((sums_even_ref, react_even_ref), (sums_odd_ref, react_odd_ref))[odd]
         for p in range(2):
@@ -375,7 +387,7 @@
                 smooth, vx, vy, vz, live = (
                     jnp.concatenate([wide_ref[n, rows, :]] * 2, axis=1) for n in (0, 2, 3, 4, 5)
                 )
-                for s in range(species):
+                for s in some:
                     low, high = fields_ref[s, rows, before], fields_ref[s, rows, after]
                     line = s * slots + g * 16
                     react = react_ref[line : line + 16, p * FACE : (p + 1) * FACE]
@@ -390,9 +402,24 @@
                     new_fields_ref[s, rows, inner] = new + (step_size * 23.0 / 12.0) * tend
                     new_tend_ref[s, rows, inner] = tend.astype(jnp.bfloat16)
 
+    thirds = [range(n * species // 3, (n + 1) * species // 3) for n in range(3)]
+    pairs = TE // 2
+
+    def stage(pair, odd):
+        after, later = jnp.minimum(pair + 1, pairs - 1), jnp.minimum(pair + 2, pairs - 1)
+        burn(after, 1 - odd)
+        for d, some in enumerate(thirds):
+            multiply(after, 1 - odd, d)
+            finish(pair, odd, some)
+            build(later, odd, some)
+
     for copy in (*ends(), *cells_in(0)):
         copy.wait()
-    sums(0, 0)
+    build(0, 0, range(species))
+    for d in range(3):
+        multiply(0, 0, d)
+    burn(0, 0)
+    build(1, 1, range(species))
 
     def four(c, carry):
         @pl.when(c + 2 < chunks)
@@ -400,16 +427,13 @@
             for copy in cells_in(c + 2):
                 copy.start()
 
-        sums(2 * c + 1, 1)
-        finish(2 * c, 0)
-
         @pl.when(c + 1 < chunks)
         def _():
             for copy in cells_in(c + 1):
                 copy.wait()
 
-        sums(jnp.minimum(2 * c + 2, 2 * (chunks - 1)), 0)
-        finish(2 * c + 1, 1)
+        stage(2 * c, 0)
+        stage(2 * c + 1, 1)
         for copy in stores(c):
             copy.start()
         return carry
@@ -439,8 +463,8 @@
     for s in range(AHEAD):
         for copy in fetches(s):
             copy.start()
-    me, first = lax.axis_index(TEAM), pl.multiple_of(lax.axis_index("grp") * peers, peers)
-    notes = table_ref[pl.ds(first, peers), :]
+    me, first = lax.axis_index(TEAM), pl.multiple_of(lax.axis_index("grp") * LANES, LANES)
+    notes = table_ref[:, pl.ds(first, LANES)]
     destination = notes[:, slots : 2 * slots]
     target = notes[:, 2 * slots : 3 * slots]
     peer = lax.broadcasted_iota(jnp.int32, (peers, slots), 0)
@@ -500,7 +524,6 @@
 ):
     slots, species, cells = fields.shape
     peers = lax.axis_size(TEAM)
-    devices = lax.axis_size(EVERY)
     brick = sensor.shape[0]
     fields, ghosts, recent, older = (
         a.transpose(1, 0, 2) for a in (fields, ghosts, recent_tend, older_tend)
@@ -554,23 +577,24 @@
         compiler_params=params(58),
         cost_estimate=pl.CostEstimate(flops=0, bytes_accessed=8 << 20, transcendentals=0),
     )(ghosts)
-    below, above, rims = lax.optimization_barrier((below, above, rims))
-
-    filtered, rows = pl.pallas_call(
+    below, above, rims, outgoing = lax.optimization_barrier((below, above, rims, outgoing))
+
+    filtered, row = pl.pallas_call(
         filter_kernel,
         name="filtered_sensor",
         out_shape=(
             jax.ShapeDtypeStruct(sensor.shape, jnp.float32),
-            jax.ShapeDtypeStruct((devices, LANES), jnp.float32),
+            jax.ShapeDtypeStruct((1, LANES), jnp.float32),
         ),
         in_specs=[smem()] + [vmem] * 6,
         out_specs=(vmem, vmem),
         compiler_params=params(32),
         cost_estimate=pl.CostEstimate(flops=0, bytes_accessed=4 << 20, transcendentals=0),
     )(flame_flags, jnp.asarray(banded(brick, brick)), sensor, below, above, *moves)
-    table = lax.all_to_all(rows, EVERY, split_axis=0, concat_axis=0, tiled=True)
-    table, outgoing = lax.optimization_barrier((table, outgoing))
+    rows = gathered(row, ("pen",))
+    rows, outgoing = lax.optimization_barrier((rows, outgoing))
     arrived = lax.all_to_all(outgoing, TEAM, split_axis=0, concat_axis=0, tiled=True)
+    table = gathered(rows, ("grp", "mig"))
     arrived = arrived.astype(jnp.float32)
 
     weights = jnp.asarray(plane_weights(), jnp.bfloat16)
@@ -596,6 +620,7 @@
             pltpu.VMEM(shape.shape, jnp.bfloat16),
             pltpu.VMEM((species * slots, depth), jnp.bfloat16),
             pltpu.VMEM((6, slots, LANES), jnp.float32),
+            pltpu.VMEM((2, slots, FACE), jnp.bfloat16),
             left,
             left,
             fuel,
@@ -644,6 +669,24 @@
     return new_fields.transpose(1, 0, 2), new_tend.transpose(1, 0, 2), filtered
 
 
+def gathered(row, axes):
+    for axis in axes:
+        count = lax.axis_size(axis)
+        here = lax.axis_index(axis)
+        rows = [row] + [passed_along(row, axis, by) for by in range(1, count)]
+        height, width = row.shape
+        if axis == "grp":
+            table = jnp.zeros((height, count * width), row.dtype)
+        else:
+            table = jnp.zeros((count * height, width), row.dtype)
+        for by, part in enumerate(rows):
+            place = (here - by) % count
+            place = (0, place * width) if axis == "grp" else (place * height, 0)
+            table = lax.dynamic_update_slice(table, part, place)
+        row = table
+    return row
+
+
 def solution(mesh):
     split = P(EVERY, None, None)
     return jax.shard_map(

time: 75.8 us -> 73.3 us (0.967)
  waiting for transfers between devices: 19.3 us -> 12 us
  starting transfers between devices: 13.5 us -> 18.2 us
  Pallas kernels: 38.2 us -> 37.3 us
  local copies, waits for them, and re-layouts: 0.03 us -> 0.81 us
    all_to_all x1, waiting for transfers between devices: 8.85 us -> 0.01 us  [local(): lax.all_to_all(outgoing, TEAM, split_axis=0, concat_axis=0, tiled=True)]
    ppermute x2 -> x9, starting transfers between devices: 5.05 us -> 12.7 us  [passed_along(): return lax.ppermute(x, axis, [(i, (i + by) % peers) for i in range(peers)])]
    all_to_all x1 -> x0, starting transfers between devices: 3.99 us -> none  [local(): table = lax.all_to_all(rows, EVERY, split_axis=0, concat_axis=0, tiled=True)]
    ppermute x2 -> x9, waiting for transfers between devices: 8.97 us -> 12 us  [passed_along(): return lax.ppermute(x, axis, [(i, (i + by) % peers) for i in range(peers)])]
    all_to_all x1 -> x0, waiting for transfers between devices: 1.51 us -> none  [local(): table = lax.all_to_all(rows, EVERY, split_axis=0, concat_axis=0, tiled=True)]
    all_to_all x1, starting transfers between devices: 4.41 us -> 5.54 us  [local(): lax.all_to_all(outgoing, TEAM, split_axis=0, concat_axis=0, tiled=True)]
    pallas_call x1, Pallas kernels: 20.3 us -> 19.4 us  [local(): pl.pallas_call(main_kernel, name='updates', out_shape=(shape, jax.ShapeDt...]
  transfers between devices with their start and end apart: 4 -> 10, of which waited for: 4 -> 6; matrix products, arithmetic and copies ran while one was open for 2% -> 2% of each run, Pallas kernels for 37% -> 37%
where the time goes in v6:
time: 73.3 us; the launch traced here: 72.9 us
  Pallas kernels  37.3 us (51%)
  starting transfers between devices  18.2 us (25%)
  waiting for transfers between devices  12 us (16%)
  other arithmetic  2.87 us (4%)
  between operations  1.67 us (2%)
  local copies, waits for them, and re-layouts  0.81 us (1%)
    pallas_call x1, Pallas kernels, local(): pl.pallas_call(main_kernel, name='updates', out_shape=(shape, jax.ShapeDt...  19.4 us
    ppermute x9, starting transfers between devices, passed_along(): return lax.ppermute(x, axis, [(i, (i + by) % peers) for i in range(peers)])  12.7 us
    ppermute x9, waiting for transfers between devices, passed_along(): return lax.ppermute(x, axis, [(i, (i + by) % peers) for i in range(peers)])  12 us
    pallas_call x1, Pallas kernels, local(): pl.pallas_call(add_kernel, name='arrived_histories', out_shape=shape, in_...  6.23 us
    all_to_all x1, starting transfers between devices, local(): lax.all_to_all(outgoing, TEAM, split_axis=0, concat_axis=0, tiled=True)  5.54 us
    pallas_call x1, Pallas kernels, local(): pl.pallas_call(send_kernel, name='outgoing_histories', out_shape=jax.Shap...  4.37 us
    pallas_call x1, Pallas kernels, local(): pl.pallas_call(rims_kernel, name='rims', out_shape=rims, in_specs=[anywhe...  3.31 us
    pallas_call x1, Pallas kernels, local(): pl.pallas_call(filter_kernel, name='filtered_sensor', out_shape=(jax.Shap...  2.17 us
  transfers between devices with their start and end apart: 10, of which 6 were waited for; matrix products, arithmetic and copies ran while one was open for 2% of the time, Pallas kernels for 37%

profile of v6, /device:TPU:0, one launch (start us, length us, event | category | flops | bytes accessed | tf_op | source)
XLA Modules:
  0.0 72.9 jit_solution(6506857530990672169)
XLA Ops:
  0.6 1.8 %raw_sensor.1 = bf16[32,4096]{1,0:T(8,128)(2,1)} custom-call(s32[2,16]{1,0:T(2,128)} %flags_ref.3, f32[32,4096]{1,0:T(8,128)} %sensor_ref.3), custom_call_target="tpu_custom_call" | custom-call | tf_op jit(solution)/shard_map/raw_sensor/pallas_call | solution.py:533
  2.4 5.0 %collective-permute-start.1 = (bf16[32,4096]{1,0:T(8,128)(2,1)}, bf16[32,4096]{1,0:T(8,128)(2,1)S(1)}, u32[]{:S(2)}, u32[]{:S(2)}) collective-permute-start(bf16[32,4096]{1,0:T(8,128)(2,1)} %raw_sensor.1), channel_id=1, source_target_pairs={{0,3},{1,0},{2,1},{3,2},{4,7},{5,4},{6,5},{7,6},{8,11},{9,8},{10,9... | collective-permute-start | bytes 786440 | tf_op jit(solution)/shard_map/ppermute | solution.py:31
  7.5 3.3 %rims.1.rims_hbm = bf16[9,32,2048]{2,1,0:T(8,128)(2,1)} custom-call(f32[9,32,1536]{2,1,0:T(8,128)} %bitcast.18), custom_call_target="tpu_custom_call" | custom-call | bytes 8388608 | tf_op jit(solution)/shard_map/rims/pallas_call | solution.py:565
  10.8 4.4 %outgoing_histories.1 = f32[16,288,128]{2,1,0:T(8,128)S(1)} custom-call(s32[1,32]{1,0:T(1,128)S(1)} %bitcast.10, bf16[9,32,4096]{2,1,0:T(8,128)(2,1)} %bitcast.14, bf16[9,32,4096]{2,1,0:T(8,128)(2,1)} %bitcast.16), custom_call_target="tpu_custom_call" | custom-call | bytes 8388608 | tf_op jit(solution)/shard_map/outgoing_histories/pallas_call | solution.py:547
  15.2 1.2 %convert_element_type.6 = f16[16,288,128]{2,1,0:T(8,128)(2,1)} convert(f32[16,288,128]{2,1,0:T(8,128)S(1)} %outgoing_histories.1) | non-fusion elementwise | flops 589824 | bytes 3538944 | tf_op jit(solution)/shard_map/convert_element_type | solution.py:561
  16.4 3.3 %collective-permute-done.below_ref = bf16[32,4096]{1,0:T(8,128)(2,1)S(1)} collective-permute-done((bf16[32,4096]{1,0:T(8,128)(2,1)}, bf16[32,4096]{1,0:T(8,128)(2,1)S(1)}, u32[]{:S(2)}, u32[]{:S(2)}) %collective-permute-start) | collective-permute-done | bytes 262176 | tf_op jit(solution)/shard_map/ppermute | solution.py:31
  19.8 2.2 %filtered_sensor.1 = (f32[32,4096]{1,0:T(8,128)}, f32[1,128]{1,0:T(1,128)S(1)}) custom-call(s32[2,16]{1,0:T(2,128)S(1)} %copy-done.3, f32[32,96]{1,0:T(8,128)S(1)} %copy-done.1, f32[32,4096]{1,0:T(8,128)S(1)} %copy-done, bf16[32,4096]{1,0:T(8,128)(2,1)S(1)} %collective-permute-done.below_ref, bf16[32,4096]{1,0:T(8,128)(2,1)S(1)} %collective-permute-done.1.above_ref, ...), custom_call_target="tpu_custom_call" | custom-call | bytes 4194304 | tf_op jit(solution)/shard_map/filtered_sensor/pallas_call | solution.py:582
  22.0 1.6 %collective-permute-start.2 = (f32[1,128]{1,0:T(1,128)S(1)}, f32[1,128]{1,0:T(1,128)S(1)}, u32[]{:S(2)}, u32[]{:S(2)}) collective-permute-start(f32[1,128]{1,0:T(1,128)S(1)} %get-tuple-element.15), channel_id=1, source_target_pairs={{0,1},{1,2},{2,3},{3,0},{4,5},{5,6},{6,7},{7,4},{8,9},{9,10},{10,1... | collective-permute-start | bytes 1544 | tf_op jit(solution)/shard_map/ppermute | solution.py:31
  23.6 0.7 collective-permute-start.3
  24.3 1.7 %collective-permute-start.4 = (f32[1,128]{1,0:T(1,128)S(1)}, f32[1,128]{1,0:T(1,128)S(1)}, u32[]{:S(2)}, u32[]{:S(2)}) collective-permute-start(f32[1,128]{1,0:T(1,128)S(1)} %get-tuple-element.15), channel_id=1, source_target_pairs={{0,3},{1,0},{2,1},{3,2},{4,7},{5,4},{6,5},{7,6},{8,11},{9,8},{10,9... | collective-permute-start | bytes 1544 | tf_op jit(solution)/shard_map/ppermute | solution.py:31
  26.0 1.3 %collective-permute-done.2 = f32[1,128]{1,0:T(1,128)S(1)} collective-permute-done((f32[1,128]{1,0:T(1,128)S(1)}, f32[1,128]{1,0:T(1,128)S(1)}, u32[]{:S(2)}, u32[]{:S(2)}) %collective-permute-start.2) | collective-permute-done | bytes 544 | tf_op jit(solution)/shard_map/ppermute | solution.py:31
  27.3 0.7 collective-permute-done.3
  28.1 5.5 %all-to-all-start = ((f16[16,288,128]{2,1,0:T(8,128)(2,1)}), f16[16,288,128]{2,1,0:T(8,128)(2,1)S(1)}, u32[]{:S(2)}, u32[]{:S(2)}) async-start(f16[16,288,128]{2,1,0:T(8,128)(2,1)} %convert_element_type.6), calls=%async_computation | async-start | bytes 2359296 | tf_op jit(solution)/shard_map/all_to_all | solution.py:596
  34.4 1.6 %collective-permute-start.5 = (f32[4,128]{1,0:T(4,128)S(1)}, f32[4,128]{1,0:T(4,128)S(1)}, u32[]{:S(2)}, u32[]{:S(2)}) collective-permute-start(f32[4,128]{1,0:T(4,128)S(1)} %dynamic_update_slice.33), channel_id=1, source_target_pairs={{0,16},{16,0},{1,17},{17,1},{2,18},{18,2},{3,19},{19,3},{4,20},{20... | collective-permute-start | bytes 6152 | tf_op jit(solution)/shard_map/ppermute | solution.py:31
  36.0 2.1 %collective-permute-done.5 = f32[4,128]{1,0:T(4,128)S(1)} collective-permute-done((f32[4,128]{1,0:T(4,128)S(1)}, f32[4,128]{1,0:T(4,128)S(1)}, u32[]{:S(2)}, u32[]{:S(2)}) %collective-permute-start.5) | collective-permute-done | bytes 2080 | tf_op jit(solution)/shard_map/ppermute | solution.py:31
  38.1 0.7 %collective-permute-start.8 = (f32[4,256]{1,0:T(4,128)S(1)}, f32[4,256]{1,0:T(4,128)S(1)}, u32[]{:S(2)}, u32[]{:S(2)}) collective-permute-start(f32[4,256]{1,0:T(4,128)S(1)} %constant_dynamic-update-slice_fusion.4), channel_id=1, source_target_pairs={{0,12},{4,0},{8,4},{12,8},{1,13},{5,1},{9,5},{13,9},{2,14},{6,2},{... | collective-permute-start | bytes 12296 | tf_op jit(solution)/shard_map/ppermute | solution.py:31
  38.8 1.1 %collective-permute-start.7 = (f32[4,256]{1,0:T(4,128)S(1)}, f32[4,256]{1,0:T(4,128)S(1)}, u32[]{:S(2)}, u32[]{:S(2)}) collective-permute-start(f32[4,256]{1,0:T(4,128)S(1)} %constant_dynamic-update-slice_fusion.4), channel_id=1, source_target_pairs={{0,8},{4,12},{8,0},{12,4},{1,9},{5,13},{9,1},{13,5},{2,10},{6,14},... | collective-permute-start | bytes 12296 | tf_op jit(solution)/shard_map/ppermute | solution.py:31
  39.9 0.2 collective-permute-start.6
  40.1 3.5 %collective-permute-done.6 = f32[4,256]{1,0:T(4,128)S(1)} collective-permute-done((f32[4,256]{1,0:T(4,128)S(1)}, f32[4,256]{1,0:T(4,128)S(1)}, u32[]{:S(2)}, u32[]{:S(2)}) %collective-permute-start.6) | collective-permute-done | bytes 4128 | tf_op jit(solution)/shard_map/ppermute | solution.py:31
  43.7 1.0 %collective-permute-done.7 = f32[4,256]{1,0:T(4,128)S(1)} collective-permute-done((f32[4,256]{1,0:T(4,128)S(1)}, f32[4,256]{1,0:T(4,128)S(1)}, u32[]{:S(2)}, u32[]{:S(2)}) %collective-permute-start.7) | collective-permute-done | bytes 4128 | tf_op jit(solution)/shard_map/ppermute | solution.py:31
  44.7 0.6 copy-done.5
  45.3 19.4 %updates.1 = (f32[9,32,4096]{2,1,0:T(8,128)}, bf16[9,32,4096]{2,1,0:T(8,128)(2,1)}) custom-call(s32[1]{0:T(128)S(6)} %copy.27.live_ref, f32[9,9]{1,0:T(8,128)} %rate_ref.1, f32[16,256]{1,0:T(8,128)} %copy-done.5, s32[1,32]{1,0:T(1,128)} %bitcast.22, f32[3,32]{1,0:T(4,128)} %velocity_ref.1, s32[1,32]{1,0:T(1,128)} %bitcast.9, s32[1,32]{1,0:T(1,128)} %bitcast.12, ...), custom_call_target="tpu_custom_call" | custom-call | bytes 41943040 | tf_op jit(solution)/shard_map/updates/pallas_call | solution.py:607
  64.8 1.7 %convert_element_type.7.arrived_hbm = f32[16,288,128]{2,1,0:T(8,128)} convert(f16[16,288,128]{2,1,0:T(8,128)(2,1)S(1)} %all-to-all-done) | non-fusion elementwise | flops 589824 | bytes 3538944 | tf_op jit(solution)/shard_map/convert_element_type | solution.py:598
  66.5 6.2 %arrived_histories.1 = f32[9,32,4096]{2,1,0:T(8,128)} custom-call(s32[1]{0:T(128)S(6)} %copy.27.live_ref, f32[16,256]{1,0:T(8,128)} %copy-done.5, f32[9,32,4096]{2,1,0:T(8,128)} %get-tuple-element.19.fields_hbm, f32[16,288,128]{2,1,0:T(8,128)} %convert_element_type.7.arrived_hbm), custom_call_target="tpu_custom_call" | custom-call | bytes 12582912 | tf_op jit(solution)/shard_map/arrived_histories/pallas_call | solution.py:654
  (29 shorter events, 0.2 us)
Async XLA Ops:
  0.6 10.2 %copy-start.2 = (s32[32]{0:T(128)S(1)}, s32[32]{0:T(128)}, u32[]{:S(2)}) copy-start(s32[32]{0:T(128)} %param.20) | copy-start | bytes 388
  2.4 14.0 %collective-permute-start.1 = (bf16[32,4096]{1,0:T(8,128)(2,1)}, bf16[32,4096]{1,0:T(8,128)(2,1)S(1)}, u32[]{:S(2)}, u32[]{:S(2)}) collective-permute-start(bf16[32,4096]{1,0:T(8,128)(2,1)} %raw_sensor.1), channel_id=1, source_target_pairs={{0,3},{1,0},{2,1},{3,2},{4,7},{5,4},{6,5},{7,6},{8,11},{9,8},{10,9... | collective-permute-start | bytes 786440 | tf_op jit(solution)/shard_map/ppermute | solution.py:31
  7.5 12.3 %collective-permute-start = (bf16[32,4096]{1,0:T(8,128)(2,1)}, bf16[32,4096]{1,0:T(8,128)(2,1)S(1)}, u32[]{:S(2)}, u32[]{:S(2)}) collective-permute-start(bf16[32,4096]{1,0:T(8,128)(2,1)} %raw_sensor.1), channel_id=1, source_target_pairs={{0,1},{1,2},{2,3},{3,0},{4,5},{5,6},{6,7},{7,4},{8,9},{9,10},{10,1... | collective-permute-start | bytes 786440 | tf_op jit(solution)/shard_map/ppermute | solution.py:31
  15.2 4.6 %copy-start = (f32[32,4096]{1,0:T(8,128)S(1)}, f32[32,4096]{1,0:T(8,128)}, u32[]{:S(2)}) copy-start(f32[32,4096]{1,0:T(8,128)} %sensor_ref.3) | copy-start | bytes 1572868
  15.2 4.6 %copy-start.1 = (f32[32,96]{1,0:T(8,128)S(1)}, f32[32,96]{1,0:T(8,128)}, u32[]{:S(2)}) copy-start(f32[32,96]{1,0:T(8,128)} %constant.95.clone.weights_ref) | copy-start | bytes 36868
  15.2 4.6 %copy-start.3 = (s32[2,16]{1,0:T(2,128)S(1)}, s32[2,16]{1,0:T(2,128)}, u32[]{:S(2)}) copy-start(s32[2,16]{1,0:T(2,128)} %flags_ref.3) | copy-start | bytes 388
  15.2 4.6 %copy-start.4 = (s32[32]{0:T(128)S(1)}, s32[32]{0:T(128)}, u32[]{:S(2)}) copy-start(s32[32]{0:T(128)} %param.21) | copy-start | bytes 388
  22.0 5.3 %collective-permute-start.2 = (f32[1,128]{1,0:T(1,128)S(1)}, f32[1,128]{1,0:T(1,128)S(1)}, u32[]{:S(2)}, u32[]{:S(2)}) collective-permute-start(f32[1,128]{1,0:T(1,128)S(1)} %get-tuple-element.15), channel_id=1, source_target_pairs={{0,1},{1,2},{2,3},{3,0},{4,5},{5,6},{6,7},{7,4},{8,9},{9,10},{10,1... | collective-permute-start | bytes 1544 | tf_op jit(solution)/shard_map/ppermute | solution.py:31
  23.6 4.4 %collective-permute-start.3 = (f32[1,128]{1,0:T(1,128)S(1)}, f32[1,128]{1,0:T(1,128)S(1)}, u32[]{:S(2)}, u32[]{:S(2)}) collective-permute-start(f32[1,128]{1,0:T(1,128)S(1)} %get-tuple-element.15), channel_id=1, source_target_pairs={{0,2},{1,3},{2,0},{3,1},{4,6},{5,7},{6,4},{7,5},{8,10},{9,11},{10,... | collective-permute-start | bytes 1544 | tf_op jit(solution)/shard_map/ppermute | solution.py:31
  24.3 3.8 %collective-permute-start.4 = (f32[1,128]{1,0:T(1,128)S(1)}, f32[1,128]{1,0:T(1,128)S(1)}, u32[]{:S(2)}, u32[]{:S(2)}) collective-permute-start(f32[1,128]{1,0:T(1,128)S(1)} %get-tuple-element.15), channel_id=1, source_target_pairs={{0,3},{1,0},{2,1},{3,2},{4,7},{5,4},{6,5},{7,6},{8,11},{9,8},{10,9... | collective-permute-start | bytes 1544 | tf_op jit(solution)/shard_map/ppermute | solution.py:31
  28.1 36.7 %all-to-all-start = ((f16[16,288,128]{2,1,0:T(8,128)(2,1)}), f16[16,288,128]{2,1,0:T(8,128)(2,1)S(1)}, u32[]{:S(2)}, u32[]{:S(2)}) async-start(f16[16,288,128]{2,1,0:T(8,128)(2,1)} %convert_element_type.6), calls=%async_computation | async-start | bytes 2359296 | tf_op jit(solution)/shard_map/all_to_all | solution.py:596
  34.4 3.7 %collective-permute-start.5 = (f32[4,128]{1,0:T(4,128)S(1)}, f32[4,128]{1,0:T(4,128)S(1)}, u32[]{:S(2)}, u32[]{:S(2)}) collective-permute-start(f32[4,128]{1,0:T(4,128)S(1)} %dynamic_update_slice.33), channel_id=1, source_target_pairs={{0,16},{16,0},{1,17},{17,1},{2,18},{18,2},{3,19},{19,3},{4,20},{20... | collective-permute-start | bytes 6152 | tf_op jit(solution)/shard_map/ppermute | solution.py:31
  38.1 6.6 %collective-permute-start.8 = (f32[4,256]{1,0:T(4,128)S(1)}, f32[4,256]{1,0:T(4,128)S(1)}, u32[]{:S(2)}, u32[]{:S(2)}) collective-permute-start(f32[4,256]{1,0:T(4,128)S(1)} %constant_dynamic-update-slice_fusion.4), channel_id=1, source_target_pairs={{0,12},{4,0},{8,4},{12,8},{1,13},{5,1},{9,5},{13,9},{2,14},{6,2},{... | collective-permute-start | bytes 12296 | tf_op jit(solution)/shard_map/ppermute | solution.py:31
  38.8 5.9 %collective-permute-start.7 = (f32[4,256]{1,0:T(4,128)S(1)}, f32[4,256]{1,0:T(4,128)S(1)}, u32[]{:S(2)}, u32[]{:S(2)}) collective-permute-start(f32[4,256]{1,0:T(4,128)S(1)} %constant_dynamic-update-slice_fusion.4), channel_id=1, source_target_pairs={{0,8},{4,12},{8,0},{12,4},{1,9},{5,13},{9,1},{13,5},{2,10},{6,14},... | collective-permute-start | bytes 12296 | tf_op jit(solution)/shard_map/ppermute | solution.py:31
  39.9 3.8 %collective-permute-start.6 = (f32[4,256]{1,0:T(4,128)S(1)}, f32[4,256]{1,0:T(4,128)S(1)}, u32[]{:S(2)}, u32[]{:S(2)}) collective-permute-start(f32[4,256]{1,0:T(4,128)S(1)} %constant_dynamic-update-slice_fusion.4), channel_id=1, source_target_pairs={{0,4},{4,8},{8,12},{12,0},{1,5},{5,9},{9,13},{13,1},{2,6},{6,10},{... | collective-permute-start | bytes 12296 | tf_op jit(solution)/shard_map/ppermute | solution.py:31
  44.7 0.6 copy-start.5

commit v7 on v6

--- a/solution.py
+++ b/solution.py
@@ -133,21 +133,30 @@
             ]
 
 
-def rims_kernel(ghosts_hbm, rims_hbm, ghosts_ref, rims_ref, got, sent):
-    species, slots, _ = ghosts_ref.shape
-
-    def fetch(s):
-        return pltpu.make_async_copy(ghosts_hbm.at[s], ghosts_ref.at[s], got.at[s])
+def lefts_kernel(
+    fields_hbm, ghosts_hbm, lefts_hbm, fields_ref, ghosts_ref, lefts_ref, got, sent
+):
+    species, slots, _ = fields_ref.shape
+
+    def fetches(s):
+        return (
+            pltpu.make_async_copy(ghosts_hbm.at[s], ghosts_ref.at[s], got.at[0, s]),
+            pltpu.make_async_copy(fields_hbm.at[s], fields_ref.at[s], got.at[1, s]),
+        )
 
     def store(s):
-        return pltpu.make_async_copy(rims_ref.at[s], rims_hbm.at[s], sent.at[s])
+        return pltpu.make_async_copy(lefts_ref.at[s], lefts_hbm.at[:, :, s], sent.at[s])
 
     for s in range(species):
-        fetch(s).start()
+        for copy in fetches(s):
+            copy.start()
     quarter = lax.broadcasted_iota(jnp.int32, (slots, LANES), 1) // (2 * TE)
+    parity = lax.broadcasted_iota(jnp.int32, (slots, FACE), 1) // TE % 2
+    masks = [jnp.where(parity == p, 1.0, 0.0).astype(jnp.bfloat16) for p in range(2)]
 
     def one(s, carry):
-        fetch(s).wait()
+        for copy in fetches(s):
+            copy.wait()
         for block in range(2):
             faces = [
                 ghosts_ref[s, :, w * FACE + block * LANES : w * FACE + (block + 1) * LANES]
@@ -160,9 +169,15 @@
                     rim = turned if n == 0 else jnp.where(quarter == n, turned, rim)
                 high = rim.astype(jnp.bfloat16)
                 low = (rim - high.astype(jnp.float32)).astype(jnp.bfloat16)
-                start = (block * 4 + q) * 2 * LANES
-                rims_ref[s, :, start : start + LANES] = high
-                rims_ref[s, :, start + LANES : start + 2 * LANES] = low
+                rim = jnp.concatenate([high, low], axis=1)
+                pair = block * 4 + q
+                for p in range(2):
+                    f = fields_ref[s, :, (2 * pair + p) * FACE : (2 * pair + p + 1) * FACE]
+                    high = f.astype(jnp.bfloat16)
+                    low = (f - high.astype(jnp.float32)).astype(jnp.bfloat16)
+                    lefts_ref[s, pair, p, :, 0:FACE] = high
+                    lefts_ref[s, pair, p, :, FACE : 2 * FACE] = low
+                    lefts_ref[s, pair, p, :, 2 * FACE :] = rim * masks[p]
         store(s).start()
         return carry
 
@@ -200,23 +215,20 @@
     weights_hbm,
     fields_hbm,
     ghosts_hbm,
-    rims_hbm,
+    lefts_hbm,
     recent_hbm,
     older_hbm,
     new_fields_hbm,
     new_tend_hbm,
     weights_ref,
     fields_ref,
-    rims_ref,
+    lefts_ref,
     recent_ref,
     older_ref,
     new_fields_ref,
     new_tend_ref,
     mix_ref,
     wide_ref,
-    mask_ref,
-    left_even_ref,
-    left_odd_ref,
     fuel_even_ref,
     fuel_odd_ref,
     sums_even_ref,
@@ -237,13 +249,13 @@
         return pl.ds(pl.multiple_of(skipped + c * length, LANES), length)
 
     def cells_in(c):
-        lanes, rims, inner = span(c, chunk), span(c, chunk // 2), span(c, chunk, FACE)
+        lanes, inner, pairs = span(c, chunk), span(c, chunk, FACE), pl.ds(c * PLANES // 2, PLANES // 2)
         return (
             pltpu.make_async_copy(
                 fields_hbm.at[:, :, lanes], fields_ref.at[:, :, inner], got.at[0, c]
             ),
             pltpu.make_async_copy(
-                rims_hbm.at[:, :, rims], rims_ref.at[:, :, rims], got.at[1, c]
+                lefts_hbm.at[pairs], lefts_ref.at[pairs], got.at[1, c]
             ),
             pltpu.make_async_copy(
                 recent_hbm.at[:, :, lanes], recent_ref.at[:, :, lanes], got.at[2, c]
@@ -326,32 +338,17 @@
     for fuel_ref in (fuel_even_ref, fuel_odd_ref):
         fuel_ref[3 * main + 3 * slots :, :] = jnp.zeros((LANES - 3 * slots, 2 * FACE), jnp.bfloat16)
 
-    parity = lax.broadcasted_iota(jnp.int32, (slots, 2 * LANES), 1) // TE % 2
-    for p in range(2):
-        mask_ref[p] = jnp.where(parity == p, 1.0, 0.0).astype(jnp.bfloat16)
     slot = lax.broadcasted_iota(jnp.int32, (slots, slots), 0)
     keep = (destination_ref[...] == lax.axis_index(TEAM)) & (target_ref[...] == slot)
     keep = keep.astype(jnp.bfloat16)
 
-    def build(pair, odd, some):
-        left_ref = (left_even_ref, left_odd_ref)[odd]
-        rims = pl.ds(pl.multiple_of(pair * FACE, FACE), FACE)
-        for s in some:
-            both = rims_ref[s, :, rims]
-            for p in range(2):
-                lanes = pl.ds(pl.multiple_of((2 * pair + p + 1) * FACE, FACE), FACE)
-                rows = slice((p * species + s) * slots, (p * species + s + 1) * slots)
-                f = fields_ref[s, :, lanes]
-                high = f.astype(jnp.bfloat16)
-                left_ref[rows, 0:FACE] = high
-                left_ref[rows, FACE : 2 * FACE] = (f - high.astype(jnp.float32)).astype(jnp.bfloat16)
-                left_ref[rows, 2 * FACE :] = both * mask_ref[p]
-
     def multiply(pair, odd, d):
-        left_ref, sums_ref = ((left_even_ref, sums_even_ref), (left_odd_ref, sums_odd_ref))[odd]
+        sums_ref = (sums_even_ref, sums_odd_ref)[odd]
         columns = slice(d * FACE, (d + 1) * FACE)
         sums_ref[:, columns] = jnp.dot(
-            left_ref[...], weights_ref[:, columns], preferred_element_type=jnp.float32
+            lefts_ref[pair].reshape(sums_ref.shape[0], 6 * LANES),
+            weights_ref[:, columns],
+            preferred_element_type=jnp.float32,
         )
 
     def burn(pair, odd):
@@ -406,20 +403,17 @@
     pairs = TE // 2
 
     def stage(pair, odd):
-        after, later = jnp.minimum(pair + 1, pairs - 1), jnp.minimum(pair + 2, pairs - 1)
+        after = jnp.minimum(pair + 1, pairs - 1)
         burn(after, 1 - odd)
         for d, some in enumerate(thirds):
             multiply(after, 1 - odd, d)
             finish(pair, odd, some)
-            build(later, odd, some)
 
     for copy in (*ends(), *cells_in(0)):
         copy.wait()
-    build(0, 0, range(species))
     for d in range(3):
         multiply(0, 0, d)
     burn(0, 0)
-    build(1, 1, range(species))
 
     def four(c, carry):
         @pl.when(c + 2 < chunks)
@@ -427,12 +421,13 @@
             for copy in cells_in(c + 2):
                 copy.start()
 
+        stage(2 * c, 0)
+
         @pl.when(c + 1 < chunks)
         def _():
             for copy in cells_in(c + 1):
                 copy.wait()
 
-        stage(2 * c, 0)
         stage(2 * c + 1, 1)
         for copy in stores(c):
             copy.start()
@@ -561,23 +556,25 @@
     outgoing = outgoing.astype(jnp.float16)
 
     shape = jax.ShapeDtypeStruct((species, slots, cells), jnp.float32)
-    rims = jax.ShapeDtypeStruct((species, slots, TE * LANES), jnp.bfloat16)
-    rims = pl.pallas_call(
-        rims_kernel,
-        name="rims",
-        out_shape=rims,
-        in_specs=[anywhere],
+    lefts = (TE // 2, 2, species, slots, 6 * LANES)
+    lefts = jax.ShapeDtypeStruct(lefts, jnp.bfloat16)
+    lefts = pl.pallas_call(
+        lefts_kernel,
+        name="left_sides",
+        out_shape=lefts,
+        in_specs=[anywhere, anywhere],
         out_specs=anywhere,
         scratch_shapes=[
+            pltpu.VMEM(shape.shape, jnp.float32),
             pltpu.VMEM(ghosts.shape, jnp.float32),
-            pltpu.VMEM(rims.shape, jnp.bfloat16),
-            pltpu.SemaphoreType.DMA((species,)),
+            pltpu.VMEM((species, TE // 2, 2, slots, 6 * LANES), jnp.bfloat16),
+            pltpu.SemaphoreType.DMA((2, species)),
             pltpu.SemaphoreType.DMA((species,)),
         ],
         compiler_params=params(58),
-        cost_estimate=pl.CostEstimate(flops=0, bytes_accessed=8 << 20, transcendentals=0),
-    )(ghosts)
-    below, above, rims, outgoing = lax.optimization_barrier((below, above, rims, outgoing))
+        cost_estimate=pl.CostEstimate(flops=0, bytes_accessed=12 << 20, transcendentals=0),
+    )(fields, ghosts)
+    below, above, lefts, outgoing = lax.optimization_barrier((below, above, lefts, outgoing))
 
     filtered, row = pl.pallas_call(
         filter_kernel,
@@ -598,7 +595,6 @@
     arrived = arrived.astype(jnp.float32)
 
     weights = jnp.asarray(plane_weights(), jnp.bfloat16)
-    left = pltpu.VMEM((2 * species * slots, 6 * LANES), jnp.bfloat16)
     sums = pltpu.VMEM((2 * species * slots, 3 * FACE), jnp.float32)
     depth = 3 * (species - 1) * slots + LANES
     fuel = pltpu.VMEM((depth, 2 * FACE), jnp.bfloat16)
@@ -613,16 +609,13 @@
         scratch_shapes=[
             pltpu.VMEM(weights.shape, jnp.bfloat16),
             pltpu.VMEM((species, slots, cells + 2 * FACE), jnp.float32),
-            pltpu.VMEM(rims.shape, jnp.bfloat16),
+            pltpu.VMEM(lefts.shape, jnp.bfloat16),
             pltpu.VMEM(shape.shape, jnp.bfloat16),
             pltpu.VMEM(shape.shape, jnp.bfloat16),
             pltpu.VMEM(shape.shape, jnp.float32),
             pltpu.VMEM(shape.shape, jnp.bfloat16),
             pltpu.VMEM((species * slots, depth), jnp.bfloat16),
             pltpu.VMEM((6, slots, LANES), jnp.float32),
-            pltpu.VMEM((2, slots, FACE), jnp.bfloat16),
-            left,
-            left,
             fuel,
             fuel,
             sums,
@@ -646,7 +639,7 @@
         weights,
         fields,
         ghosts,
-        rims,
+        lefts,
         recent,
         older,
     )

time: 73.3 us -> 76.9 us (1.049)
  Pallas kernels: 37.3 us -> 43.3 us
  waiting for transfers between devices: 12 us -> 10.2 us
  starting transfers between devices: 18.2 us -> 17 us
    pallas_call x1, Pallas kernels: 19.4 us -> 22.9 us  [local(): pl.pallas_call(main_kernel, name='updates', out_shape=(shape, jax.ShapeDt...]
    pallas_call x1, Pallas kernels: 3.31 us -> 5.84 us  [local(): pl.pallas_call(lefts_kernel, name='left_sides', out_shape=lefts, in_specs...]
    ppermute x9, waiting for transfers between devices: 12 us -> 10.2 us  [passed_along(): return lax.ppermute(x, axis, [(i, (i + by) % peers) for i in range(peers)])]
    all_to_all x1, starting transfers between devices: 5.54 us -> 4.11 us  [local(): lax.all_to_all(outgoing, TEAM, split_axis=0, concat_axis=0, tiled=True)]
  transfers between devices with their start and end apart: 10 -> 10, of which waited for: 6 -> 7; matrix products, arithmetic and copies ran while one was open for 2% -> 2% of each run, Pallas kernels for 37% -> 43%
where the time goes in v7:
time: 76.9 us; the launch traced here: 76.5 us
  Pallas kernels  43.3 us (56%)
  starting transfers between devices  17 us (22%)
  waiting for transfers between devices  10.2 us (13%)
  other arithmetic  2.83 us (4%)
  between operations  1.65 us (2%)
  local copies, waits for them, and re-layouts  1.45 us (2%)
    pallas_call x1, Pallas kernels, local(): pl.pallas_call(main_kernel, name='updates', out_shape=(shape, jax.ShapeDt...  22.9 us
    ppermute x9, starting transfers between devices, passed_along(): return lax.ppermute(x, axis, [(i, (i + by) % peers) for i in range(peers)])  12.9 us
    ppermute x9, waiting for transfers between devices, passed_along(): return lax.ppermute(x, axis, [(i, (i + by) % peers) for i in range(peers)])  10.2 us
    pallas_call x1, Pallas kernels, local(): pl.pallas_call(add_kernel, name='arrived_histories', out_shape=shape, in_...  6.23 us
    pallas_call x1, Pallas kernels, local(): pl.pallas_call(lefts_kernel, name='left_sides', out_shape=lefts, in_specs...  5.84 us
    pallas_call x1, Pallas kernels, local(): pl.pallas_call(send_kernel, name='outgoing_histories', out_shape=jax.Shap...  4.37 us
    all_to_all x1, starting transfers between devices, local(): lax.all_to_all(outgoing, TEAM, split_axis=0, concat_axis=0, tiled=True)  4.11 us
    pallas_call x1, Pallas kernels, local(): pl.pallas_call(filter_kernel, name='filtered_sensor', out_shape=(jax.Shap...  2.17 us
  transfers between devices with their start and end apart: 10, of which 7 were waited for; matrix products, arithmetic and copies ran while one was open for 2% of the time, Pallas kernels for 43%

profile of v7, /device:TPU:0, one launch (start us, length us, event | category | flops | bytes accessed | tf_op | source)
XLA Modules:
  0.0 76.5 jit_solution(10737533876930631948)
XLA Ops:
  0.6 1.8 %raw_sensor.1 = bf16[32,4096]{1,0:T(8,128)(2,1)} custom-call(s32[2,16]{1,0:T(2,128)} %flags_ref.3, f32[32,4096]{1,0:T(8,128)} %sensor_ref.3), custom_call_target="tpu_custom_call" | custom-call | tf_op jit(solution)/shard_map/raw_sensor/pallas_call | solution.py:528
  2.4 5.0 %collective-permute-start.1 = (bf16[32,4096]{1,0:T(8,128)(2,1)}, bf16[32,4096]{1,0:T(8,128)(2,1)S(1)}, u32[]{:S(2)}, u32[]{:S(2)}) collective-permute-start(bf16[32,4096]{1,0:T(8,128)(2,1)} %raw_sensor.1), channel_id=1, source_target_pairs={{0,3},{1,0},{2,1},{3,2},{4,7},{5,4},{6,5},{7,6},{8,11},{9,8},{10,9... | collective-permute-start | bytes 786440 | tf_op jit(solution)/shard_map/ppermute | solution.py:31
  7.5 0.7 copy-done.2
  8.1 4.4 %outgoing_histories.1 = f32[16,288,128]{2,1,0:T(8,128)S(1)} custom-call(s32[1,32]{1,0:T(1,128)S(1)} %bitcast.10, bf16[9,32,4096]{2,1,0:T(8,128)(2,1)} %bitcast.16, bf16[9,32,4096]{2,1,0:T(8,128)(2,1)} %bitcast.18), custom_call_target="tpu_custom_call" | custom-call | bytes 8388608 | tf_op jit(solution)/shard_map/outgoing_histories/pallas_call | solution.py:542
  12.5 1.2 %convert_element_type.6 = f16[16,288,128]{2,1,0:T(8,128)(2,1)} convert(f32[16,288,128]{2,1,0:T(8,128)S(1)} %outgoing_histories.1) | non-fusion elementwise | flops 589824 | bytes 3538944 | tf_op jit(solution)/shard_map/convert_element_type | solution.py:556
  13.7 5.8 %left_sides.1.lefts_hbm = bf16[8,2,9,32,768]{4,3,2,1,0:T(8,128)(2,1)} custom-call(f32[9,32,4096]{2,1,0:T(8,128)} %bitcast.14, f32[9,32,1536]{2,1,0:T(8,128)} %bitcast.20), custom_call_target="tpu_custom_call" | custom-call | bytes 12582912 | tf_op jit(solution)/shard_map/left_sides/pallas_call | solution.py:561
  19.8 2.2 %filtered_sensor.1 = (f32[32,4096]{1,0:T(8,128)}, f32[1,128]{1,0:T(1,128)S(1)}) custom-call(s32[2,16]{1,0:T(2,128)S(1)} %copy-done.4, f32[32,96]{1,0:T(8,128)S(1)} %copy-done.1, f32[32,4096]{1,0:T(8,128)S(1)} %copy-done, bf16[32,4096]{1,0:T(8,128)(2,1)S(1)} %collective-permute-done.below_ref, bf16[32,4096]{1,0:T(8,128)(2,1)S(1)} %collective-permute-done.1.above_ref, ...), custom_call_target="tpu_custom_call" | custom-call | bytes 4194304 | tf_op jit(solution)/shard_map/filtered_sensor/pallas_call | solution.py:579
  22.0 1.6 %collective-permute-start.2 = (f32[1,128]{1,0:T(1,128)S(1)}, f32[1,128]{1,0:T(1,128)S(1)}, u32[]{:S(2)}, u32[]{:S(2)}) collective-permute-start(f32[1,128]{1,0:T(1,128)S(1)} %get-tuple-element.15), channel_id=1, source_target_pairs={{0,1},{1,2},{2,3},{3,0},{4,5},{5,6},{6,7},{7,4},{8,9},{9,10},{10,1... | collective-permute-start | bytes 1544 | tf_op jit(solution)/shard_map/ppermute | solution.py:31
  23.6 2.6 %collective-permute-start.3 = (f32[1,128]{1,0:T(1,128)S(1)}, f32[1,128]{1,0:T(1,128)S(1)}, u32[]{:S(2)}, u32[]{:S(2)}) collective-permute-start(f32[1,128]{1,0:T(1,128)S(1)} %get-tuple-element.15), channel_id=1, source_target_pairs={{0,2},{1,3},{2,0},{3,1},{4,6},{5,7},{6,4},{7,5},{8,10},{9,11},{10,... | collective-permute-start | bytes 1544 | tf_op jit(solution)/shard_map/ppermute | solution.py:31
  26.2 1.1 %collective-permute-done.2 = f32[1,128]{1,0:T(1,128)S(1)} collective-permute-done((f32[1,128]{1,0:T(1,128)S(1)}, f32[1,128]{1,0:T(1,128)S(1)}, u32[]{:S(2)}, u32[]{:S(2)}) %collective-permute-start.2) | collective-permute-done | bytes 544 | tf_op jit(solution)/shard_map/ppermute | solution.py:31
  27.3 0.7 collective-permute-done.3
  28.1 1.7 %collective-permute-done.4 = f32[1,128]{1,0:T(1,128)S(1)} collective-permute-done((f32[1,128]{1,0:T(1,128)S(1)}, f32[1,128]{1,0:T(1,128)S(1)}, u32[]{:S(2)}, u32[]{:S(2)}) %collective-permute-start.4) | collective-permute-done | bytes 544 | tf_op jit(solution)/shard_map/ppermute | solution.py:31
  29.7 4.1 %all-to-all-start = ((f16[16,288,128]{2,1,0:T(8,128)(2,1)}), f16[16,288,128]{2,1,0:T(8,128)(2,1)S(1)}, u32[]{:S(2)}, u32[]{:S(2)}) async-start(f16[16,288,128]{2,1,0:T(8,128)(2,1)} %convert_element_type.6), calls=%async_computation | async-start | bytes 2359296 | tf_op jit(solution)/shard_map/all_to_all | solution.py:593
  34.6 1.6 %collective-permute-start.5 = (f32[4,128]{1,0:T(4,128)S(1)}, f32[4,128]{1,0:T(4,128)S(1)}, u32[]{:S(2)}, u32[]{:S(2)}) collective-permute-start(f32[4,128]{1,0:T(4,128)S(1)} %dynamic_update_slice.33), channel_id=1, source_target_pairs={{0,16},{16,0},{1,17},{17,1},{2,18},{18,2},{3,19},{19,3},{4,20},{20... | collective-permute-start | bytes 6152 | tf_op jit(solution)/shard_map/ppermute | solution.py:31
  36.2 2.1 %collective-permute-done.5 = f32[4,128]{1,0:T(4,128)S(1)} collective-permute-done((f32[4,128]{1,0:T(4,128)S(1)}, f32[4,128]{1,0:T(4,128)S(1)}, u32[]{:S(2)}, u32[]{:S(2)}) %collective-permute-start.5) | collective-permute-done | bytes 2080 | tf_op jit(solution)/shard_map/ppermute | solution.py:31
  38.3 0.7 collective-permute-start.8
  39.0 1.1 %collective-permute-start.7 = (f32[4,256]{1,0:T(4,128)S(1)}, f32[4,256]{1,0:T(4,128)S(1)}, u32[]{:S(2)}, u32[]{:S(2)}) collective-permute-start(f32[4,256]{1,0:T(4,128)S(1)} %constant_dynamic-update-slice_fusion.4), channel_id=1, source_target_pairs={{0,8},{4,12},{8,0},{12,4},{1,9},{5,13},{9,1},{13,5},{2,10},{6,14},... | collective-permute-start | bytes 12296 | tf_op jit(solution)/shard_map/ppermute | solution.py:31
  40.1 0.2 collective-permute-start.6
  40.4 3.5 %collective-permute-done.6 = f32[4,256]{1,0:T(4,128)S(1)} collective-permute-done((f32[4,256]{1,0:T(4,128)S(1)}, f32[4,256]{1,0:T(4,128)S(1)}, u32[]{:S(2)}, u32[]{:S(2)}) %collective-permute-start.6) | collective-permute-done | bytes 4128 | tf_op jit(solution)/shard_map/ppermute | solution.py:31
  43.9 1.0 %collective-permute-done.7 = f32[4,256]{1,0:T(4,128)S(1)} collective-permute-done((f32[4,256]{1,0:T(4,128)S(1)}, f32[4,256]{1,0:T(4,128)S(1)}, u32[]{:S(2)}, u32[]{:S(2)}) %collective-permute-start.7) | collective-permute-done | bytes 4128 | tf_op jit(solution)/shard_map/ppermute | solution.py:31
  44.9 0.6 copy-done.6
  45.5 22.9 %updates.1 = (f32[9,32,4096]{2,1,0:T(8,128)}, bf16[9,32,4096]{2,1,0:T(8,128)(2,1)}) custom-call(s32[1]{0:T(128)S(6)} %copy.27.live_ref, f32[9,9]{1,0:T(8,128)} %rate_ref.1, f32[16,256]{1,0:T(8,128)} %copy-done.6, s32[1,32]{1,0:T(1,128)} %bitcast.23, f32[3,32]{1,0:T(4,128)} %velocity_ref.1, s32[1,32]{1,0:T(1,128)} %bitcast.9, s32[1,32]{1,0:T(1,128)} %bitcast.12, ...), custom_call_target="tpu_custom_call" | custom-call | bytes 41943040 | tf_op jit(solution)/shard_map/updates/pallas_call | solution.py:603
  68.4 1.7 %convert_element_type.7.arrived_hbm = f32[16,288,128]{2,1,0:T(8,128)} convert(f16[16,288,128]{2,1,0:T(8,128)(2,1)S(1)} %all-to-all-done) | non-fusion elementwise | flops 589824 | bytes 3538944 | tf_op jit(solution)/shard_map/convert_element_type | solution.py:595
  70.1 6.2 %arrived_histories.1 = f32[9,32,4096]{2,1,0:T(8,128)} custom-call(s32[1]{0:T(128)S(6)} %copy.27.live_ref, f32[16,256]{1,0:T(8,128)} %copy-done.6, f32[9,32,4096]{2,1,0:T(8,128)} %get-tuple-element.19.fields_hbm, f32[16,288,128]{2,1,0:T(8,128)} %convert_element_type.7.arrived_hbm), custom_call_target="tpu_custom_call" | custom-call | bytes 12582912 | tf_op jit(solution)/shard_map/arrived_histories/pallas_call | solution.py:647
  (31 shorter events, 0.4 us)
Async XLA Ops:
  2.4 17.1 %collective-permute-start.1 = (bf16[32,4096]{1,0:T(8,128)(2,1)}, bf16[32,4096]{1,0:T(8,128)(2,1)S(1)}, u32[]{:S(2)}, u32[]{:S(2)}) collective-permute-start(bf16[32,4096]{1,0:T(8,128)(2,1)} %raw_sensor.1), channel_id=1, source_target_pairs={{0,3},{1,0},{2,1},{3,2},{4,7},{5,4},{6,5},{7,6},{8,11},{9,8},{10,9... | collective-permute-start | bytes 786440 | tf_op jit(solution)/shard_map/ppermute | solution.py:31
  7.5 12.3 %collective-permute-start = (bf16[32,4096]{1,0:T(8,128)(2,1)}, bf16[32,4096]{1,0:T(8,128)(2,1)S(1)}, u32[]{:S(2)}, u32[]{:S(2)}) collective-permute-start(bf16[32,4096]{1,0:T(8,128)(2,1)} %raw_sensor.1), channel_id=1, source_target_pairs={{0,1},{1,2},{2,3},{3,0},{4,5},{5,6},{6,7},{7,4},{8,9},{9,10},{10,1... | collective-permute-start | bytes 786440 | tf_op jit(solution)/shard_map/ppermute | solution.py:31
  7.5 0.7 copy-start.2
  13.7 6.1 %copy-start = (f32[32,4096]{1,0:T(8,128)S(1)}, f32[32,4096]{1,0:T(8,128)}, u32[]{:S(2)}) copy-start(f32[32,4096]{1,0:T(8,128)} %sensor_ref.3) | copy-start | bytes 1572868
  13.7 6.1 %copy-start.1 = (f32[32,96]{1,0:T(8,128)S(1)}, f32[32,96]{1,0:T(8,128)}, u32[]{:S(2)}) copy-start(f32[32,96]{1,0:T(8,128)} %constant.95.clone.weights_ref) | copy-start | bytes 36868
  13.7 6.1 %copy-start.3 = (s32[32]{0:T(128)S(1)}, s32[32]{0:T(128)}, u32[]{:S(2)}) copy-start(s32[32]{0:T(128)} %param.20) | copy-start | bytes 388
  13.7 6.1 %copy-start.4 = (s32[2,16]{1,0:T(2,128)S(1)}, s32[2,16]{1,0:T(2,128)}, u32[]{:S(2)}) copy-start(s32[2,16]{1,0:T(2,128)} %flags_ref.3) | copy-start | bytes 388
  13.7 6.1 %copy-start.5 = (s32[32]{0:T(128)S(1)}, s32[32]{0:T(128)}, u32[]{:S(2)}) copy-start(s32[32]{0:T(128)} %param.21) | copy-start | bytes 388
  22.0 5.3 %collective-permute-start.2 = (f32[1,128]{1,0:T(1,128)S(1)}, f32[1,128]{1,0:T(1,128)S(1)}, u32[]{:S(2)}, u32[]{:S(2)}) collective-permute-start(f32[1,128]{1,0:T(1,128)S(1)} %get-tuple-element.15), channel_id=1, source_target_pairs={{0,1},{1,2},{2,3},{3,0},{4,5},{5,6},{6,7},{7,4},{8,9},{9,10},{10,1... | collective-permute-start | bytes 1544 | tf_op jit(solution)/shard_map/ppermute | solution.py:31
  23.6 4.4 %collective-permute-start.3 = (f32[1,128]{1,0:T(1,128)S(1)}, f32[1,128]{1,0:T(1,128)S(1)}, u32[]{:S(2)}, u32[]{:S(2)}) collective-permute-start(f32[1,128]{1,0:T(1,128)S(1)} %get-tuple-element.15), channel_id=1, source_target_pairs={{0,2},{1,3},{2,0},{3,1},{4,6},{5,7},{6,4},{7,5},{8,10},{9,11},{10,... | collective-permute-start | bytes 1544 | tf_op jit(solution)/shard_map/ppermute | solution.py:31
  26.2 3.5 %collective-permute-start.4 = (f32[1,128]{1,0:T(1,128)S(1)}, f32[1,128]{1,0:T(1,128)S(1)}, u32[]{:S(2)}, u32[]{:S(2)}) collective-permute-start(f32[1,128]{1,0:T(1,128)S(1)} %get-tuple-element.15), channel_id=1, source_target_pairs={{0,3},{1,0},{2,1},{3,2},{4,7},{5,4},{6,5},{7,6},{8,11},{9,8},{10,9... | collective-permute-start | bytes 1544 | tf_op jit(solution)/shard_map/ppermute | solution.py:31
  29.7 38.7 %all-to-all-start = ((f16[16,288,128]{2,1,0:T(8,128)(2,1)}), f16[16,288,128]{2,1,0:T(8,128)(2,1)S(1)}, u32[]{:S(2)}, u32[]{:S(2)}) async-start(f16[16,288,128]{2,1,0:T(8,128)(2,1)} %convert_element_type.6), calls=%async_computation | async-start | bytes 2359296 | tf_op jit(solution)/shard_map/all_to_all | solution.py:593
  34.6 3.7 %collective-permute-start.5 = (f32[4,128]{1,0:T(4,128)S(1)}, f32[4,128]{1,0:T(4,128)S(1)}, u32[]{:S(2)}, u32[]{:S(2)}) collective-permute-start(f32[4,128]{1,0:T(4,128)S(1)} %dynamic_update_slice.33), channel_id=1, source_target_pairs={{0,16},{16,0},{1,17},{17,1},{2,18},{18,2},{3,19},{19,3},{4,20},{20... | collective-permute-start | bytes 6152 | tf_op jit(solution)/shard_map/ppermute | solution.py:31
  38.3 6.6 %collective-permute-start.8 = (f32[4,256]{1,0:T(4,128)S(1)}, f32[4,256]{1,0:T(4,128)S(1)}, u32[]{:S(2)}, u32[]{:S(2)}) collective-permute-start(f32[4,256]{1,0:T(4,128)S(1)} %constant_dynamic-update-slice_fusion.4), channel_id=1, source_target_pairs={{0,12},{4,0},{8,4},{12,8},{1,13},{5,1},{9,5},{13,9},{2,14},{6,2},{... | collective-permute-start | bytes 12296 | tf_op jit(solution)/shard_map/ppermute | solution.py:31
  39.0 5.9 %collective-permute-start.7 = (f32[4,256]{1,0:T(4,128)S(1)}, f32[4,256]{1,0:T(4,128)S(1)}, u32[]{:S(2)}, u32[]{:S(2)}) collective-permute-start(f32[4,256]{1,0:T(4,128)S(1)} %constant_dynamic-update-slice_fusion.4), channel_id=1, source_target_pairs={{0,8},{4,12},{8,0},{12,4},{1,9},{5,13},{9,1},{13,5},{2,10},{6,14},... | collective-permute-start | bytes 12296 | tf_op jit(solution)/shard_map/ppermute | solution.py:31
  40.1 3.8 %collective-permute-start.6 = (f32[4,256]{1,0:T(4,128)S(1)}, f32[4,256]{1,0:T(4,128)S(1)}, u32[]{:S(2)}, u32[]{:S(2)}) collective-permute-start(f32[4,256]{1,0:T(4,128)S(1)} %constant_dynamic-update-slice_fusion.4), channel_id=1, source_target_pairs={{0,4},{4,8},{8,12},{12,0},{1,5},{5,9},{9,13},{13,1},{2,6},{6,10},{... | collective-permute-start | bytes 12296 | tf_op jit(solution)/shard_map/ppermute | solution.py:31
  44.9 0.6 copy-start.6

commit v8 on v6

--- a/solution.py
+++ b/solution.py
@@ -42,12 +42,30 @@
     return (weights / total).astype(np.float32)
 
 
-def raw_kernel(flags_ref, sensor_ref, raw_ref):
-    for r in range(TZ):
-        for k in range(TCOL):
-            rows, cols = slice(r * TE, (r + 1) * TE), slice(k * FACE, (k + 1) * FACE)
-            flag = flags_ref[r, k].astype(jnp.float32)
-            raw_ref[rows, cols] = (sensor_ref[rows, cols] * flag).astype(jnp.bfloat16)
+def raw_kernel(flags_ref, sensor_hbm, raw_hbm, sensor_ref, raw_ref, got, sent):
+    parts = got.shape[0]
+    tiles = TCOL // parts
+
+    def fetch(c):
+        columns = pl.ds(c * tiles * FACE, tiles * FACE)
+        return pltpu.make_async_copy(sensor_hbm.at[:, columns], sensor_ref.at[:, columns], got.at[c])
+
+    def store(c):
+        columns = pl.ds(c * tiles * FACE, tiles * FACE)
+        return pltpu.make_async_copy(raw_ref.at[:, columns], raw_hbm.at[:, columns], sent.at[c])
+
+    for c in range(parts):
+        fetch(c).start()
+    for c in range(parts):
+        fetch(c).wait()
+        for r in range(TZ):
+            for k in range(c * tiles, (c + 1) * tiles):
+                rows, cols = slice(r * TE, (r + 1) * TE), slice(k * FACE, (k + 1) * FACE)
+                flag = flags_ref[r, k].astype(jnp.float32)
+                raw_ref[rows, cols] = (sensor_ref[rows, cols] * flag).astype(jnp.bfloat16)
+        store(c).start()
+    for c in range(parts):
+        store(c).wait()
 
 
 def filter_kernel(
@@ -453,7 +471,7 @@
     def fetches(s):
         part = arrived_hbm.at[:, pl.ds(s * ROWS, ROWS)]
         return (
-            pltpu.make_async_copy(part, arrived_ref.at[s], got.at[0, s]),
+            pltpu.make_async_copy(part, arrived_ref.at[s, :, pl.ds(0, ROWS)], got.at[0, s]),
             pltpu.make_async_copy(fields_hbm.at[s], fields_ref.at[s], got.at[1, s]),
         )
 
@@ -480,11 +498,12 @@
                 copy.start()
         for copy in fetches(s):
             copy.wait()
-        flat = arrived_ref.at[s].reshape(peers * ROWS, LANES)
+        apart = arrived_ref.shape[2]
+        flat = arrived_ref.at[s].reshape(peers * apart, LANES)
         for c in range(ROWS // 2):
             lanes = slice(c * 2 * LANES, (c + 1) * 2 * LANES)
             arrived = jnp.concatenate(
-                [flat[pl.ds(2 * c + k, peers, stride=ROWS), :] for k in range(2)], axis=1
+                [flat[pl.ds(2 * c + k, peers, stride=apart), :] for k in range(2)], axis=1
             )
             high = arrived.astype(jnp.bfloat16)
             low = (arrived - high.astype(jnp.float32)).astype(jnp.bfloat16)
@@ -534,8 +553,14 @@
         raw_kernel,
         name="raw_sensor",
         out_shape=jax.ShapeDtypeStruct(sensor.shape, jnp.bfloat16),
-        in_specs=[smem(), pl.BlockSpec(memory_space=pltpu.VMEM)],
-        out_specs=pl.BlockSpec(memory_space=pltpu.VMEM),
+        in_specs=[smem(), pl.BlockSpec(memory_space=pl.ANY)],
+        out_specs=pl.BlockSpec(memory_space=pl.ANY),
+        scratch_shapes=[
+            pltpu.VMEM(sensor.shape, jnp.float32),
+            pltpu.VMEM(sensor.shape, jnp.bfloat16),
+            pltpu.SemaphoreType.DMA((4,)),
+            pltpu.SemaphoreType.DMA((4,)),
+        ],
         compiler_params=params(58),
     )(flame_flags, sensor)
     below = passed_along(raw, "pen", 1)
@@ -591,10 +616,10 @@
         compiler_params=params(32),
         cost_estimate=pl.CostEstimate(flops=0, bytes_accessed=4 << 20, transcendentals=0),
     )(flame_flags, jnp.asarray(banded(brick, brick)), sensor, below, above, *moves)
-    rows = gathered(row, ("pen",))
+    rows = stacked(row)
     rows, outgoing = lax.optimization_barrier((rows, outgoing))
     arrived = lax.all_to_all(outgoing, TEAM, split_axis=0, concat_axis=0, tiled=True)
-    table = gathered(rows, ("grp", "mig"))
+    table = spread(rows)
     arrived = arrived.astype(jnp.float32)
 
     weights = jnp.asarray(plane_weights(), jnp.bfloat16)
@@ -659,7 +684,7 @@
         out_specs=anywhere,
         scratch_shapes=[
             pltpu.VMEM(shape.shape, jnp.float32),
-            pltpu.VMEM((species, peers, ROWS, LANES), jnp.float32),
+            pltpu.VMEM((species, peers, ROWS + 8, LANES), jnp.float32),
             pltpu.SemaphoreType.DMA((2, species)),
             pltpu.SemaphoreType.DMA((species,)),
         ],
@@ -669,22 +694,33 @@
     return new_fields.transpose(1, 0, 2), new_tend.transpose(1, 0, 2), filtered
 
 
-def gathered(row, axes):
-    for axis in axes:
-        count = lax.axis_size(axis)
-        here = lax.axis_index(axis)
-        rows = [row] + [passed_along(row, axis, by) for by in range(1, count)]
-        height, width = row.shape
-        if axis == "grp":
-            table = jnp.zeros((height, count * width), row.dtype)
-        else:
-            table = jnp.zeros((count * height, width), row.dtype)
-        for by, part in enumerate(rows):
-            place = (here - by) % count
-            place = (0, place * width) if axis == "grp" else (place * height, 0)
+def stacked(row):
+    count, here = lax.axis_size("pen"), lax.axis_index("pen")
+    table = jnp.zeros((count, row.shape[1]), row.dtype)
+    for by in range(count):
+        part = row if by == 0 else passed_along(row, "pen", by)
+        table = lax.dynamic_update_slice(table, part, ((here - by) % count, 0))
+    return table
+
+
+def spread(rows):
+    groups, migs = lax.axis_size("grp"), lax.axis_size("mig")
+    group, mig = lax.axis_index("grp"), lax.axis_index("mig")
+    height, width = rows.shape
+    table = jnp.zeros((migs * height, groups * width), rows.dtype)
+    for by_group in range(groups):
+        for by_mig in range(migs):
+            part = rows
+            if by_group + by_mig > 0:
+                pairs = [
+                    (g * migs + m, (g + by_group) % groups * migs + (m + by_mig) % migs)
+                    for g in range(groups)
+                    for m in range(migs)
+                ]
+                part = lax.ppermute(rows, ("grp", "mig"), pairs)
+            place = ((mig - by_mig) % migs * height, (group - by_group) % groups * width)
             table = lax.dynamic_update_slice(table, part, place)
-        row = table
-    return row
+    return table
 
 
 def solution(mesh):

time: 73.3 us -> 79.7 us (1.087)
  local copies, waits for them, and re-layouts: 0.81 us -> 3.74 us
  starting transfers between devices: 18.2 us -> 21.1 us
    ppermute x9 -> x5, waiting for transfers between devices: 12 us -> 5.34 us  [passed_along(): return lax.ppermute(x, axis, [(i, (i + by) % peers) for i in range(peers)])]
    ppermute x0 -> x7, waiting for transfers between devices: none -> 6.49 us  [spread(): part = lax.ppermute(rows, ('grp', 'mig'), pairs)]
    ppermute x0 -> x7, starting transfers between devices: none -> 6.44 us  [spread(): part = lax.ppermute(rows, ('grp', 'mig'), pairs)]
    ppermute x9 -> x5, starting transfers between devices: 12.7 us -> 9.09 us  [passed_along(): return lax.ppermute(x, axis, [(i, (i + by) % peers) for i in range(peers)])]
    dynamic_update_slice x10 -> x12, local copies, waits for them, and re-layouts: 0.18 us -> 3.11 us  [the longest x8 2.98 us: spread(): table = lax.dynamic_update_slice(table, part, place)]
    pallas_call x1, Pallas kernels: 1.79 us -> 2.63 us  [local(): pl.pallas_call(raw_kernel, name='raw_sensor', out_shape=jax.ShapeDtypeStr...]
  transfers between devices with their start and end apart: 10 -> 13, of which waited for: 6 -> 5; matrix products, arithmetic and copies ran while one was open for 2% -> 5% of each run, Pallas kernels for 37% -> 34%
where the time goes in v8:
time: 79.7 us; the launch traced here: 79.3 us
  Pallas kernels  38 us (48%)
  starting transfers between devices  21.1 us (26%)
  waiting for transfers between devices  11.8 us (15%)
  local copies, waits for them, and re-layouts  3.74 us (5%)
  other arithmetic  2.89 us (4%)
  between operations  1.72 us (2%)
    pallas_call x1, Pallas kernels, local(): pl.pallas_call(main_kernel, name='updates', out_shape=(shape, jax.ShapeDt...  19.5 us
    ppermute x5, starting transfers between devices, passed_along(): return lax.ppermute(x, axis, [(i, (i + by) % peers) for i in range(peers)])  9.09 us
    ppermute x7, waiting for transfers between devices, spread(): part = lax.ppermute(rows, ('grp', 'mig'), pairs)  6.49 us
    ppermute x7, starting transfers between devices, spread(): part = lax.ppermute(rows, ('grp', 'mig'), pairs)  6.44 us
    pallas_call x1, Pallas kernels, local(): pl.pallas_call(add_kernel, name='arrived_histories', out_shape=shape, in_...  6.1 us
    all_to_all x1, starting transfers between devices, local(): lax.all_to_all(outgoing, TEAM, split_axis=0, concat_axis=0, tiled=True)  5.54 us
    ppermute x5, waiting for transfers between devices, passed_along(): return lax.ppermute(x, axis, [(i, (i + by) % peers) for i in range(peers)])  5.34 us
    pallas_call x1, Pallas kernels, local(): pl.pallas_call(send_kernel, name='outgoing_histories', out_shape=jax.Shap...  4.37 us
  transfers between devices with their start and end apart: 13, of which 5 were waited for; matrix products, arithmetic and copies ran while one was open for 5% of the time, Pallas kernels for 34%

profile of v8, /device:TPU:0, one launch (start us, length us, event | category | flops | bytes accessed | tf_op | source)
XLA Modules:
  0.0 79.3 jit_solution(1966478982547372844)
XLA Ops:
  0.6 2.6 %raw_sensor.1 = bf16[32,4096]{1,0:T(8,128)(2,1)} custom-call(s32[2,16]{1,0:T(2,128)} %flags_ref.3, f32[32,4096]{1,0:T(8,128)} %sensor_ref.1), custom_call_target="tpu_custom_call" | custom-call | tf_op jit(solution)/shard_map/raw_sensor/pallas_call | solution.py:552
  3.3 5.1 %collective-permute-start.1 = (bf16[32,4096]{1,0:T(8,128)(2,1)}, bf16[32,4096]{1,0:T(8,128)(2,1)S(1)}, u32[]{:S(2)}, u32[]{:S(2)}) collective-permute-start(bf16[32,4096]{1,0:T(8,128)(2,1)} %raw_sensor.1), channel_id=1, source_target_pairs={{0,3},{1,0},{2,1},{3,2},{4,7},{5,4},{6,5},{7,6},{8,11},{9,8},{10,9... | collective-permute-start | bytes 786440 | tf_op jit(solution)/shard_map/ppermute | solution.py:31
  8.4 3.3 %rims.1.rims_hbm = bf16[9,32,2048]{2,1,0:T(8,128)(2,1)} custom-call(f32[9,32,1536]{2,1,0:T(8,128)} %bitcast.18), custom_call_target="tpu_custom_call" | custom-call | bytes 8388608 | tf_op jit(solution)/shard_map/rims/pallas_call | solution.py:590
  11.7 4.4 %outgoing_histories.1 = f32[16,288,128]{2,1,0:T(8,128)S(1)} custom-call(s32[1,32]{1,0:T(1,128)S(1)} %bitcast.10, bf16[9,32,4096]{2,1,0:T(8,128)(2,1)} %bitcast.14, bf16[9,32,4096]{2,1,0:T(8,128)(2,1)} %bitcast.16), custom_call_target="tpu_custom_call" | custom-call | bytes 8388608 | tf_op jit(solution)/shard_map/outgoing_histories/pallas_call | solution.py:572
  16.1 1.2 %convert_element_type.6 = f16[16,288,128]{2,1,0:T(8,128)(2,1)} convert(f32[16,288,128]{2,1,0:T(8,128)S(1)} %outgoing_histories.1) | non-fusion elementwise | flops 589824 | bytes 3538944 | tf_op jit(solution)/shard_map/convert_element_type | solution.py:586
  17.3 3.3 %collective-permute-done.below_ref = bf16[32,4096]{1,0:T(8,128)(2,1)S(1)} collective-permute-done((bf16[32,4096]{1,0:T(8,128)(2,1)}, bf16[32,4096]{1,0:T(8,128)(2,1)S(1)}, u32[]{:S(2)}, u32[]{:S(2)}) %collective-permute-start) | collective-permute-done | bytes 262176 | tf_op jit(solution)/shard_map/ppermute | solution.py:31
  20.7 2.2 %filtered_sensor.1 = (f32[32,4096]{1,0:T(8,128)}, f32[1,128]{1,0:T(1,128)S(1)}) custom-call(s32[2,16]{1,0:T(2,128)S(1)} %copy-done.3, f32[32,96]{1,0:T(8,128)S(1)} %copy-done.1, f32[32,4096]{1,0:T(8,128)S(1)} %copy-done, bf16[32,4096]{1,0:T(8,128)(2,1)S(1)} %collective-permute-done.below_ref, bf16[32,4096]{1,0:T(8,128)(2,1)S(1)} %collective-permute-done.1.above_ref, ...), custom_call_target="tpu_custom_call" | custom-call | bytes 4194304 | tf_op jit(solution)/shard_map/filtered_sensor/pallas_call | solution.py:607
  22.9 1.6 %collective-permute-start.2 = (f32[1,128]{1,0:T(1,128)S(1)}, f32[1,128]{1,0:T(1,128)S(1)}, u32[]{:S(2)}, u32[]{:S(2)}) collective-permute-start(f32[1,128]{1,0:T(1,128)S(1)} %get-tuple-element.15), channel_id=1, source_target_pairs={{0,1},{1,2},{2,3},{3,0},{4,5},{5,6},{6,7},{7,4},{8,9},{9,10},{10,1... | collective-permute-start | bytes 1544 | tf_op jit(solution)/shard_map/ppermute | solution.py:31
  24.5 0.7 collective-permute-start.3
  25.2 1.7 %collective-permute-start.4 = (f32[1,128]{1,0:T(1,128)S(1)}, f32[1,128]{1,0:T(1,128)S(1)}, u32[]{:S(2)}, u32[]{:S(2)}) collective-permute-start(f32[1,128]{1,0:T(1,128)S(1)} %get-tuple-element.15), channel_id=1, source_target_pairs={{0,3},{1,0},{2,1},{3,2},{4,7},{5,4},{6,5},{7,6},{8,11},{9,8},{10,9... | collective-permute-start | bytes 1544 | tf_op jit(solution)/shard_map/ppermute | solution.py:31
  26.9 1.3 %collective-permute-done.2 = f32[1,128]{1,0:T(1,128)S(1)} collective-permute-done((f32[1,128]{1,0:T(1,128)S(1)}, f32[1,128]{1,0:T(1,128)S(1)}, u32[]{:S(2)}, u32[]{:S(2)}) %collective-permute-start.2) | collective-permute-done | bytes 544 | tf_op jit(solution)/shard_map/ppermute | solution.py:31
  28.2 0.7 collective-permute-done.3
  29.0 5.5 %all-to-all-start = ((f16[16,288,128]{2,1,0:T(8,128)(2,1)}), f16[16,288,128]{2,1,0:T(8,128)(2,1)S(1)}, u32[]{:S(2)}, u32[]{:S(2)}) async-start(f16[16,288,128]{2,1,0:T(8,128)(2,1)} %convert_element_type.6), calls=%async_computation | async-start | bytes 2359296 | tf_op jit(solution)/shard_map/all_to_all | solution.py:621
  34.6 1.9 %collective-permute-start.6 = (f32[4,128]{1,0:T(4,128)S(1)}, f32[4,128]{1,0:T(4,128)S(1)}, u32[]{:S(2)}, u32[]{:S(2)}) collective-permute-start(f32[4,128]{1,0:T(4,128)S(1)} %dynamic_update_slice.39), channel_id=1, source_target_pairs={{0,8},{4,12},{8,0},{12,4},{16,24},{20,28},{24,16},{28,20},{1,9},{5... | collective-permute-start | bytes 6152 | tf_op jit(solution)/shard_map/ppermute | solution.py:720
  36.5 1.7 %collective-permute-start.7 = (f32[4,128]{1,0:T(4,128)S(1)}, f32[4,128]{1,0:T(4,128)S(1)}, u32[]{:S(2)}, u32[]{:S(2)}) collective-permute-start(f32[4,128]{1,0:T(4,128)S(1)} %dynamic_update_slice.39), channel_id=1, source_target_pairs={{0,12},{4,0},{8,4},{12,8},{16,28},{20,16},{24,20},{28,24},{1,13},{... | collective-permute-start | bytes 6152 | tf_op jit(solution)/shard_map/ppermute | solution.py:720
  38.2 1.5 %collective-permute-start.8 = (f32[4,128]{1,0:T(4,128)S(1)}, f32[4,128]{1,0:T(4,128)S(1)}, u32[]{:S(2)}, u32[]{:S(2)}) collective-permute-start(f32[4,128]{1,0:T(4,128)S(1)} %dynamic_update_slice.39), channel_id=1, source_target_pairs={{0,16},{4,20},{8,24},{12,28},{16,0},{20,4},{24,8},{28,12},{1,17},{... | collective-permute-start | bytes 6152 | tf_op jit(solution)/shard_map/ppermute | solution.py:720
  39.7 5.7 %collective-permute-done.6 = f32[4,128]{1,0:T(4,128)S(1)} collective-permute-done((f32[4,128]{1,0:T(4,128)S(1)}, f32[4,128]{1,0:T(4,128)S(1)}, u32[]{:S(2)}, u32[]{:S(2)}) %collective-permute-start.6) | collective-permute-done | bytes 2080 | tf_op jit(solution)/shard_map/ppermute | solution.py:720
  45.4 1.1 %collective-permute-start.10 = (f32[4,128]{1,0:T(4,128)S(1)}, f32[4,128]{1,0:T(4,128)S(1)}, u32[]{:S(2)}, u32[]{:S(2)}) collective-permute-start(f32[4,128]{1,0:T(4,128)S(1)} %dynamic_update_slice.39), channel_id=1, source_target_pairs={{0,24},{4,28},{8,16},{12,20},{16,8},{20,12},{24,0},{28,4},{1,25},{... | collective-permute-start | bytes 6152 | tf_op jit(solution)/shard_map/ppermute | solution.py:720
  48.6 0.5 dynamic_update_slice.43
  49.8 0.8 %collective-permute-done.10 = f32[4,128]{1,0:T(4,128)S(1)} collective-permute-done((f32[4,128]{1,0:T(4,128)S(1)}, f32[4,128]{1,0:T(4,128)S(1)}, u32[]{:S(2)}, u32[]{:S(2)}) %collective-permute-start.10) | collective-permute-done | bytes 2080 | tf_op jit(solution)/shard_map/ppermute | solution.py:720
  51.3 0.6 copy-done.5
  51.9 19.5 %updates.1 = (f32[9,32,4096]{2,1,0:T(8,128)}, bf16[9,32,4096]{2,1,0:T(8,128)(2,1)}) custom-call(s32[1]{0:T(128)S(6)} %copy.29.live_ref, f32[9,9]{1,0:T(8,128)} %rate_ref.1, f32[16,256]{1,0:T(8,128)} %copy-done.5, s32[1,32]{1,0:T(1,128)} %bitcast.22, f32[3,32]{1,0:T(4,128)} %velocity_ref.1, s32[1,32]{1,0:T(1,128)} %bitcast.9, s32[1,32]{1,0:T(1,128)} %bitcast.12, ...), custom_call_target="tpu_custom_call" | custom-call | bytes 41943040 | tf_op jit(solution)/shard_map/updates/pallas_call | solution.py:632
  71.3 1.7 %convert_element_type.7.arrived_hbm = f32[16,288,128]{2,1,0:T(8,128)} convert(f16[16,288,128]{2,1,0:T(8,128)(2,1)S(1)} %all-to-all-done) | non-fusion elementwise | flops 589824 | bytes 3538944 | tf_op jit(solution)/shard_map/convert_element_type | solution.py:623
  73.0 6.1 %arrived_histories.1 = f32[9,32,4096]{2,1,0:T(8,128)} custom-call(s32[1]{0:T(128)S(6)} %copy.29.live_ref, f32[16,256]{1,0:T(8,128)} %copy-done.5, f32[9,32,4096]{2,1,0:T(8,128)} %get-tuple-element.19.fields_hbm, f32[16,288,128]{2,1,0:T(8,128)} %convert_element_type.7.arrived_hbm), custom_call_target="tpu_custom_call" | custom-call | bytes 12582912 | tf_op jit(solution)/shard_map/arrived_histories/pallas_call | solution.py:679
  (36 shorter events, 2.9 us)
Async XLA Ops:
  0.6 11.1 %copy-start.2 = (s32[32]{0:T(128)S(1)}, s32[32]{0:T(128)}, u32[]{:S(2)}) copy-start(s32[32]{0:T(128)} %param.20) | copy-start | bytes 388
  3.3 14.1 %collective-permute-start.1 = (bf16[32,4096]{1,0:T(8,128)(2,1)}, bf16[32,4096]{1,0:T(8,128)(2,1)S(1)}, u32[]{:S(2)}, u32[]{:S(2)}) collective-permute-start(bf16[32,4096]{1,0:T(8,128)(2,1)} %raw_sensor.1), channel_id=1, source_target_pairs={{0,3},{1,0},{2,1},{3,2},{4,7},{5,4},{6,5},{7,6},{8,11},{9,8},{10,9... | collective-permute-start | bytes 786440 | tf_op jit(solution)/shard_map/ppermute | solution.py:31
  8.4 12.3 %collective-permute-start = (bf16[32,4096]{1,0:T(8,128)(2,1)}, bf16[32,4096]{1,0:T(8,128)(2,1)S(1)}, u32[]{:S(2)}, u32[]{:S(2)}) collective-permute-start(bf16[32,4096]{1,0:T(8,128)(2,1)} %raw_sensor.1), channel_id=1, source_target_pairs={{0,1},{1,2},{2,3},{3,0},{4,5},{5,6},{6,7},{7,4},{8,9},{9,10},{10,1... | collective-permute-start | bytes 786440 | tf_op jit(solution)/shard_map/ppermute | solution.py:31
  16.1 4.6 %copy-start = (f32[32,4096]{1,0:T(8,128)S(1)}, f32[32,4096]{1,0:T(8,128)}, u32[]{:S(2)}) copy-start(f32[32,4096]{1,0:T(8,128)} %sensor_ref.1) | copy-start | bytes 1572868
  16.1 4.6 %copy-start.1 = (f32[32,96]{1,0:T(8,128)S(1)}, f32[32,96]{1,0:T(8,128)}, u32[]{:S(2)}) copy-start(f32[32,96]{1,0:T(8,128)} %constant.114.clone.weights_ref) | copy-start | bytes 36868
  16.1 4.6 %copy-start.3 = (s32[2,16]{1,0:T(2,128)S(1)}, s32[2,16]{1,0:T(2,128)}, u32[]{:S(2)}) copy-start(s32[2,16]{1,0:T(2,128)} %flags_ref.3) | copy-start | bytes 388
  16.1 4.6 %copy-start.4 = (s32[32]{0:T(128)S(1)}, s32[32]{0:T(128)}, u32[]{:S(2)}) copy-start(s32[32]{0:T(128)} %param.21) | copy-start | bytes 388
  22.9 5.3 %collective-permute-start.2 = (f32[1,128]{1,0:T(1,128)S(1)}, f32[1,128]{1,0:T(1,128)S(1)}, u32[]{:S(2)}, u32[]{:S(2)}) collective-permute-start(f32[1,128]{1,0:T(1,128)S(1)} %get-tuple-element.15), channel_id=1, source_target_pairs={{0,1},{1,2},{2,3},{3,0},{4,5},{5,6},{6,7},{7,4},{8,9},{9,10},{10,1... | collective-permute-start | bytes 1544 | tf_op jit(solution)/shard_map/ppermute | solution.py:31
  24.5 4.4 %collective-permute-start.3 = (f32[1,128]{1,0:T(1,128)S(1)}, f32[1,128]{1,0:T(1,128)S(1)}, u32[]{:S(2)}, u32[]{:S(2)}) collective-permute-start(f32[1,128]{1,0:T(1,128)S(1)} %get-tuple-element.15), channel_id=1, source_target_pairs={{0,2},{1,3},{2,0},{3,1},{4,6},{5,7},{6,4},{7,5},{8,10},{9,11},{10,... | collective-permute-start | bytes 1544 | tf_op jit(solution)/shard_map/ppermute | solution.py:31
  25.2 3.8 %collective-permute-start.4 = (f32[1,128]{1,0:T(1,128)S(1)}, f32[1,128]{1,0:T(1,128)S(1)}, u32[]{:S(2)}, u32[]{:S(2)}) collective-permute-start(f32[1,128]{1,0:T(1,128)S(1)} %get-tuple-element.15), channel_id=1, source_target_pairs={{0,3},{1,0},{2,1},{3,2},{4,7},{5,4},{6,5},{7,6},{8,11},{9,8},{10,9... | collective-permute-start | bytes 1544 | tf_op jit(solution)/shard_map/ppermute | solution.py:31
  29.0 42.3 %all-to-all-start = ((f16[16,288,128]{2,1,0:T(8,128)(2,1)}), f16[16,288,128]{2,1,0:T(8,128)(2,1)S(1)}, u32[]{:S(2)}, u32[]{:S(2)}) async-start(f16[16,288,128]{2,1,0:T(8,128)(2,1)} %convert_element_type.6), calls=%async_computation | async-start | bytes 2359296 | tf_op jit(solution)/shard_map/all_to_all | solution.py:621
  34.6 10.8 %collective-permute-start.6 = (f32[4,128]{1,0:T(4,128)S(1)}, f32[4,128]{1,0:T(4,128)S(1)}, u32[]{:S(2)}, u32[]{:S(2)}) collective-permute-start(f32[4,128]{1,0:T(4,128)S(1)} %dynamic_update_slice.39), channel_id=1, source_target_pairs={{0,8},{4,12},{8,0},{12,4},{16,24},{20,28},{24,16},{28,20},{1,9},{5... | collective-permute-start | bytes 6152 | tf_op jit(solution)/shard_map/ppermute | solution.py:720
  36.5 10.1 %collective-permute-start.5 = (f32[4,128]{1,0:T(4,128)S(1)}, f32[4,128]{1,0:T(4,128)S(1)}, u32[]{:S(2)}, u32[]{:S(2)}) collective-permute-start(f32[4,128]{1,0:T(4,128)S(1)} %dynamic_update_slice.39), channel_id=1, source_target_pairs={{0,4},{4,8},{8,12},{12,0},{16,20},{20,24},{24,28},{28,16},{1,5},{5... | collective-permute-start | bytes 6152 | tf_op jit(solution)/shard_map/ppermute | solution.py:720
  36.5 12.1 %collective-permute-start.7 = (f32[4,128]{1,0:T(4,128)S(1)}, f32[4,128]{1,0:T(4,128)S(1)}, u32[]{:S(2)}, u32[]{:S(2)}) collective-permute-start(f32[4,128]{1,0:T(4,128)S(1)} %dynamic_update_slice.39), channel_id=1, source_target_pairs={{0,12},{4,0},{8,4},{12,8},{16,28},{20,16},{24,20},{28,24},{1,13},{... | collective-permute-start | bytes 6152 | tf_op jit(solution)/shard_map/ppermute | solution.py:720
  38.2 10.9 %collective-permute-start.8 = (f32[4,128]{1,0:T(4,128)S(1)}, f32[4,128]{1,0:T(4,128)S(1)}, u32[]{:S(2)}, u32[]{:S(2)}) collective-permute-start(f32[4,128]{1,0:T(4,128)S(1)} %dynamic_update_slice.39), channel_id=1, source_target_pairs={{0,16},{4,20},{8,24},{12,28},{16,0},{20,4},{24,8},{28,12},{1,17},{... | collective-permute-start | bytes 6152 | tf_op jit(solution)/shard_map/ppermute | solution.py:720
  39.7 9.7 %collective-permute-start.9 = (f32[4,128]{1,0:T(4,128)S(1)}, f32[4,128]{1,0:T(4,128)S(1)}, u32[]{:S(2)}, u32[]{:S(2)}) collective-permute-start(f32[4,128]{1,0:T(4,128)S(1)} %dynamic_update_slice.39), channel_id=1, source_target_pairs={{0,20},{4,24},{8,28},{12,16},{16,4},{20,8},{24,12},{28,0},{1,21},{... | collective-permute-start | bytes 6152 | tf_op jit(solution)/shard_map/ppermute | solution.py:720
  45.4 5.2 %collective-permute-start.10 = (f32[4,128]{1,0:T(4,128)S(1)}, f32[4,128]{1,0:T(4,128)S(1)}, u32[]{:S(2)}, u32[]{:S(2)}) collective-permute-start(f32[4,128]{1,0:T(4,128)S(1)} %dynamic_update_slice.39), channel_id=1, source_target_pairs={{0,24},{4,28},{8,16},{12,20},{16,8},{20,12},{24,0},{28,4},{1,25},{... | collective-permute-start | bytes 6152 | tf_op jit(solution)/shard_map/ppermute | solution.py:720
  46.5 4.3 %collective-permute-start.11 = (f32[4,128]{1,0:T(4,128)S(1)}, f32[4,128]{1,0:T(4,128)S(1)}, u32[]{:S(2)}, u32[]{:S(2)}) collective-permute-start(f32[4,128]{1,0:T(4,128)S(1)} %dynamic_update_slice.39), channel_id=1, source_target_pairs={{0,28},{4,16},{8,20},{12,24},{16,12},{20,0},{24,4},{28,8},{1,29},{... | collective-permute-start | bytes 6152 | tf_op jit(solution)/shard_map/ppermute | solution.py:720
  51.3 0.6 copy-start.5

commit v9 on v6

--- a/solution.py
+++ b/solution.py
@@ -277,11 +277,8 @@
             ),
         )
 
-    for copy in ends():
+    for copy in (*cells_in(0), *ends(), *cells_in(1)):
         copy.start()
-    for c in range(2):
-        for copy in cells_in(c):
-            copy.start()
 
     marks = jnp.concatenate(
         [velocity_ref[...], tiles_ref[...].astype(jnp.float32), jnp.zeros((4, slots), jnp.float32)], axis=0
@@ -453,7 +450,7 @@
     def fetches(s):
         part = arrived_hbm.at[:, pl.ds(s * ROWS, ROWS)]
         return (
-            pltpu.make_async_copy(part, arrived_ref.at[s], got.at[0, s]),
+            pltpu.make_async_copy(part, arrived_ref.at[s, :, pl.ds(0, ROWS)], got.at[0, s]),
             pltpu.make_async_copy(fields_hbm.at[s], fields_ref.at[s], got.at[1, s]),
         )
 
@@ -480,11 +477,12 @@
                 copy.start()
         for copy in fetches(s):
             copy.wait()
-        flat = arrived_ref.at[s].reshape(peers * ROWS, LANES)
+        apart = arrived_ref.shape[2]
+        flat = arrived_ref.at[s].reshape(peers * apart, LANES)
         for c in range(ROWS // 2):
             lanes = slice(c * 2 * LANES, (c + 1) * 2 * LANES)
             arrived = jnp.concatenate(
-                [flat[pl.ds(2 * c + k, peers, stride=ROWS), :] for k in range(2)], axis=1
+                [flat[pl.ds(2 * c + k, peers, stride=apart), :] for k in range(2)], axis=1
             )
             high = arrived.astype(jnp.bfloat16)
             low = (arrived - high.astype(jnp.float32)).astype(jnp.bfloat16)
@@ -634,7 +632,7 @@
             pltpu.SemaphoreType.DMA((5, TE // PLANES)),
             pltpu.SemaphoreType.DMA((2, TE // PLANES)),
         ],
-        compiler_params=params(58),
+        compiler_params=params(52),
         cost_estimate=pl.CostEstimate(flops=0, bytes_accessed=40 << 20, transcendentals=0),
     )(
         live_counts,
@@ -659,11 +657,11 @@
         out_specs=anywhere,
         scratch_shapes=[
             pltpu.VMEM(shape.shape, jnp.float32),
-            pltpu.VMEM((species, peers, ROWS, LANES), jnp.float32),
+            pltpu.VMEM((species, peers, ROWS + 8, LANES), jnp.float32),
             pltpu.SemaphoreType.DMA((2, species)),
             pltpu.SemaphoreType.DMA((species,)),
         ],
-        compiler_params=params(58),
+        compiler_params=params(50),
         cost_estimate=pl.CostEstimate(flops=0, bytes_accessed=12 << 20, transcendentals=0),
     )(live_counts, table, new_fields, arrived)
     return new_fields.transpose(1, 0, 2), new_tend.transpose(1, 0, 2), filtered

time: 73.3 us -> 69.1 us (0.943)
  Pallas kernels: 37.3 us -> 35.2 us
  other arithmetic: 2.87 us -> 1.43 us
    convert_element_type x1, other arithmetic: 1.68 us -> 0.23 us  [local(): arrived = arrived.astype(jnp.float32)]
    pallas_call x1, Pallas kernels: 6.23 us -> 5.05 us  [local(): pl.pallas_call(add_kernel, name='arrived_histories', out_shape=shape, in_...]
    pallas_call x1, Pallas kernels: 19.4 us -> 18.5 us  [local(): pl.pallas_call(main_kernel, name='updates', out_shape=(shape, jax.ShapeDt...]
  transfers between devices with their start and end apart: 10 -> 10, of which waited for: 6 -> 7; matrix products, arithmetic and copies ran while one was open for 2% -> 2% of each run, Pallas kernels for 37% -> 38%
where the time goes in v9:
time: 69.1 us; the launch traced here: 68.7 us
  Pallas kernels  35.2 us (51%)
  starting transfers between devices  18.2 us (26%)
  waiting for transfers between devices  12.1 us (18%)
  between operations  1.55 us (2%)
  other arithmetic  1.43 us (2%)
    pallas_call x1, Pallas kernels, local(): pl.pallas_call(main_kernel, name='updates', out_shape=(shape, jax.ShapeDt...  18.5 us
    ppermute x9, starting transfers between devices, passed_along(): return lax.ppermute(x, axis, [(i, (i + by) % peers) for i in range(peers)])  12.7 us
    ppermute x9, waiting for transfers between devices, passed_along(): return lax.ppermute(x, axis, [(i, (i + by) % peers) for i in range(peers)])  11.9 us
    all_to_all x1, starting transfers between devices, local(): lax.all_to_all(outgoing, TEAM, split_axis=0, concat_axis=0, tiled=True)  5.54 us
    pallas_call x1, Pallas kernels, local(): pl.pallas_call(add_kernel, name='arrived_histories', out_shape=shape, in_...  5.05 us
    pallas_call x1, Pallas kernels, local(): pl.pallas_call(send_kernel, name='outgoing_histories', out_shape=jax.Shap...  4.37 us
    pallas_call x1, Pallas kernels, local(): pl.pallas_call(rims_kernel, name='rims', out_shape=rims, in_specs=[anywhe...  3.31 us
    pallas_call x1, Pallas kernels, local(): pl.pallas_call(filter_kernel, name='filtered_sensor', out_shape=(jax.Shap...  2.17 us
  transfers between devices with their start and end apart: 10, of which 7 were waited for; matrix products, arithmetic and copies ran while one was open for 2% of the time, Pallas kernels for 38%

profile of v9, /device:TPU:0, one launch (start us, length us, event | category | flops | bytes accessed | tf_op | source)
XLA Modules:
  0.0 68.7 jit_solution(4774121514758915202)
XLA Ops:
  0.6 1.8 %raw_sensor.1 = bf16[32,4096]{1,0:T(8,128)(2,1)} custom-call(s32[2,16]{1,0:T(2,128)} %flags_ref.3, f32[32,4096]{1,0:T(8,128)} %sensor_ref.3), custom_call_target="tpu_custom_call" | custom-call | tf_op jit(solution)/shard_map/raw_sensor/pallas_call | solution.py:531
  2.4 5.0 %collective-permute-start.1 = (bf16[32,4096]{1,0:T(8,128)(2,1)}, bf16[32,4096]{1,0:T(8,128)(2,1)S(1)}, u32[]{:S(2)}, u32[]{:S(2)}) collective-permute-start(bf16[32,4096]{1,0:T(8,128)(2,1)} %raw_sensor.1), channel_id=1, source_target_pairs={{0,3},{1,0},{2,1},{3,2},{4,7},{5,4},{6,5},{7,6},{8,11},{9,8},{10,9... | collective-permute-start | bytes 786440 | tf_op jit(solution)/shard_map/ppermute | solution.py:31
  7.5 3.3 %rims.1.rims_hbm = bf16[9,32,2048]{2,1,0:T(8,128)(2,1)} custom-call(f32[9,32,1536]{2,1,0:T(8,128)} %bitcast.19), custom_call_target="tpu_custom_call" | custom-call | bytes 8388608 | tf_op jit(solution)/shard_map/rims/pallas_call | solution.py:563
  10.8 4.4 %outgoing_histories.1 = f32[16,288,128]{2,1,0:T(8,128)S(1)} custom-call(s32[1,32]{1,0:T(1,128)S(1)} %bitcast.9, bf16[9,32,4096]{2,1,0:T(8,128)(2,1)} %bitcast.15, bf16[9,32,4096]{2,1,0:T(8,128)(2,1)} %bitcast.17), custom_call_target="tpu_custom_call" | custom-call | bytes 8388608 | tf_op jit(solution)/shard_map/outgoing_histories/pallas_call | solution.py:545
  15.2 1.2 %convert_element_type.6 = f16[16,288,128]{2,1,0:T(8,128)(2,1)} convert(f32[16,288,128]{2,1,0:T(8,128)S(1)} %outgoing_histories.1) | non-fusion elementwise | flops 589824 | bytes 3538944 | tf_op jit(solution)/shard_map/convert_element_type | solution.py:559
  16.5 3.3 %collective-permute-done.below_ref = bf16[32,4096]{1,0:T(8,128)(2,1)S(1)} collective-permute-done((bf16[32,4096]{1,0:T(8,128)(2,1)}, bf16[32,4096]{1,0:T(8,128)(2,1)S(1)}, u32[]{:S(2)}, u32[]{:S(2)}) %collective-permute-start) | collective-permute-done | bytes 262176 | tf_op jit(solution)/shard_map/ppermute | solution.py:31
  19.8 2.2 %filtered_sensor.1 = (f32[32,4096]{1,0:T(8,128)}, f32[1,128]{1,0:T(1,128)S(1)}) custom-call(s32[2,16]{1,0:T(2,128)S(1)} %copy-done.5, f32[32,96]{1,0:T(8,128)S(1)} %copy-done.2, f32[32,4096]{1,0:T(8,128)S(1)} %copy-done, bf16[32,4096]{1,0:T(8,128)(2,1)S(1)} %collective-permute-done.below_ref, bf16[32,4096]{1,0:T(8,128)(2,1)S(1)} %collective-permute-done.1.above_ref, ...), custom_call_target="tpu_custom_call" | custom-call | bytes 4194304 | tf_op jit(solution)/shard_map/filtered_sensor/pallas_call | solution.py:580
  22.0 1.6 %collective-permute-start.2 = (f32[1,128]{1,0:T(1,128)S(1)}, f32[1,128]{1,0:T(1,128)S(1)}, u32[]{:S(2)}, u32[]{:S(2)}) collective-permute-start(f32[1,128]{1,0:T(1,128)S(1)} %get-tuple-element.15), channel_id=1, source_target_pairs={{0,1},{1,2},{2,3},{3,0},{4,5},{5,6},{6,7},{7,4},{8,9},{9,10},{10,1... | collective-permute-start | bytes 1544 | tf_op jit(solution)/shard_map/ppermute | solution.py:31
  23.6 0.7 %collective-permute-start.3 = (f32[1,128]{1,0:T(1,128)S(1)}, f32[1,128]{1,0:T(1,128)S(1)}, u32[]{:S(2)}, u32[]{:S(2)}) collective-permute-start(f32[1,128]{1,0:T(1,128)S(1)} %get-tuple-element.15), channel_id=1, source_target_pairs={{0,2},{1,3},{2,0},{3,1},{4,6},{5,7},{6,4},{7,5},{8,10},{9,11},{10,... | collective-permute-start | bytes 1544 | tf_op jit(solution)/shard_map/ppermute | solution.py:31
  24.3 1.7 %collective-permute-start.4 = (f32[1,128]{1,0:T(1,128)S(1)}, f32[1,128]{1,0:T(1,128)S(1)}, u32[]{:S(2)}, u32[]{:S(2)}) collective-permute-start(f32[1,128]{1,0:T(1,128)S(1)} %get-tuple-element.15), channel_id=1, source_target_pairs={{0,3},{1,0},{2,1},{3,2},{4,7},{5,4},{6,5},{7,6},{8,11},{9,8},{10,9... | collective-permute-start | bytes 1544 | tf_op jit(solution)/shard_map/ppermute | solution.py:31
  26.0 1.3 %collective-permute-done.2 = f32[1,128]{1,0:T(1,128)S(1)} collective-permute-done((f32[1,128]{1,0:T(1,128)S(1)}, f32[1,128]{1,0:T(1,128)S(1)}, u32[]{:S(2)}, u32[]{:S(2)}) %collective-permute-start.2) | collective-permute-done | bytes 544 | tf_op jit(solution)/shard_map/ppermute | solution.py:31
  27.3 0.7 %collective-permute-done.3 = f32[1,128]{1,0:T(1,128)S(1)} collective-permute-done((f32[1,128]{1,0:T(1,128)S(1)}, f32[1,128]{1,0:T(1,128)S(1)}, u32[]{:S(2)}, u32[]{:S(2)}) %collective-permute-start.3) | collective-permute-done | bytes 544 | tf_op jit(solution)/shard_map/ppermute | solution.py:31
  28.1 5.5 %all-to-all-start = ((f16[16,288,128]{2,1,0:T(8,128)(2,1)}), f16[16,288,128]{2,1,0:T(8,128)(2,1)S(1)}, u32[]{:S(2)}, u32[]{:S(2)}) async-start(f16[16,288,128]{2,1,0:T(8,128)(2,1)} %convert_element_type.6), calls=%async_computation | async-start | bytes 2359296 | tf_op jit(solution)/shard_map/all_to_all | solution.py:594
  34.4 1.6 %collective-permute-start.5 = (f32[4,128]{1,0:T(4,128)S(1)}, f32[4,128]{1,0:T(4,128)S(1)}, u32[]{:S(2)}, u32[]{:S(2)}) collective-permute-start(f32[4,128]{1,0:T(4,128)S(1)} %dynamic_update_slice.33), channel_id=1, source_target_pairs={{0,16},{16,0},{1,17},{17,1},{2,18},{18,2},{3,19},{19,3},{4,20},{20... | collective-permute-start | bytes 6152 | tf_op jit(solution)/shard_map/ppermute | solution.py:31
  36.0 2.1 %collective-permute-done.5 = f32[4,128]{1,0:T(4,128)S(1)} collective-permute-done((f32[4,128]{1,0:T(4,128)S(1)}, f32[4,128]{1,0:T(4,128)S(1)}, u32[]{:S(2)}, u32[]{:S(2)}) %collective-permute-start.5) | collective-permute-done | bytes 2080 | tf_op jit(solution)/shard_map/ppermute | solution.py:31
  38.1 0.7 %collective-permute-start.8 = (f32[4,256]{1,0:T(4,128)S(1)}, f32[4,256]{1,0:T(4,128)S(1)}, u32[]{:S(2)}, u32[]{:S(2)}) collective-permute-start(f32[4,256]{1,0:T(4,128)S(1)} %constant_dynamic-update-slice_fusion.4), channel_id=1, source_target_pairs={{0,12},{4,0},{8,4},{12,8},{1,13},{5,1},{9,5},{13,9},{2,14},{6,2},{... | collective-permute-start | bytes 12296 | tf_op jit(solution)/shard_map/ppermute | solution.py:31
  38.8 1.1 %collective-permute-start.7 = (f32[4,256]{1,0:T(4,128)S(1)}, f32[4,256]{1,0:T(4,128)S(1)}, u32[]{:S(2)}, u32[]{:S(2)}) collective-permute-start(f32[4,256]{1,0:T(4,128)S(1)} %constant_dynamic-update-slice_fusion.4), channel_id=1, source_target_pairs={{0,8},{4,12},{8,0},{12,4},{1,9},{5,13},{9,1},{13,5},{2,10},{6,14},... | collective-permute-start | bytes 12296 | tf_op jit(solution)/shard_map/ppermute | solution.py:31
  39.9 0.2 collective-permute-start.6
  40.1 3.5 %collective-permute-done.6 = f32[4,256]{1,0:T(4,128)S(1)} collective-permute-done((f32[4,256]{1,0:T(4,128)S(1)}, f32[4,256]{1,0:T(4,128)S(1)}, u32[]{:S(2)}, u32[]{:S(2)}) %collective-permute-start.6) | collective-permute-done | bytes 4128 | tf_op jit(solution)/shard_map/ppermute | solution.py:31
  43.7 1.0 %collective-permute-done.7 = f32[4,256]{1,0:T(4,128)S(1)} collective-permute-done((f32[4,256]{1,0:T(4,128)S(1)}, f32[4,256]{1,0:T(4,128)S(1)}, u32[]{:S(2)}, u32[]{:S(2)}) %collective-permute-start.7) | collective-permute-done | bytes 4128 | tf_op jit(solution)/shard_map/ppermute | solution.py:31
  44.7 18.5 %updates.1 = (f32[9,32,4096]{2,1,0:T(8,128)}, bf16[9,32,4096]{2,1,0:T(8,128)(2,1)}) custom-call(s32[1]{0:T(128)S(6)} %copy.27.live_ref, f32[9,9]{1,0:T(8,128)S(1)} %copy-done.3, f32[16,256]{1,0:T(8,128)S(1)} %constant_dynamic-update-slice_fusion.table_ref, s32[1,32]{1,0:T(1,128)S(1)} %bitcast.14, f32[3,32]{1,0:T(4,128)S(1)} %copy-done.7, ...), custom_call_target="tpu_custom_call" | custom-call | bytes 41943040 | tf_op jit(solution)/shard_map/updates/pallas_call | solution.py:605
  63.2 0.2 all-to-all-done
  63.4 0.2 convert_element_type.7.arrived_hbm
  63.7 5.1 %arrived_histories.1 = f32[9,32,4096]{2,1,0:T(8,128)} custom-call(s32[1]{0:T(128)S(6)} %copy.27.live_ref, f32[16,256]{1,0:T(8,128)S(1)} %constant_dynamic-update-slice_fusion.table_ref, f32[9,32,4096]{2,1,0:T(8,128)} %get-tuple-element.19.fields_hbm, f32[16,288,128]{2,1,0:T(8,128)S(1)} %convert_element_type.7.arrived_hbm), custom_call_target="tpu_custom_call" | custom-call | bytes 12582912 | tf_op jit(solution)/shard_map/arrived_histories/pallas_call | solution.py:652
  (35 shorter events, 0.2 us)
Async XLA Ops:
  0.6 10.2 %copy-start.4 = (s32[32]{0:T(128)S(1)}, s32[32]{0:T(128)}, u32[]{:S(2)}) copy-start(s32[32]{0:T(128)} %param.20) | copy-start | bytes 388
  2.4 14.0 %collective-permute-start.1 = (bf16[32,4096]{1,0:T(8,128)(2,1)}, bf16[32,4096]{1,0:T(8,128)(2,1)S(1)}, u32[]{:S(2)}, u32[]{:S(2)}) collective-permute-start(bf16[32,4096]{1,0:T(8,128)(2,1)} %raw_sensor.1), channel_id=1, source_target_pairs={{0,3},{1,0},{2,1},{3,2},{4,7},{5,4},{6,5},{7,6},{8,11},{9,8},{10,9... | collective-permute-start | bytes 786440 | tf_op jit(solution)/shard_map/ppermute | solution.py:31
  7.5 12.3 %collective-permute-start = (bf16[32,4096]{1,0:T(8,128)(2,1)}, bf16[32,4096]{1,0:T(8,128)(2,1)S(1)}, u32[]{:S(2)}, u32[]{:S(2)}) collective-permute-start(bf16[32,4096]{1,0:T(8,128)(2,1)} %raw_sensor.1), channel_id=1, source_target_pairs={{0,1},{1,2},{2,3},{3,0},{4,5},{5,6},{6,7},{7,4},{8,9},{9,10},{10,1... | collective-permute-start | bytes 786440 | tf_op jit(solution)/shard_map/ppermute | solution.py:31
  15.2 4.6 %copy-start = (f32[32,4096]{1,0:T(8,128)S(1)}, f32[32,4096]{1,0:T(8,128)}, u32[]{:S(2)}) copy-start(f32[32,4096]{1,0:T(8,128)} %sensor_ref.3) | copy-start | bytes 1572868
  15.2 4.6 %copy-start.2 = (f32[32,96]{1,0:T(8,128)S(1)}, f32[32,96]{1,0:T(8,128)}, u32[]{:S(2)}) copy-start(f32[32,96]{1,0:T(8,128)} %constant.95.clone.weights_ref) | copy-start | bytes 36868
  15.2 4.6 %copy-start.5 = (s32[2,16]{1,0:T(2,128)S(1)}, s32[2,16]{1,0:T(2,128)}, u32[]{:S(2)}) copy-start(s32[2,16]{1,0:T(2,128)} %flags_ref.3) | copy-start | bytes 388
  15.2 4.6 %copy-start.6 = (s32[32]{0:T(128)S(1)}, s32[32]{0:T(128)}, u32[]{:S(2)}) copy-start(s32[32]{0:T(128)} %param.21) | copy-start | bytes 388
  16.4 28.3 %copy-start.1 = (bf16[768,768]{1,0:T(8,128)(2,1)S(1)}, bf16[768,768]{1,0:T(8,128)(2,1)}, u32[]{:S(2)}) copy-start(bf16[768,768]{1,0:T(8,128)(2,1)} %constant.96.clone.weights_hbm) | copy-start | bytes 3538948
  16.4 28.3 %copy-start.3 = (f32[9,9]{1,0:T(8,128)S(1)}, f32[9,9]{1,0:T(8,128)}, u32[]{:S(2)}) copy-start(f32[9,9]{1,0:T(8,128)} %rate_ref.1) | copy-start | bytes 976
  16.5 28.3 %copy-start.7 = (f32[3,32]{1,0:T(4,128)S(1)}, f32[3,32]{1,0:T(4,128)}, u32[]{:S(2)}) copy-start(f32[3,32]{1,0:T(4,128)} %velocity_ref.1) | copy-start | bytes 1156
  16.5 28.3 %copy-start.8 = (s32[32]{0:T(128)S(1)}, s32[32]{0:T(128)}, u32[]{:S(2)}) copy-start(s32[32]{0:T(128)} %param.23) | copy-start | bytes 388
  22.0 5.3 %collective-permute-start.2 = (f32[1,128]{1,0:T(1,128)S(1)}, f32[1,128]{1,0:T(1,128)S(1)}, u32[]{:S(2)}, u32[]{:S(2)}) collective-permute-start(f32[1,128]{1,0:T(1,128)S(1)} %get-tuple-element.15), channel_id=1, source_target_pairs={{0,1},{1,2},{2,3},{3,0},{4,5},{5,6},{6,7},{7,4},{8,9},{9,10},{10,1... | collective-permute-start | bytes 1544 | tf_op jit(solution)/shard_map/ppermute | solution.py:31
  23.6 4.4 %collective-permute-start.3 = (f32[1,128]{1,0:T(1,128)S(1)}, f32[1,128]{1,0:T(1,128)S(1)}, u32[]{:S(2)}, u32[]{:S(2)}) collective-permute-start(f32[1,128]{1,0:T(1,128)S(1)} %get-tuple-element.15), channel_id=1, source_target_pairs={{0,2},{1,3},{2,0},{3,1},{4,6},{5,7},{6,4},{7,5},{8,10},{9,11},{10,... | collective-permute-start | bytes 1544 | tf_op jit(solution)/shard_map/ppermute | solution.py:31
  24.3 3.8 %collective-permute-start.4 = (f32[1,128]{1,0:T(1,128)S(1)}, f32[1,128]{1,0:T(1,128)S(1)}, u32[]{:S(2)}, u32[]{:S(2)}) collective-permute-start(f32[1,128]{1,0:T(1,128)S(1)} %get-tuple-element.15), channel_id=1, source_target_pairs={{0,3},{1,0},{2,1},{3,2},{4,7},{5,4},{6,5},{7,6},{8,11},{9,8},{10,9... | collective-permute-start | bytes 1544 | tf_op jit(solution)/shard_map/ppermute | solution.py:31
  28.1 35.3 %all-to-all-start = ((f16[16,288,128]{2,1,0:T(8,128)(2,1)}), f16[16,288,128]{2,1,0:T(8,128)(2,1)S(1)}, u32[]{:S(2)}, u32[]{:S(2)}) async-start(f16[16,288,128]{2,1,0:T(8,128)(2,1)} %convert_element_type.6), calls=%async_computation | async-start | bytes 2359296 | tf_op jit(solution)/shard_map/all_to_all | solution.py:594
  34.4 3.7 %collective-permute-start.5 = (f32[4,128]{1,0:T(4,128)S(1)}, f32[4,128]{1,0:T(4,128)S(1)}, u32[]{:S(2)}, u32[]{:S(2)}) collective-permute-start(f32[4,128]{1,0:T(4,128)S(1)} %dynamic_update_slice.33), channel_id=1, source_target_pairs={{0,16},{16,0},{1,17},{17,1},{2,18},{18,2},{3,19},{19,3},{4,20},{20... | collective-permute-start | bytes 6152 | tf_op jit(solution)/shard_map/ppermute | solution.py:31
  38.1 6.6 %collective-permute-start.8 = (f32[4,256]{1,0:T(4,128)S(1)}, f32[4,256]{1,0:T(4,128)S(1)}, u32[]{:S(2)}, u32[]{:S(2)}) collective-permute-start(f32[4,256]{1,0:T(4,128)S(1)} %constant_dynamic-update-slice_fusion.4), channel_id=1, source_target_pairs={{0,12},{4,0},{8,4},{12,8},{1,13},{5,1},{9,5},{13,9},{2,14},{6,2},{... | collective-permute-start | bytes 12296 | tf_op jit(solution)/shard_map/ppermute | solution.py:31
  38.8 5.9 %collective-permute-start.7 = (f32[4,256]{1,0:T(4,128)S(1)}, f32[4,256]{1,0:T(4,128)S(1)}, u32[]{:S(2)}, u32[]{:S(2)}) collective-permute-start(f32[4,256]{1,0:T(4,128)S(1)} %constant_dynamic-update-slice_fusion.4), channel_id=1, source_target_pairs={{0,8},{4,12},{8,0},{12,4},{1,9},{5,13},{9,1},{13,5},{2,10},{6,14},... | collective-permute-start | bytes 12296 | tf_op jit(solution)/shard_map/ppermute | solution.py:31
  39.9 3.8 %collective-permute-start.6 = (f32[4,256]{1,0:T(4,128)S(1)}, f32[4,256]{1,0:T(4,128)S(1)}, u32[]{:S(2)}, u32[]{:S(2)}) collective-permute-start(f32[4,256]{1,0:T(4,128)S(1)} %constant_dynamic-update-slice_fusion.4), channel_id=1, source_target_pairs={{0,4},{4,8},{8,12},{12,0},{1,5},{5,9},{9,13},{13,1},{2,6},{6,10},{... | collective-permute-start | bytes 12296 | tf_op jit(solution)/shard_map/ppermute | solution.py:31

commit v10 on v9

--- a/solution.py
+++ b/solution.py
@@ -632,7 +632,7 @@
             pltpu.SemaphoreType.DMA((5, TE // PLANES)),
             pltpu.SemaphoreType.DMA((2, TE // PLANES)),
         ],
-        compiler_params=params(52),
+        compiler_params=params(47),
         cost_estimate=pl.CostEstimate(flops=0, bytes_accessed=40 << 20, transcendentals=0),
     )(
         live_counts,

time: 69.1 us -> 76.9 us (1.11)
  local copies, waits for them, and re-layouts: 0.23 us -> 6.9 us
  other arithmetic: 1.43 us -> 2.67 us
    unnamed x18 -> x28, local copies, waits for them, and re-layouts: 0.04 us -> 6.12 us
    convert_element_type x1, other arithmetic: 0.23 us -> 1.5 us  [local(): arrived = arrived.astype(jnp.float32)]
  transfers between devices with their start and end apart: 10 -> 10, of which waited for: 7 -> 5; matrix products, arithmetic and copies ran while one was open for 2% -> 3% of each run, Pallas kernels for 38% -> 34%
where the time goes in v10:
time: 76.9 us; the launch traced here: 76.3 us
  Pallas kernels  35.4 us (46%)
  starting transfers between devices  18.2 us (24%)
  waiting for transfers between devices  11.5 us (15%)
  local copies, waits for them, and re-layouts  6.9 us (9%)
  other arithmetic  2.67 us (3%)
  between operations  1.54 us (2%)
    pallas_call x1, Pallas kernels, local(): pl.pallas_call(main_kernel, name='updates', out_shape=(shape, jax.ShapeDt...  18.3 us
    ppermute x9, starting transfers between devices, passed_along(): return lax.ppermute(x, axis, [(i, (i + by) % peers) for i in range(peers)])  12.6 us
    ppermute x9, waiting for transfers between devices, passed_along(): return lax.ppermute(x, axis, [(i, (i + by) % peers) for i in range(peers)])  11.5 us
    unnamed x28, local copies, waits for them, and re-layouts  6.12 us
    all_to_all x1, starting transfers between devices, local(): lax.all_to_all(outgoing, TEAM, split_axis=0, concat_axis=0, tiled=True)  5.57 us
    pallas_call x1, Pallas kernels, local(): pl.pallas_call(add_kernel, name='arrived_histories', out_shape=shape, in_...  5.06 us
    pallas_call x1, Pallas kernels, local(): pl.pallas_call(send_kernel, name='outgoing_histories', out_shape=jax.Shap...  4.37 us
    pallas_call x1, Pallas kernels, local(): pl.pallas_call(rims_kernel, name='rims', out_shape=rims, in_specs=[anywhe...  3.31 us
  transfers between devices with their start and end apart: 10, of which 5 were waited for; matrix products, arithmetic and copies ran while one was open for 3% of the time, Pallas kernels for 34%

profile of v10, /device:TPU:0, one launch (start us, length us, event | category | flops | bytes accessed | tf_op | source)
XLA Modules:
  0.0 76.3 jit_solution(1506838141555256281)
XLA Ops:
  0.6 1.8 %raw_sensor.1 = bf16[32,4096]{1,0:T(8,128)(2,1)} custom-call(s32[2,16]{1,0:T(2,128)} %flags_ref.3, f32[32,4096]{1,0:T(8,128)} %sensor_ref.3), custom_call_target="tpu_custom_call" | custom-call | tf_op jit(solution)/shard_map/raw_sensor/pallas_call | solution.py:531
  2.4 5.0 %collective-permute-start.1 = (bf16[32,4096]{1,0:T(8,128)(2,1)}, bf16[32,4096]{1,0:T(8,128)(2,1)}, u32[]{:S(2)}, u32[]{:S(2)}) collective-permute-start(bf16[32,4096]{1,0:T(8,128)(2,1)} %raw_sensor.1), channel_id=1, source_target_pairs={{0,3},{1,0},{2,1},{3,2},{4,7},{5,4},{6,5},{7,6},{8,11},{9,8},{10,9... | collective-permute-start | bytes 786440 | tf_op jit(solution)/shard_map/ppermute | solution.py:31
  7.5 3.3 %rims.1.rims_hbm = bf16[9,32,2048]{2,1,0:T(8,128)(2,1)} custom-call(f32[9,32,1536]{2,1,0:T(8,128)} %bitcast.11), custom_call_target="tpu_custom_call" | custom-call | bytes 8388608 | tf_op jit(solution)/shard_map/rims/pallas_call | solution.py:563
  10.8 4.4 %outgoing_histories.1 = f32[16,288,128]{2,1,0:T(8,128)S(1)} custom-call(s32[1,32]{1,0:T(1,128)S(1)} %bitcast.13, bf16[9,32,4096]{2,1,0:T(8,128)(2,1)} %bitcast.9, bf16[9,32,4096]{2,1,0:T(8,128)(2,1)} %bitcast.19), custom_call_target="tpu_custom_call" | custom-call | bytes 8388608 | tf_op jit(solution)/shard_map/outgoing_histories/pallas_call | solution.py:545
  15.2 1.2 %convert_element_type.6 = f16[16,288,128]{2,1,0:T(8,128)(2,1)} convert(f32[16,288,128]{2,1,0:T(8,128)S(1)} %outgoing_histories.1) | non-fusion elementwise | flops 589824 | bytes 3538944 | tf_op jit(solution)/shard_map/convert_element_type | solution.py:559
  16.4 3.5 %collective-permute-done.below_ref = bf16[32,4096]{1,0:T(8,128)(2,1)} collective-permute-done((bf16[32,4096]{1,0:T(8,128)(2,1)}, bf16[32,4096]{1,0:T(8,128)(2,1)}, u32[]{:S(2)}, u32[]{:S(2)}) %collective-permute-start) | collective-permute-done | bytes 262176 | tf_op jit(solution)/shard_map/ppermute | solution.py:31
  19.9 2.6 %filtered_sensor.1 = (f32[32,4096]{1,0:T(8,128)}, f32[1,128]{1,0:T(1,128)S(1)}) custom-call(s32[2,16]{1,0:T(2,128)S(1)} %copy-done.9, f32[32,96]{1,0:T(8,128)S(1)} %copy-done.5, f32[32,4096]{1,0:T(8,128)S(1)} %copy-done.3, bf16[32,4096]{1,0:T(8,128)(2,1)} %collective-permute-done.below_ref, bf16[32,4096]{1,0:T(8,128)(2,1)} %collective-permute-done.1.above_ref, ...), custom_call_target="tpu_custom_call" | custom-call | bytes 4194304 | tf_op jit(solution)/shard_map/filtered_sensor/pallas_call | solution.py:580
  22.5 1.6 %collective-permute-start.2 = (f32[1,128]{1,0:T(1,128)S(1)}, f32[1,128]{1,0:T(1,128)}, u32[]{:S(2)}, u32[]{:S(2)}) collective-permute-start(f32[1,128]{1,0:T(1,128)S(1)} %get-tuple-element.15), channel_id=1, source_target_pairs={{0,1},{1,2},{2,3},{3,0},{4,5},{5,6},{6,7},{7,4},{8,9},{9,10},{10,1... | collective-permute-start | bytes 1544 | tf_op jit(solution)/shard_map/ppermute | solution.py:31
  24.2 0.7 collective-permute-start.3
  24.9 1.7 %collective-permute-start.4 = (f32[1,128]{1,0:T(1,128)S(1)}, f32[1,128]{1,0:T(1,128)S(1)}, u32[]{:S(2)}, u32[]{:S(2)}) collective-permute-start(f32[1,128]{1,0:T(1,128)S(1)} %get-tuple-element.15), channel_id=1, source_target_pairs={{0,3},{1,0},{2,1},{3,2},{4,7},{5,4},{6,5},{7,6},{8,11},{9,8},{10,9... | collective-permute-start | bytes 1544 | tf_op jit(solution)/shard_map/ppermute | solution.py:31
  26.6 1.4 %collective-permute-done.2 = f32[1,128]{1,0:T(1,128)} collective-permute-done((f32[1,128]{1,0:T(1,128)S(1)}, f32[1,128]{1,0:T(1,128)}, u32[]{:S(2)}, u32[]{:S(2)}) %collective-permute-start.2) | collective-permute-done | bytes 544 | tf_op jit(solution)/shard_map/ppermute | solution.py:31
  28.7 5.6 %all-to-all-start = ((f16[16,288,128]{2,1,0:T(8,128)(2,1)}), f16[16,288,128]{2,1,0:T(8,128)(2,1)}, u32[]{:S(2)}, u32[]{:S(2)}) async-start(f16[16,288,128]{2,1,0:T(8,128)(2,1)} %convert_element_type.6), calls=%async_computation | async-start | bytes 2359296 | tf_op jit(solution)/shard_map/all_to_all | solution.py:594
  35.0 1.6 %collective-permute-start.5 = (f32[4,128]{1,0:T(4,128)S(1)}, f32[4,128]{1,0:T(4,128)S(1)}, u32[]{:S(2)}, u32[]{:S(2)}) collective-permute-start(f32[4,128]{1,0:T(4,128)S(1)} %dynamic_update_slice.33), channel_id=1, source_target_pairs={{0,16},{16,0},{1,17},{17,1},{2,18},{18,2},{3,19},{19,3},{4,20},{20... | collective-permute-start | bytes 6152 | tf_op jit(solution)/shard_map/ppermute | solution.py:31
  36.6 2.1 %collective-permute-done.5 = f32[4,128]{1,0:T(4,128)S(1)} collective-permute-done((f32[4,128]{1,0:T(4,128)S(1)}, f32[4,128]{1,0:T(4,128)S(1)}, u32[]{:S(2)}, u32[]{:S(2)}) %collective-permute-start.5) | collective-permute-done | bytes 2080 | tf_op jit(solution)/shard_map/ppermute | solution.py:31
  38.7 0.8 %collective-permute-start.8 = (f32[4,256]{1,0:T(4,128)S(1)}, f32[4,256]{1,0:T(4,128)S(1)}, u32[]{:S(2)}, u32[]{:S(2)}) collective-permute-start(f32[4,256]{1,0:T(4,128)S(1)} %constant_dynamic-update-slice_fusion.4), channel_id=1, source_target_pairs={{0,12},{4,0},{8,4},{12,8},{1,13},{5,1},{9,5},{13,9},{2,14},{6,2},{... | collective-permute-start | bytes 12296 | tf_op jit(solution)/shard_map/ppermute | solution.py:31
  39.5 1.0 %collective-permute-start.7 = (f32[4,256]{1,0:T(4,128)S(1)}, f32[4,256]{1,0:T(4,128)S(1)}, u32[]{:S(2)}, u32[]{:S(2)}) collective-permute-start(f32[4,256]{1,0:T(4,128)S(1)} %constant_dynamic-update-slice_fusion.4), channel_id=1, source_target_pairs={{0,8},{4,12},{8,0},{12,4},{1,9},{5,13},{9,1},{13,5},{2,10},{6,14},... | collective-permute-start | bytes 12296 | tf_op jit(solution)/shard_map/ppermute | solution.py:31
  40.7 3.5 %collective-permute-done.6 = f32[4,256]{1,0:T(4,128)S(1)} collective-permute-done((f32[4,256]{1,0:T(4,128)S(1)}, f32[4,256]{1,0:T(4,128)S(1)}, u32[]{:S(2)}, u32[]{:S(2)}) %collective-permute-start.6) | collective-permute-done | bytes 4128 | tf_op jit(solution)/shard_map/ppermute | solution.py:31
  44.3 1.0 %collective-permute-done.7 = f32[4,256]{1,0:T(4,128)S(1)} collective-permute-done((f32[4,256]{1,0:T(4,128)S(1)}, f32[4,256]{1,0:T(4,128)S(1)}, u32[]{:S(2)}, u32[]{:S(2)}) %collective-permute-start.7) | collective-permute-done | bytes 4128 | tf_op jit(solution)/shard_map/ppermute | solution.py:31
  45.3 1.5 %copy-done.1 = f32[32,9,1536]{2,0,1:T(8,128)S(1)} copy-done((f32[32,9,1536]{2,0,1:T(8,128)S(1)}, f32[32,9,1536]{2,0,1:T(8,128)}, u32[]{:S(2)}) %copy-start.1) | copy-done | bytes 1769496
  46.8 1.3 %copy-done.4 = bf16[768,768]{1,0:T(8,128)(2,1)S(1)} copy-done((bf16[768,768]{1,0:T(8,128)(2,1)S(1)}, bf16[768,768]{1,0:T(8,128)(2,1)}, u32[]{:S(2)}) %copy-start.4) | copy-done | bytes 1179672
  48.1 0.7 copy-done.6
  51.4 18.3 %updates.1 = (f32[9,32,4096]{2,1,0:T(8,128)}, bf16[9,32,4096]{2,1,0:T(8,128)(2,1)}) custom-call(s32[1]{0:T(128)S(6)} %copy.27.live_ref, f32[9,9]{1,0:T(8,128)S(1)} %copy-done.6, f32[16,256]{1,0:T(8,128)S(1)} %constant_dynamic-update-slice_fusion.table_ref, s32[1,32]{1,0:T(1,128)S(1)} %bitcast.18, f32[3,32]{1,0:T(4,128)S(1)} %copy-done.12, ...), custom_call_target="tpu_custom_call" | custom-call | bytes 41943040 | tf_op jit(solution)/shard_map/updates/pallas_call | solution.py:605
  69.7 1.5 %convert_element_type.7.arrived_hbm = f32[16,288,128]{2,1,0:T(8,128)S(1)} convert(f16[16,288,128]{2,1,0:T(8,128)(2,1)} %all-to-all-done) | non-fusion elementwise | flops 589824 | bytes 3538944 | tf_op jit(solution)/shard_map/convert_element_type | solution.py:596
  71.2 5.1 %arrived_histories.1 = f32[9,32,4096]{2,1,0:T(8,128)} custom-call(s32[1]{0:T(128)S(6)} %copy.27.live_ref, f32[16,256]{1,0:T(8,128)S(1)} %constant_dynamic-update-slice_fusion.table_ref, f32[9,32,4096]{2,1,0:T(8,128)} %get-tuple-element.19.fields_hbm, f32[16,288,128]{2,1,0:T(8,128)S(1)} %convert_element_type.7.arrived_hbm), custom_call_target="tpu_custom_call" | custom-call | bytes 12582912 | tf_op jit(solution)/shard_map/arrived_histories/pallas_call | solution.py:652
  (45 shorter events, 3.7 us)
Async XLA Ops:
  0.6 10.2 %copy-start.7 = (s32[32]{0:T(128)S(1)}, s32[32]{0:T(128)}, u32[]{:S(2)}) copy-start(s32[32]{0:T(128)} %param.20) | copy-start | bytes 388
  2.4 14.0 %collective-permute-start.1 = (bf16[32,4096]{1,0:T(8,128)(2,1)}, bf16[32,4096]{1,0:T(8,128)(2,1)}, u32[]{:S(2)}, u32[]{:S(2)}) collective-permute-start(bf16[32,4096]{1,0:T(8,128)(2,1)} %raw_sensor.1), channel_id=1, source_target_pairs={{0,3},{1,0},{2,1},{3,2},{4,7},{5,4},{6,5},{7,6},{8,11},{9,8},{10,9... | collective-permute-start | bytes 786440 | tf_op jit(solution)/shard_map/ppermute | solution.py:31
  7.5 12.4 %collective-permute-start = (bf16[32,4096]{1,0:T(8,128)(2,1)}, bf16[32,4096]{1,0:T(8,128)(2,1)}, u32[]{:S(2)}, u32[]{:S(2)}) collective-permute-start(bf16[32,4096]{1,0:T(8,128)(2,1)} %raw_sensor.1), channel_id=1, source_target_pairs={{0,1},{1,2},{2,3},{3,0},{4,5},{5,6},{6,7},{7,4},{8,9},{9,10},{10,1... | collective-permute-start | bytes 786440 | tf_op jit(solution)/shard_map/ppermute | solution.py:31
  15.2 4.7 %copy-start.3 = (f32[32,4096]{1,0:T(8,128)S(1)}, f32[32,4096]{1,0:T(8,128)}, u32[]{:S(2)}) copy-start(f32[32,4096]{1,0:T(8,128)} %sensor_ref.3) | copy-start | bytes 1572868
  15.2 4.7 %copy-start.5 = (f32[32,96]{1,0:T(8,128)S(1)}, f32[32,96]{1,0:T(8,128)}, u32[]{:S(2)}) copy-start(f32[32,96]{1,0:T(8,128)} %constant.95.clone.weights_ref) | copy-start | bytes 36868
  15.2 4.7 %copy-start.9 = (s32[2,16]{1,0:T(2,128)S(1)}, s32[2,16]{1,0:T(2,128)}, u32[]{:S(2)}) copy-start(s32[2,16]{1,0:T(2,128)} %flags_ref.3) | copy-start | bytes 388
  15.2 4.7 %copy-start.10 = (s32[32]{0:T(128)S(1)}, s32[32]{0:T(128)}, u32[]{:S(2)}) copy-start(s32[32]{0:T(128)} %param.21) | copy-start | bytes 388
  16.4 28.9 %copy-start = (bf16[32,9,4096]{2,0,1:T(8,128)(2,1)S(1)}, bf16[32,9,4096]{2,0,1:T(8,128)(2,1)}, u32[]{:S(2)}) copy-start(bf16[32,9,4096]{2,0,1:T(8,128)(2,1)} %param.18) | copy-start | bytes 7077892
  16.4 28.9 %copy-start.2 = (bf16[9,32,2048]{2,1,0:T(8,128)(2,1)S(1)}, bf16[9,32,2048]{2,1,0:T(8,128)(2,1)}, u32[]{:S(2)}) copy-start(bf16[9,32,2048]{2,1,0:T(8,128)(2,1)} %rims.1.rims_hbm) | copy-start | bytes 3538948
  22.5 5.4 %collective-permute-start.2 = (f32[1,128]{1,0:T(1,128)S(1)}, f32[1,128]{1,0:T(1,128)}, u32[]{:S(2)}, u32[]{:S(2)}) collective-permute-start(f32[1,128]{1,0:T(1,128)S(1)} %get-tuple-element.15), channel_id=1, source_target_pairs={{0,1},{1,2},{2,3},{3,0},{4,5},{5,6},{6,7},{7,4},{8,9},{9,10},{10,1... | collective-permute-start | bytes 1544 | tf_op jit(solution)/shard_map/ppermute | solution.py:31
  24.2 4.5 %collective-permute-start.3 = (f32[1,128]{1,0:T(1,128)S(1)}, f32[1,128]{1,0:T(1,128)S(1)}, u32[]{:S(2)}, u32[]{:S(2)}) collective-permute-start(f32[1,128]{1,0:T(1,128)S(1)} %get-tuple-element.15), channel_id=1, source_target_pairs={{0,2},{1,3},{2,0},{3,1},{4,6},{5,7},{6,4},{7,5},{8,10},{9,11},{10,... | collective-permute-start | bytes 1544 | tf_op jit(solution)/shard_map/ppermute | solution.py:31
  24.9 3.8 %collective-permute-start.4 = (f32[1,128]{1,0:T(1,128)S(1)}, f32[1,128]{1,0:T(1,128)S(1)}, u32[]{:S(2)}, u32[]{:S(2)}) collective-permute-start(f32[1,128]{1,0:T(1,128)S(1)} %get-tuple-element.15), channel_id=1, source_target_pairs={{0,3},{1,0},{2,1},{3,2},{4,7},{5,4},{6,5},{7,6},{8,11},{9,8},{10,9... | collective-permute-start | bytes 1544 | tf_op jit(solution)/shard_map/ppermute | solution.py:31
  28.7 41.0 %all-to-all-start = ((f16[16,288,128]{2,1,0:T(8,128)(2,1)}), f16[16,288,128]{2,1,0:T(8,128)(2,1)}, u32[]{:S(2)}, u32[]{:S(2)}) async-start(f16[16,288,128]{2,1,0:T(8,128)(2,1)} %convert_element_type.6), calls=%async_computation | async-start | bytes 2359296 | tf_op jit(solution)/shard_map/all_to_all | solution.py:594
  35.0 3.7 %collective-permute-start.5 = (f32[4,128]{1,0:T(4,128)S(1)}, f32[4,128]{1,0:T(4,128)S(1)}, u32[]{:S(2)}, u32[]{:S(2)}) collective-permute-start(f32[4,128]{1,0:T(4,128)S(1)} %dynamic_update_slice.33), channel_id=1, source_target_pairs={{0,16},{16,0},{1,17},{17,1},{2,18},{18,2},{3,19},{19,3},{4,20},{20... | collective-permute-start | bytes 6152 | tf_op jit(solution)/shard_map/ppermute | solution.py:31
  38.7 6.6 %collective-permute-start.8 = (f32[4,256]{1,0:T(4,128)S(1)}, f32[4,256]{1,0:T(4,128)S(1)}, u32[]{:S(2)}, u32[]{:S(2)}) collective-permute-start(f32[4,256]{1,0:T(4,128)S(1)} %constant_dynamic-update-slice_fusion.4), channel_id=1, source_target_pairs={{0,12},{4,0},{8,4},{12,8},{1,13},{5,1},{9,5},{13,9},{2,14},{6,2},{... | collective-permute-start | bytes 12296 | tf_op jit(solution)/shard_map/ppermute | solution.py:31
  39.5 5.8 %collective-permute-start.7 = (f32[4,256]{1,0:T(4,128)S(1)}, f32[4,256]{1,0:T(4,128)S(1)}, u32[]{:S(2)}, u32[]{:S(2)}) collective-permute-start(f32[4,256]{1,0:T(4,128)S(1)} %constant_dynamic-update-slice_fusion.4), channel_id=1, source_target_pairs={{0,8},{4,12},{8,0},{12,4},{1,9},{5,13},{9,1},{13,5},{2,10},{6,14},... | collective-permute-start | bytes 12296 | tf_op jit(solution)/shard_map/ppermute | solution.py:31
  40.5 3.8 %collective-permute-start.6 = (f32[4,256]{1,0:T(4,128)S(1)}, f32[4,256]{1,0:T(4,128)S(1)}, u32[]{:S(2)}, u32[]{:S(2)}) collective-permute-start(f32[4,256]{1,0:T(4,128)S(1)} %constant_dynamic-update-slice_fusion.4), channel_id=1, source_target_pairs={{0,4},{4,8},{8,12},{12,0},{1,5},{5,9},{9,13},{13,1},{2,6},{6,10},{... | collective-permute-start | bytes 12296 | tf_op jit(solution)/shard_map/ppermute | solution.py:31
  45.3 1.5 %copy-start.1 = (f32[32,9,1536]{2,0,1:T(8,128)S(1)}, f32[32,9,1536]{2,0,1:T(8,128)}, u32[]{:S(2)}) copy-start(f32[32,9,1536]{2,0,1:T(8,128)} %param.15) | copy-start | bytes 5308420
  46.8 1.3 %copy-start.4 = (bf16[768,768]{1,0:T(8,128)(2,1)S(1)}, bf16[768,768]{1,0:T(8,128)(2,1)}, u32[]{:S(2)}) copy-start(bf16[768,768]{1,0:T(8,128)(2,1)} %constant.96.clone.weights_hbm) | copy-start | bytes 3538948
  48.1 0.7 copy-start.6
  48.8 0.7 copy-start.8
  49.4 0.7 copy-start.11
  50.1 0.7 copy-start.12
  50.7 0.7 copy-start.13

commit v11 on v9

--- a/solution.py
+++ b/solution.py
@@ -20,7 +20,7 @@
 
 SCALE = 4096.0
 PLANES = 4
-AHEAD = 4
+AHEAD = 9
 
 EVERY = ("grp", "mig", "pen")
 TEAM = ("mig", "pen")
@@ -267,7 +267,7 @@
         )
 
     def stores(c):
-        lanes = span(c, chunk)
+        lanes = span(c, 2 * FACE)
         return (
             pltpu.make_async_copy(
                 new_fields_ref.at[:, :, lanes], new_fields_hbm.at[:, :, lanes], sent.at[0, c]
@@ -430,14 +430,16 @@
                 copy.wait()
 
         stage(2 * c, 0)
+        for copy in stores(2 * c):
+            copy.start()
         stage(2 * c + 1, 1)
-        for copy in stores(c):
+        for copy in stores(2 * c + 1):
             copy.start()
         return carry
 
     lax.fori_loop(0, chunks, four, 0)
-    for c in range(chunks):
-        for copy in stores(c):
+    for pair in range(pairs):
+        for copy in stores(pair):
             copy.wait()
 
 
@@ -630,7 +632,7 @@
             kept,
             kept,
             pltpu.SemaphoreType.DMA((5, TE // PLANES)),
-            pltpu.SemaphoreType.DMA((2, TE // PLANES)),
+            pltpu.SemaphoreType.DMA((2, TE // 2)),
         ],
         compiler_params=params(52),
         cost_estimate=pl.CostEstimate(flops=0, bytes_accessed=40 << 20, transcendentals=0),

time: 69.1 us -> 68 us (0.984)
  Pallas kernels: 35.2 us -> 33.8 us
    pallas_call x1, Pallas kernels: 5.05 us -> 4.04 us  [local(): pl.pallas_call(add_kernel, name='arrived_histories', out_shape=shape, in_...]
where the time goes in v11:
time: 68 us; the launch traced here: 67.7 us
  Pallas kernels  33.8 us (50%)
  starting transfers between devices  18.2 us (27%)
  waiting for transfers between devices  12.5 us (18%)
  between operations  1.55 us (2%)
  other arithmetic  1.43 us (2%)
    pallas_call x1, Pallas kernels, local(): pl.pallas_call(main_kernel, name='updates', out_shape=(shape, jax.ShapeDt...  18.1 us
    ppermute x9, starting transfers between devices, passed_along(): return lax.ppermute(x, axis, [(i, (i + by) % peers) for i in range(peers)])  12.7 us
    ppermute x9, waiting for transfers between devices, passed_along(): return lax.ppermute(x, axis, [(i, (i + by) % peers) for i in range(peers)])  11.9 us
    all_to_all x1, starting transfers between devices, local(): lax.all_to_all(outgoing, TEAM, split_axis=0, concat_axis=0, tiled=True)  5.54 us
    pallas_call x1, Pallas kernels, local(): pl.pallas_call(send_kernel, name='outgoing_histories', out_shape=jax.Shap...  4.37 us
    pallas_call x1, Pallas kernels, local(): pl.pallas_call(add_kernel, name='arrived_histories', out_shape=shape, in_...  4.04 us
    pallas_call x1, Pallas kernels, local(): pl.pallas_call(rims_kernel, name='rims', out_shape=rims, in_specs=[anywhe...  3.31 us
    pallas_call x1, Pallas kernels, local(): pl.pallas_call(filter_kernel, name='filtered_sensor', out_shape=(jax.Shap...  2.17 us
  transfers between devices with their start and end apart: 10, of which 7 were waited for; matrix products, arithmetic and copies ran while one was open for 2% of the time, Pallas kernels for 38%

profile of v11, /device:TPU:0, one launch (start us, length us, event | category | flops | bytes accessed | tf_op | source)
XLA Modules:
  0.0 67.7 jit_solution(17133500604492867733)
XLA Ops:
  0.6 1.8 %raw_sensor.1 = bf16[32,4096]{1,0:T(8,128)(2,1)} custom-call(s32[2,16]{1,0:T(2,128)} %flags_ref.3, f32[32,4096]{1,0:T(8,128)} %sensor_ref.3), custom_call_target="tpu_custom_call" | custom-call | tf_op jit(solution)/shard_map/raw_sensor/pallas_call | solution.py:533
  2.4 5.0 %collective-permute-start.1 = (bf16[32,4096]{1,0:T(8,128)(2,1)}, bf16[32,4096]{1,0:T(8,128)(2,1)S(1)}, u32[]{:S(2)}, u32[]{:S(2)}) collective-permute-start(bf16[32,4096]{1,0:T(8,128)(2,1)} %raw_sensor.1), channel_id=1, source_target_pairs={{0,3},{1,0},{2,1},{3,2},{4,7},{5,4},{6,5},{7,6},{8,11},{9,8},{10,9... | collective-permute-start | bytes 786440 | tf_op jit(solution)/shard_map/ppermute | solution.py:31
  7.5 3.3 %rims.1.rims_hbm = bf16[9,32,2048]{2,1,0:T(8,128)(2,1)} custom-call(f32[9,32,1536]{2,1,0:T(8,128)} %bitcast.19), custom_call_target="tpu_custom_call" | custom-call | bytes 8388608 | tf_op jit(solution)/shard_map/rims/pallas_call | solution.py:565
  10.8 4.4 %outgoing_histories.1 = f32[16,288,128]{2,1,0:T(8,128)S(1)} custom-call(s32[1,32]{1,0:T(1,128)S(1)} %bitcast.9, bf16[9,32,4096]{2,1,0:T(8,128)(2,1)} %bitcast.15, bf16[9,32,4096]{2,1,0:T(8,128)(2,1)} %bitcast.17), custom_call_target="tpu_custom_call" | custom-call | bytes 8388608 | tf_op jit(solution)/shard_map/outgoing_histories/pallas_call | solution.py:547
  15.2 1.2 %convert_element_type.6 = f16[16,288,128]{2,1,0:T(8,128)(2,1)} convert(f32[16,288,128]{2,1,0:T(8,128)S(1)} %outgoing_histories.1) | non-fusion elementwise | flops 589824 | bytes 3538944 | tf_op jit(solution)/shard_map/convert_element_type | solution.py:561
  16.5 3.3 %collective-permute-done.below_ref = bf16[32,4096]{1,0:T(8,128)(2,1)S(1)} collective-permute-done((bf16[32,4096]{1,0:T(8,128)(2,1)}, bf16[32,4096]{1,0:T(8,128)(2,1)S(1)}, u32[]{:S(2)}, u32[]{:S(2)}) %collective-permute-start) | collective-permute-done | bytes 262176 | tf_op jit(solution)/shard_map/ppermute | solution.py:31
  19.8 2.2 %filtered_sensor.1 = (f32[32,4096]{1,0:T(8,128)}, f32[1,128]{1,0:T(1,128)S(1)}) custom-call(s32[2,16]{1,0:T(2,128)S(1)} %copy-done.5, f32[32,96]{1,0:T(8,128)S(1)} %copy-done.2, f32[32,4096]{1,0:T(8,128)S(1)} %copy-done, bf16[32,4096]{1,0:T(8,128)(2,1)S(1)} %collective-permute-done.below_ref, bf16[32,4096]{1,0:T(8,128)(2,1)S(1)} %collective-permute-done.1.above_ref, ...), custom_call_target="tpu_custom_call" | custom-call | bytes 4194304 | tf_op jit(solution)/shard_map/filtered_sensor/pallas_call | solution.py:582
  22.0 1.6 %collective-permute-start.2 = (f32[1,128]{1,0:T(1,128)S(1)}, f32[1,128]{1,0:T(1,128)S(1)}, u32[]{:S(2)}, u32[]{:S(2)}) collective-permute-start(f32[1,128]{1,0:T(1,128)S(1)} %get-tuple-element.15), channel_id=1, source_target_pairs={{0,1},{1,2},{2,3},{3,0},{4,5},{5,6},{6,7},{7,4},{8,9},{9,10},{10,1... | collective-permute-start | bytes 1544 | tf_op jit(solution)/shard_map/ppermute | solution.py:31
  23.6 0.7 %collective-permute-start.3 = (f32[1,128]{1,0:T(1,128)S(1)}, f32[1,128]{1,0:T(1,128)S(1)}, u32[]{:S(2)}, u32[]{:S(2)}) collective-permute-start(f32[1,128]{1,0:T(1,128)S(1)} %get-tuple-element.15), channel_id=1, source_target_pairs={{0,2},{1,3},{2,0},{3,1},{4,6},{5,7},{6,4},{7,5},{8,10},{9,11},{10,... | collective-permute-start | bytes 1544 | tf_op jit(solution)/shard_map/ppermute | solution.py:31
  24.3 1.7 %collective-permute-start.4 = (f32[1,128]{1,0:T(1,128)S(1)}, f32[1,128]{1,0:T(1,128)S(1)}, u32[]{:S(2)}, u32[]{:S(2)}) collective-permute-start(f32[1,128]{1,0:T(1,128)S(1)} %get-tuple-element.15), channel_id=1, source_target_pairs={{0,3},{1,0},{2,1},{3,2},{4,7},{5,4},{6,5},{7,6},{8,11},{9,8},{10,9... | collective-permute-start | bytes 1544 | tf_op jit(solution)/shard_map/ppermute | solution.py:31
  26.0 1.3 %collective-permute-done.2 = f32[1,128]{1,0:T(1,128)S(1)} collective-permute-done((f32[1,128]{1,0:T(1,128)S(1)}, f32[1,128]{1,0:T(1,128)S(1)}, u32[]{:S(2)}, u32[]{:S(2)}) %collective-permute-start.2) | collective-permute-done | bytes 544 | tf_op jit(solution)/shard_map/ppermute | solution.py:31
  27.3 0.7 %collective-permute-done.3 = f32[1,128]{1,0:T(1,128)S(1)} collective-permute-done((f32[1,128]{1,0:T(1,128)S(1)}, f32[1,128]{1,0:T(1,128)S(1)}, u32[]{:S(2)}, u32[]{:S(2)}) %collective-permute-start.3) | collective-permute-done | bytes 544 | tf_op jit(solution)/shard_map/ppermute | solution.py:31
  28.1 5.5 %all-to-all-start = ((f16[16,288,128]{2,1,0:T(8,128)(2,1)}), f16[16,288,128]{2,1,0:T(8,128)(2,1)S(1)}, u32[]{:S(2)}, u32[]{:S(2)}) async-start(f16[16,288,128]{2,1,0:T(8,128)(2,1)} %convert_element_type.6), calls=%async_computation | async-start | bytes 2359296 | tf_op jit(solution)/shard_map/all_to_all | solution.py:596
  34.4 1.6 %collective-permute-start.5 = (f32[4,128]{1,0:T(4,128)S(1)}, f32[4,128]{1,0:T(4,128)S(1)}, u32[]{:S(2)}, u32[]{:S(2)}) collective-permute-start(f32[4,128]{1,0:T(4,128)S(1)} %dynamic_update_slice.33), channel_id=1, source_target_pairs={{0,16},{16,0},{1,17},{17,1},{2,18},{18,2},{3,19},{19,3},{4,20},{20... | collective-permute-start | bytes 6152 | tf_op jit(solution)/shard_map/ppermute | solution.py:31
  36.0 2.1 %collective-permute-done.5 = f32[4,128]{1,0:T(4,128)S(1)} collective-permute-done((f32[4,128]{1,0:T(4,128)S(1)}, f32[4,128]{1,0:T(4,128)S(1)}, u32[]{:S(2)}, u32[]{:S(2)}) %collective-permute-start.5) | collective-permute-done | bytes 2080 | tf_op jit(solution)/shard_map/ppermute | solution.py:31
  38.1 0.7 %collective-permute-start.8 = (f32[4,256]{1,0:T(4,128)S(1)}, f32[4,256]{1,0:T(4,128)S(1)}, u32[]{:S(2)}, u32[]{:S(2)}) collective-permute-start(f32[4,256]{1,0:T(4,128)S(1)} %constant_dynamic-update-slice_fusion.4), channel_id=1, source_target_pairs={{0,12},{4,0},{8,4},{12,8},{1,13},{5,1},{9,5},{13,9},{2,14},{6,2},{... | collective-permute-start | bytes 12296 | tf_op jit(solution)/shard_map/ppermute | solution.py:31
  38.8 1.1 %collective-permute-start.7 = (f32[4,256]{1,0:T(4,128)S(1)}, f32[4,256]{1,0:T(4,128)S(1)}, u32[]{:S(2)}, u32[]{:S(2)}) collective-permute-start(f32[4,256]{1,0:T(4,128)S(1)} %constant_dynamic-update-slice_fusion.4), channel_id=1, source_target_pairs={{0,8},{4,12},{8,0},{12,4},{1,9},{5,13},{9,1},{13,5},{2,10},{6,14},... | collective-permute-start | bytes 12296 | tf_op jit(solution)/shard_map/ppermute | solution.py:31
  39.9 0.2 collective-permute-start.6
  40.1 3.5 %collective-permute-done.6 = f32[4,256]{1,0:T(4,128)S(1)} collective-permute-done((f32[4,256]{1,0:T(4,128)S(1)}, f32[4,256]{1,0:T(4,128)S(1)}, u32[]{:S(2)}, u32[]{:S(2)}) %collective-permute-start.6) | collective-permute-done | bytes 4128 | tf_op jit(solution)/shard_map/ppermute | solution.py:31
  43.7 1.0 %collective-permute-done.7 = f32[4,256]{1,0:T(4,128)S(1)} collective-permute-done((f32[4,256]{1,0:T(4,128)S(1)}, f32[4,256]{1,0:T(4,128)S(1)}, u32[]{:S(2)}, u32[]{:S(2)}) %collective-permute-start.7) | collective-permute-done | bytes 4128 | tf_op jit(solution)/shard_map/ppermute | solution.py:31
  44.7 18.1 %updates.1 = (f32[9,32,4096]{2,1,0:T(8,128)}, bf16[9,32,4096]{2,1,0:T(8,128)(2,1)}) custom-call(s32[1]{0:T(128)S(6)} %copy.27.live_ref, f32[9,9]{1,0:T(8,128)S(1)} %copy-done.3, f32[16,256]{1,0:T(8,128)S(1)} %constant_dynamic-update-slice_fusion.table_ref, s32[1,32]{1,0:T(1,128)S(1)} %bitcast.14, f32[3,32]{1,0:T(4,128)S(1)} %copy-done.7, ...), custom_call_target="tpu_custom_call" | custom-call | bytes 41943040 | tf_op jit(solution)/shard_map/updates/pallas_call | solution.py:607
  62.9 0.6 all-to-all-done
  63.4 0.2 convert_element_type.7.arrived_hbm
  63.7 4.0 %arrived_histories.1 = f32[9,32,4096]{2,1,0:T(8,128)} custom-call(s32[1]{0:T(128)S(6)} %copy.27.live_ref, f32[16,256]{1,0:T(8,128)S(1)} %constant_dynamic-update-slice_fusion.table_ref, f32[9,32,4096]{2,1,0:T(8,128)} %get-tuple-element.19.fields_hbm, f32[16,288,128]{2,1,0:T(8,128)S(1)} %convert_element_type.7.arrived_hbm), custom_call_target="tpu_custom_call" | custom-call | bytes 12582912 | tf_op jit(solution)/shard_map/arrived_histories/pallas_call | solution.py:654
  (35 shorter events, 0.2 us)
Async XLA Ops:
  0.6 10.2 %copy-start.4 = (s32[32]{0:T(128)S(1)}, s32[32]{0:T(128)}, u32[]{:S(2)}) copy-start(s32[32]{0:T(128)} %param.20) | copy-start | bytes 388
  2.4 14.0 %collective-permute-start.1 = (bf16[32,4096]{1,0:T(8,128)(2,1)}, bf16[32,4096]{1,0:T(8,128)(2,1)S(1)}, u32[]{:S(2)}, u32[]{:S(2)}) collective-permute-start(bf16[32,4096]{1,0:T(8,128)(2,1)} %raw_sensor.1), channel_id=1, source_target_pairs={{0,3},{1,0},{2,1},{3,2},{4,7},{5,4},{6,5},{7,6},{8,11},{9,8},{10,9... | collective-permute-start | bytes 786440 | tf_op jit(solution)/shard_map/ppermute | solution.py:31
  7.5 12.3 %collective-permute-start = (bf16[32,4096]{1,0:T(8,128)(2,1)}, bf16[32,4096]{1,0:T(8,128)(2,1)S(1)}, u32[]{:S(2)}, u32[]{:S(2)}) collective-permute-start(bf16[32,4096]{1,0:T(8,128)(2,1)} %raw_sensor.1), channel_id=1, source_target_pairs={{0,1},{1,2},{2,3},{3,0},{4,5},{5,6},{6,7},{7,4},{8,9},{9,10},{10,1... | collective-permute-start | bytes 786440 | tf_op jit(solution)/shard_map/ppermute | solution.py:31
  15.2 4.6 %copy-start = (f32[32,4096]{1,0:T(8,128)S(1)}, f32[32,4096]{1,0:T(8,128)}, u32[]{:S(2)}) copy-start(f32[32,4096]{1,0:T(8,128)} %sensor_ref.3) | copy-start | bytes 1572868
  15.2 4.6 %copy-start.2 = (f32[32,96]{1,0:T(8,128)S(1)}, f32[32,96]{1,0:T(8,128)}, u32[]{:S(2)}) copy-start(f32[32,96]{1,0:T(8,128)} %constant.95.clone.weights_ref) | copy-start | bytes 36868
  15.2 4.6 %copy-start.5 = (s32[2,16]{1,0:T(2,128)S(1)}, s32[2,16]{1,0:T(2,128)}, u32[]{:S(2)}) copy-start(s32[2,16]{1,0:T(2,128)} %flags_ref.3) | copy-start | bytes 388
  15.2 4.6 %copy-start.6 = (s32[32]{0:T(128)S(1)}, s32[32]{0:T(128)}, u32[]{:S(2)}) copy-start(s32[32]{0:T(128)} %param.21) | copy-start | bytes 388
  16.4 28.3 %copy-start.1 = (bf16[768,768]{1,0:T(8,128)(2,1)S(1)}, bf16[768,768]{1,0:T(8,128)(2,1)}, u32[]{:S(2)}) copy-start(bf16[768,768]{1,0:T(8,128)(2,1)} %constant.96.clone.weights_hbm) | copy-start | bytes 3538948
  16.4 28.3 %copy-start.3 = (f32[9,9]{1,0:T(8,128)S(1)}, f32[9,9]{1,0:T(8,128)}, u32[]{:S(2)}) copy-start(f32[9,9]{1,0:T(8,128)} %rate_ref.1) | copy-start | bytes 976
  16.5 28.3 %copy-start.7 = (f32[3,32]{1,0:T(4,128)S(1)}, f32[3,32]{1,0:T(4,128)}, u32[]{:S(2)}) copy-start(f32[3,32]{1,0:T(4,128)} %velocity_ref.1) | copy-start | bytes 1156
  16.5 28.3 %copy-start.8 = (s32[32]{0:T(128)S(1)}, s32[32]{0:T(128)}, u32[]{:S(2)}) copy-start(s32[32]{0:T(128)} %param.23) | copy-start | bytes 388
  22.0 5.3 %collective-permute-start.2 = (f32[1,128]{1,0:T(1,128)S(1)}, f32[1,128]{1,0:T(1,128)S(1)}, u32[]{:S(2)}, u32[]{:S(2)}) collective-permute-start(f32[1,128]{1,0:T(1,128)S(1)} %get-tuple-element.15), channel_id=1, source_target_pairs={{0,1},{1,2},{2,3},{3,0},{4,5},{5,6},{6,7},{7,4},{8,9},{9,10},{10,1... | collective-permute-start | bytes 1544 | tf_op jit(solution)/shard_map/ppermute | solution.py:31
  23.6 4.4 %collective-permute-start.3 = (f32[1,128]{1,0:T(1,128)S(1)}, f32[1,128]{1,0:T(1,128)S(1)}, u32[]{:S(2)}, u32[]{:S(2)}) collective-permute-start(f32[1,128]{1,0:T(1,128)S(1)} %get-tuple-element.15), channel_id=1, source_target_pairs={{0,2},{1,3},{2,0},{3,1},{4,6},{5,7},{6,4},{7,5},{8,10},{9,11},{10,... | collective-permute-start | bytes 1544 | tf_op jit(solution)/shard_map/ppermute | solution.py:31
  24.3 3.8 %collective-permute-start.4 = (f32[1,128]{1,0:T(1,128)S(1)}, f32[1,128]{1,0:T(1,128)S(1)}, u32[]{:S(2)}, u32[]{:S(2)}) collective-permute-start(f32[1,128]{1,0:T(1,128)S(1)} %get-tuple-element.15), channel_id=1, source_target_pairs={{0,3},{1,0},{2,1},{3,2},{4,7},{5,4},{6,5},{7,6},{8,11},{9,8},{10,9... | collective-permute-start | bytes 1544 | tf_op jit(solution)/shard_map/ppermute | solution.py:31
  28.1 35.3 %all-to-all-start = ((f16[16,288,128]{2,1,0:T(8,128)(2,1)}), f16[16,288,128]{2,1,0:T(8,128)(2,1)S(1)}, u32[]{:S(2)}, u32[]{:S(2)}) async-start(f16[16,288,128]{2,1,0:T(8,128)(2,1)} %convert_element_type.6), calls=%async_computation | async-start | bytes 2359296 | tf_op jit(solution)/shard_map/all_to_all | solution.py:596
  34.4 3.7 %collective-permute-start.5 = (f32[4,128]{1,0:T(4,128)S(1)}, f32[4,128]{1,0:T(4,128)S(1)}, u32[]{:S(2)}, u32[]{:S(2)}) collective-permute-start(f32[4,128]{1,0:T(4,128)S(1)} %dynamic_update_slice.33), channel_id=1, source_target_pairs={{0,16},{16,0},{1,17},{17,1},{2,18},{18,2},{3,19},{19,3},{4,20},{20... | collective-permute-start | bytes 6152 | tf_op jit(solution)/shard_map/ppermute | solution.py:31
  38.1 6.6 %collective-permute-start.8 = (f32[4,256]{1,0:T(4,128)S(1)}, f32[4,256]{1,0:T(4,128)S(1)}, u32[]{:S(2)}, u32[]{:S(2)}) collective-permute-start(f32[4,256]{1,0:T(4,128)S(1)} %constant_dynamic-update-slice_fusion.4), channel_id=1, source_target_pairs={{0,12},{4,0},{8,4},{12,8},{1,13},{5,1},{9,5},{13,9},{2,14},{6,2},{... | collective-permute-start | bytes 12296 | tf_op jit(solution)/shard_map/ppermute | solution.py:31
  38.8 5.9 %collective-permute-start.7 = (f32[4,256]{1,0:T(4,128)S(1)}, f32[4,256]{1,0:T(4,128)S(1)}, u32[]{:S(2)}, u32[]{:S(2)}) collective-permute-start(f32[4,256]{1,0:T(4,128)S(1)} %constant_dynamic-update-slice_fusion.4), channel_id=1, source_target_pairs={{0,8},{4,12},{8,0},{12,4},{1,9},{5,13},{9,1},{13,5},{2,10},{6,14},... | collective-permute-start | bytes 12296 | tf_op jit(solution)/shard_map/ppermute | solution.py:31
  39.9 3.8 %collective-permute-start.6 = (f32[4,256]{1,0:T(4,128)S(1)}, f32[4,256]{1,0:T(4,128)S(1)}, u32[]{:S(2)}, u32[]{:S(2)}) collective-permute-start(f32[4,256]{1,0:T(4,128)S(1)} %constant_dynamic-update-slice_fusion.4), channel_id=1, source_target_pairs={{0,4},{4,8},{8,12},{12,0},{1,5},{5,9},{9,13},{13,1},{2,6},{6,10},{... | collective-permute-start | bytes 12296 | tf_op jit(solution)/shard_map/ppermute | solution.py:31
